TPU v7x, 32 devices: a whole 2x2x4 slice. The times are simulated.
32 devices in a mesh: outer: 2 (over core), nodes: 16 (over z, y, x).
Axes of the slice: x: 2, y: 2, z: 4, core: 2. Of those that a mesh axis runs over, the one named last changes fastest.
Arguments:
- features: bfloat16 [16384, 512], P(('outer', 'nodes')), may hold values from -6 to 6
- w_query: bfloat16 [512, 512], replicated, may hold values from -0.25 to 0.25
- w_key: bfloat16 [512, 512], replicated, may hold values from -0.75 to 0.75
- w_value: bfloat16 [512, 512], replicated, may hold values from -0.25 to 0.25
- bases: bfloat16 [2, 512, 512], replicated, may hold values from -0.09375 to 0.09375
- rel_coef: float32 [8, 2], replicated, may hold values from -4 to 4
- send_rows: int32 [32, 16, 32], P(('outer', 'nodes')), may hold values from 0 to 511
- tile_src: int32 [32, 8, 4, 128], P(('outer', 'nodes')), may hold values from 0 to 1023, as said below
- tile_dst: int32 [32, 8, 4, 128], P(('outer', 'nodes')), may hold values from 0 to 127
- tile_count: int32 [32, 8, 4], P(('outer', 'nodes')), may hold values from 1 to 128, as said below
- cotangent: float32 [16384, 512], P(('outer', 'nodes')), may hold values from -6 to 6
Outputs:
- layer_out: float32 [16384, 512], P(('outer', 'nodes'))
- grad_x: float32 [16384, 512], P(('outer', 'nodes'))
- query_grad: float32 [512, 512], replicated
- key_grad: float32 [512, 512], replicated
- value_grad: float32 [512, 512], replicated
- bases_grad: float32 [2, 512, 512], replicated
- coef_grad: float32 [8, 2], replicated
Inputs may be any that keep to these rules, and one draw needn't show every extreme that they name: `send_rows`: row indices into the sending device's own 512 rows. `tile_src`: rows of the device's table (its own 512 rows, then 32 slots from each node position of its group in order). Edges read only slots of other devices of the group, and of each sender only its first slots, as many as that sender fills for this device, between 1 and 32. The first tile_count slots of a tile hold its edges. Every device has a tile with all 128 slots used.
All inputs are finite; a program needn't handle non-finite values.
Results may differ from a plain program's by a relative error of at most 0.0041.
Values may be sent and summed in bfloat16 or wider, within the bound.
No kernel may reach another device: no remote copies, remote signals or barrier semaphores. Data moves between devices by JAX's collectives and lax.ppermute only.
A program may use at most 128 MiB of HBM per device.

v0:
```python
import math

import jax
import jax.numpy as jnp
from jax import lax
from jax.sharding import PartitionSpec as P

HEADS = 8
HEAD_DIM = 64
TILE = 128


precise = lax.Precision.HIGHEST


def tile_rows(halo_table, sources, targets, counts):
    slot_count = sources.shape[-1]
    live_mask = jnp.arange(slot_count)[None, :] < counts[:, None]
    hit_mask = (targets[:, None, :] == jnp.arange(TILE)[None, :, None]) & live_mask[:, None, :]
    picked = halo_table[sources]
    row_sums = jnp.einsum(
        "tje,ted->tjd", hit_mask.astype(jnp.bfloat16), picked, preferred_element_type=jnp.float32
    )
    degree = jnp.sum(hit_mask.astype(jnp.float32), axis=2)
    feat_width = halo_table.shape[1]
    row_sums = row_sums.reshape(-1, feat_width)
    degree = jnp.maximum(degree.reshape(-1), 1.0)
    return (row_sums / degree[:, None], degree, live_mask)


def per_device(
    features,
    w_query,
    w_key,
    w_value,
    bases,
    rel_coef,
    send_rows,
    tile_src,
    tile_dst,
    tile_count,
    cotangent,
):
    node_rows, feat_width = features.shape
    peer_count = lax.axis_size("nodes")
    total_nodes = node_rows * peer_count * lax.axis_size("outer")
    norm_scale = 1.0 / math.sqrt(total_nodes)
    basis_count = bases.shape[0]
    send_list = send_rows[0]
    peer_slots = send_list.shape[1]
    outgoing = features[send_list.reshape(-1)].reshape(peer_count, peer_slots, feat_width)
    incoming = lax.all_to_all(outgoing, "nodes", split_axis=0, concat_axis=0, tiled=True)
    halo_table = jnp.concatenate([features, incoming.reshape(-1, feat_width)], axis=0)
    table_rows = halo_table.shape[0]
    w_all = jnp.concatenate([w_query, w_key, w_value], axis=1)
    projected = jnp.dot(features, w_all, preferred_element_type=jnp.float32)
    exp_query = jnp.exp(projected[:, :feat_width]).reshape(node_rows, HEADS, HEAD_DIM)
    exp_key = jnp.exp(projected[:, feat_width : 2 * feat_width]).reshape(node_rows, HEADS, HEAD_DIM)
    values = projected[:, 2 * feat_width :].reshape(node_rows, HEADS, HEAD_DIM)
    kv_part = jnp.einsum("ihd,ihe->hde", exp_key, values, precision=precise)
    ks_part = jnp.sum(exp_key, axis=0)
    kv_sum, ks_sum = lax.psum((kv_part, ks_part), ("outer", "nodes"))
    src_all = tile_src[0]
    dst_all = tile_dst[0]
    count_all = tile_count[0]

    def forward_step(basis_acc, inputs):
        sources, targets, counts, coef_row = inputs
        aggregate, degree, live_mask = tile_rows(halo_table, sources, targets, counts)
        return (basis_acc + coef_row[:, None, None] * aggregate[None], None)

    basis_acc, _ = lax.scan(
        forward_step,
        jnp.zeros((basis_count, node_rows, feat_width), jnp.float32),
        (src_all, dst_all, count_all, rel_coef),
    )
    basis_in = basis_acc.astype(jnp.bfloat16)
    conv_out = jnp.einsum("bmd,bde->me", basis_in, bases, preferred_element_type=jnp.float32)
    normalizer = jnp.einsum("ihd,hd->ih", exp_query, ks_sum, precision=precise)
    attended = (
        jnp.einsum("ihd,hde->ihe", exp_query, kv_sum, precision=precise) / normalizer[:, :, None]
    )
    layer_out = attended.reshape(node_rows, feat_width) + conv_out
    cot_half = cotangent.astype(jnp.bfloat16)
    basis_grad = jnp.einsum("me,bde->bmd", cot_half, bases, preferred_element_type=jnp.float32)

    def backward_step(table_grad, inputs):
        sources, targets, counts, coef_row = inputs
        aggregate, degree, live_mask = tile_rows(halo_table, sources, targets, counts)
        coef_part = jnp.einsum("md,bmd->b", aggregate, basis_grad, precision=precise)
        agg_grad = (
            jnp.einsum("b,bmd->md", coef_row, basis_grad, precision=precise) / degree[:, None]
        )
        target = (jnp.arange(sources.shape[0])[:, None] * TILE + targets).reshape(-1)
        moved = agg_grad[target] * live_mask.reshape(-1, 1).astype(jnp.float32)
        table_grad = table_grad + jax.ops.segment_sum(
            moved, sources.reshape(-1), num_segments=table_rows
        )
        return (table_grad, coef_part)

    table_grad, coef_part = lax.scan(
        backward_step,
        jnp.zeros((table_rows, feat_width), jnp.float32),
        (src_all, dst_all, count_all, rel_coef),
    )
    grad_heads = cotangent.reshape(node_rows, HEADS, HEAD_DIM)
    num_grad = grad_heads / normalizer[:, :, None]
    den_grad = -jnp.sum(grad_heads * attended, axis=2) / normalizer
    dkv_part = jnp.einsum("ihd,ihe->hde", exp_query, num_grad, precision=precise)
    dks_part = jnp.einsum("ihd,ih->hd", exp_query, den_grad, precision=precise)
    dkv_sum, dks_sum, coef_sum = lax.psum((dkv_part, dks_part, coef_part), ("outer", "nodes"))
    query_side = (
        jnp.einsum("ihe,hde->ihd", num_grad, kv_sum, precision=precise)
        + den_grad[:, :, None] * ks_sum[None]
    )
    key_side = jnp.einsum("ihe,hde->ihd", values, dkv_sum, precision=precise) + dks_sum[None]
    value_side = jnp.einsum("ihd,hde->ihe", exp_key, dkv_sum, precision=precise)
    proj_grad = jnp.concatenate(
        [
            (query_side * exp_query).reshape(node_rows, feat_width),
            (key_side * exp_key).reshape(node_rows, feat_width),
            value_side.reshape(node_rows, feat_width),
        ],
        axis=1,
    ).astype(jnp.bfloat16)
    grad_x = jnp.einsum("mc,dc->md", proj_grad, w_all, preferred_element_type=jnp.float32)
    returned = lax.all_to_all(
        table_grad[node_rows:].reshape(peer_count, peer_slots, feat_width),
        "nodes",
        split_axis=0,
        concat_axis=0,
        tiled=True,
    )
    grad_x = (
        grad_x
        + table_grad[:node_rows]
        + jax.ops.segment_sum(
            returned.reshape(-1, feat_width), send_list.reshape(-1), num_segments=node_rows
        )
    )
    feat_part = jnp.einsum("mc,me->ce", features, proj_grad, preferred_element_type=jnp.float32)
    basis_part = jnp.einsum("bmc,me->cbe", basis_in, cot_half, preferred_element_type=jnp.float32)
    stacked = lax.psum(
        jnp.concatenate([feat_part, basis_part.reshape(feat_width, -1)], axis=1), ("outer", "nodes")
    )
    stacked = stacked * norm_scale
    query_grad = stacked[:, :feat_width]
    key_grad = stacked[:, feat_width : 2 * feat_width]
    value_grad = stacked[:, 2 * feat_width : 3 * feat_width]
    bases_grad = jnp.transpose(
        stacked[:, 3 * feat_width :].reshape(feat_width, basis_count, feat_width), (1, 0, 2)
    )
    coef_grad = coef_sum * norm_scale
    return (layer_out, grad_x, query_grad, key_grad, value_grad, bases_grad, coef_grad)


def solution(mesh):
    in_specs = (
        P(("outer", "nodes"), None),
        P(),
        P(),
        P(),
        P(),
        P(),
        P(("outer", "nodes"), None, None),
        P(("outer", "nodes"), None, None, None),
        P(("outer", "nodes"), None, None, None),
        P(("outer", "nodes"), None, None),
        P(("outer", "nodes"), None),
    )
    out_specs = (P(("outer", "nodes"), None), P(("outer", "nodes"), None), P(), P(), P(), P(), P())
    return jax.shard_map(
        per_device, mesh=mesh, in_specs=in_specs, out_specs=out_specs, check_vma=False
    )
```

profile of v0, /device:TPU:0, one launch (start us, length us, event | category | flops | bytes accessed | tf_op | source)
XLA Modules:
  0.0 728.3 jit_solution(13980191790541305902)
XLA Ops:
  11.9 8.3 %all-to-all-start = ((bf16[16,32,512]{2,1,0:T(8,128)(2,1)}), bf16[16,32,512]{2,1,0:T(8,128)(2,1)S(1)}, u32[]{:S(2)}, u32[]{:S(2)}) async-start(bf16[16,32,512]{2,1,0:T(8,128)(2,1)} %bitcast.32), calls=%async_computation | async-start | bytes 1048576 | tf_op jit(solution)/shard_map/all_to_all | solution.py:52
  28.9 40.6 %psum.43 = f32[8,64]{1,0:T(8,128)S(1)} all-reduce(f32[8,64]{1,0:T(8,128)S(1)} %reduce_sum.39), channel_id=1, replica_groups=mesh['outer'=2,'nodes'=16] {'outer','nodes'}, use_global_device_ids=true, to_apply=%region_2.0 | all-reduce | flops 512 | bytes 4096 | tf_op jit(solution)/shard_map/psum | solution.py:62
  83.1 121.6 %all-reduce.7.cloned.1.call-done = (f32[8,64,64]{2,1,0:T(8,128)}, f32[8,64,64]{2,1,0:T(8,128)}) async-done(((f32[8,64,64]{2,1,0:T(8,128)}, f32[8,64,64]{2,1,0:T(8,128)}), (f32[8,64,64]{2,1,0:T(8,128)}, f32[8,64,64]{2,1,0:T(8,128)})) %all-reduce.7.cloned.1.call-update) | async-done | bytes 262160 | tf_op jit(solution)/shard_map/psum | solution.py:62
  215.0 216.1 %while.23 = (s32[]{:T(128)}, f32[1024,512]{1,0:T(8,128)}, f32[8,2]{1,0:T(8,128)S(1)}, s32[8,4,128]{2,1,0:T(4,128)}, f32[8,2]{1,0:T(8,128)S(1)}, /*index=5*/f32[2...) while((s32[]{:T(128)}, f32[1024,512]{1,0:T(8,128)}, ...), condition=%wide.region_12.13_spmd, body=%wide.region_9.12_spmd.sunk | while | flops 75897344 | bytes 24703252 | solution.py:101
  220.3 11.1 %fusion.94 = f32[1,512,512]{2,0,1:T(1,128)S(1)} fusion(f32[2,512,512]{2,1,0:T(8,128)} %get-tuple-element.351, f32[8,2]{1,0:T(8,128)S(1)} %get-tuple-element.350, s32[]{:T(128)S(6)} %copy.75), kind=kOutput, calls=%fused_computation.25.clone.1 | convolution fusion | flops 6291456 | bytes 3146244 | tf_op jit(solution)/shard_map/while/body/eval_jaxpr/b,bmd->md/dot_general | solution.py:92
  233.7 8.3 %scatter_custom_fusion.6 = f32[1024,512]{1,0:T(8,128)} fusion(f32[1024,512]{1,0:T(8,128)} %get-tuple-element.336, s32[512]{0:T(512)S(1)} %dynamic-slice_bitcast_fusion.4, f32[512]{0:T(512)S(1)} %get-tuple-element.286, f32[512,512]{1,0:T(8,128)S(1)} %get-tuple-element.288, s32[1024]{0:T(1024)S(1)} %pad_clamp_fusion.8), kind=kCustom, calls=%fused_computation.29.clone.1 | custom fusion | flops 524288 | bytes 3151872 | tf_op jit(solution)/shard_map/while/body/eval_jaxpr/scatter-add | solution.py:96
  247.4 11.1 %fusion.94 = f32[1,512,512]{2,0,1:T(1,128)S(1)} fusion(f32[2,512,512]{2,1,0:T(8,128)} %get-tuple-element.351, f32[8,2]{1,0:T(8,128)S(1)} %get-tuple-element.350, s32[]{:T(128)S(6)} %copy.75), kind=kOutput, calls=%fused_computation.25.clone.1 | convolution fusion | flops 6291456 | bytes 3146244 | tf_op jit(solution)/shard_map/while/body/eval_jaxpr/b,bmd->md/dot_general | solution.py:92
  260.7 8.3 %scatter_custom_fusion.6 = f32[1024,512]{1,0:T(8,128)} fusion(f32[1024,512]{1,0:T(8,128)} %get-tuple-element.336, s32[512]{0:T(512)S(1)} %dynamic-slice_bitcast_fusion.4, f32[512]{0:T(512)S(1)} %get-tuple-element.286, f32[512,512]{1,0:T(8,128)S(1)} %get-tuple-element.288, s32[1024]{0:T(1024)S(1)} %pad_clamp_fusion.8), kind=kCustom, calls=%fused_computation.29.clone.1 | custom fusion | flops 524288 | bytes 3151872 | tf_op jit(solution)/shard_map/while/body/eval_jaxpr/scatter-add | solution.py:96
  274.4 11.1 %fusion.94 = f32[1,512,512]{2,0,1:T(1,128)S(1)} fusion(f32[2,512,512]{2,1,0:T(8,128)} %get-tuple-element.351, f32[8,2]{1,0:T(8,128)S(1)} %get-tuple-element.350, s32[]{:T(128)S(6)} %copy.75), kind=kOutput, calls=%fused_computation.25.clone.1 | convolution fusion | flops 6291456 | bytes 3146244 | tf_op jit(solution)/shard_map/while/body/eval_jaxpr/b,bmd->md/dot_general | solution.py:92
  287.8 8.3 %scatter_custom_fusion.6 = f32[1024,512]{1,0:T(8,128)} fusion(f32[1024,512]{1,0:T(8,128)} %get-tuple-element.336, s32[512]{0:T(512)S(1)} %dynamic-slice_bitcast_fusion.4, f32[512]{0:T(512)S(1)} %get-tuple-element.286, f32[512,512]{1,0:T(8,128)S(1)} %get-tuple-element.288, s32[1024]{0:T(1024)S(1)} %pad_clamp_fusion.8), kind=kCustom, calls=%fused_computation.29.clone.1 | custom fusion | flops 524288 | bytes 3151872 | tf_op jit(solution)/shard_map/while/body/eval_jaxpr/scatter-add | solution.py:96
  301.4 11.1 %fusion.94 = f32[1,512,512]{2,0,1:T(1,128)S(1)} fusion(f32[2,512,512]{2,1,0:T(8,128)} %get-tuple-element.351, f32[8,2]{1,0:T(8,128)S(1)} %get-tuple-element.350, s32[]{:T(128)S(6)} %copy.75), kind=kOutput, calls=%fused_computation.25.clone.1 | convolution fusion | flops 6291456 | bytes 3146244 | tf_op jit(solution)/shard_map/while/body/eval_jaxpr/b,bmd->md/dot_general | solution.py:92
  314.8 8.3 %scatter_custom_fusion.6 = f32[1024,512]{1,0:T(8,128)} fusion(f32[1024,512]{1,0:T(8,128)} %get-tuple-element.336, s32[512]{0:T(512)S(1)} %dynamic-slice_bitcast_fusion.4, f32[512]{0:T(512)S(1)} %get-tuple-element.286, f32[512,512]{1,0:T(8,128)S(1)} %get-tuple-element.288, s32[1024]{0:T(1024)S(1)} %pad_clamp_fusion.8), kind=kCustom, calls=%fused_computation.29.clone.1 | custom fusion | flops 524288 | bytes 3151872 | tf_op jit(solution)/shard_map/while/body/eval_jaxpr/scatter-add | solution.py:96
  328.4 11.1 %fusion.94 = f32[1,512,512]{2,0,1:T(1,128)S(1)} fusion(f32[2,512,512]{2,1,0:T(8,128)} %get-tuple-element.351, f32[8,2]{1,0:T(8,128)S(1)} %get-tuple-element.350, s32[]{:T(128)S(6)} %copy.75), kind=kOutput, calls=%fused_computation.25.clone.1 | convolution fusion | flops 6291456 | bytes 3146244 | tf_op jit(solution)/shard_map/while/body/eval_jaxpr/b,bmd->md/dot_general | solution.py:92
  341.8 8.3 %scatter_custom_fusion.6 = f32[1024,512]{1,0:T(8,128)} fusion(f32[1024,512]{1,0:T(8,128)} %get-tuple-element.336, s32[512]{0:T(512)S(1)} %dynamic-slice_bitcast_fusion.4, f32[512]{0:T(512)S(1)} %get-tuple-element.286, f32[512,512]{1,0:T(8,128)S(1)} %get-tuple-element.288, s32[1024]{0:T(1024)S(1)} %pad_clamp_fusion.8), kind=kCustom, calls=%fused_computation.29.clone.1 | custom fusion | flops 524288 | bytes 3151872 | tf_op jit(solution)/shard_map/while/body/eval_jaxpr/scatter-add | solution.py:96
  355.4 11.1 %fusion.94 = f32[1,512,512]{2,0,1:T(1,128)S(1)} fusion(f32[2,512,512]{2,1,0:T(8,128)} %get-tuple-element.351, f32[8,2]{1,0:T(8,128)S(1)} %get-tuple-element.350, s32[]{:T(128)S(6)} %copy.75), kind=kOutput, calls=%fused_computation.25.clone.1 | convolution fusion | flops 6291456 | bytes 3146244 | tf_op jit(solution)/shard_map/while/body/eval_jaxpr/b,bmd->md/dot_general | solution.py:92
  368.8 8.3 %scatter_custom_fusion.6 = f32[1024,512]{1,0:T(8,128)} fusion(f32[1024,512]{1,0:T(8,128)} %get-tuple-element.336, s32[512]{0:T(512)S(1)} %dynamic-slice_bitcast_fusion.4, f32[512]{0:T(512)S(1)} %get-tuple-element.286, f32[512,512]{1,0:T(8,128)S(1)} %get-tuple-element.288, s32[1024]{0:T(1024)S(1)} %pad_clamp_fusion.8), kind=kCustom, calls=%fused_computation.29.clone.1 | custom fusion | flops 524288 | bytes 3151872 | tf_op jit(solution)/shard_map/while/body/eval_jaxpr/scatter-add | solution.py:96
  382.4 11.1 %fusion.94 = f32[1,512,512]{2,0,1:T(1,128)S(1)} fusion(f32[2,512,512]{2,1,0:T(8,128)} %get-tuple-element.351, f32[8,2]{1,0:T(8,128)S(1)} %get-tuple-element.350, s32[]{:T(128)S(6)} %copy.75), kind=kOutput, calls=%fused_computation.25.clone.1 | convolution fusion | flops 6291456 | bytes 3146244 | tf_op jit(solution)/shard_map/while/body/eval_jaxpr/b,bmd->md/dot_general | solution.py:92
  395.8 8.3 %scatter_custom_fusion.6 = f32[1024,512]{1,0:T(8,128)} fusion(f32[1024,512]{1,0:T(8,128)} %get-tuple-element.336, s32[512]{0:T(512)S(1)} %dynamic-slice_bitcast_fusion.4, f32[512]{0:T(512)S(1)} %get-tuple-element.286, f32[512,512]{1,0:T(8,128)S(1)} %get-tuple-element.288, s32[1024]{0:T(1024)S(1)} %pad_clamp_fusion.8), kind=kCustom, calls=%fused_computation.29.clone.1 | custom fusion | flops 524288 | bytes 3151872 | tf_op jit(solution)/shard_map/while/body/eval_jaxpr/scatter-add | solution.py:96
  409.4 11.1 %fusion.94 = f32[1,512,512]{2,0,1:T(1,128)S(1)} fusion(f32[2,512,512]{2,1,0:T(8,128)} %get-tuple-element.351, f32[8,2]{1,0:T(8,128)S(1)} %get-tuple-element.350, s32[]{:T(128)S(6)} %copy.75), kind=kOutput, calls=%fused_computation.25.clone.1 | convolution fusion | flops 6291456 | bytes 3146244 | tf_op jit(solution)/shard_map/while/body/eval_jaxpr/b,bmd->md/dot_general | solution.py:92
  422.8 8.3 %scatter_custom_fusion.6 = f32[1024,512]{1,0:T(8,128)} fusion(f32[1024,512]{1,0:T(8,128)} %get-tuple-element.336, s32[512]{0:T(512)S(1)} %dynamic-slice_bitcast_fusion.4, f32[512]{0:T(512)S(1)} %get-tuple-element.286, f32[512,512]{1,0:T(8,128)S(1)} %get-tuple-element.288, s32[1024]{0:T(1024)S(1)} %pad_clamp_fusion.8), kind=kCustom, calls=%fused_computation.29.clone.1 | custom fusion | flops 524288 | bytes 3151872 | tf_op jit(solution)/shard_map/while/body/eval_jaxpr/scatter-add | solution.py:96
  431.2 57.2 %while.24 = (s32[]{:T(128)}, f32[2,512,512]{2,1,0:T(8,128)}, f32[8,2]{1,0:T(8,128)S(1)}, s32[8,4,128]{2,1,0:T(4,128)}, s32[8,4]{1,0:T(8,128)S(1)}, /*index=5*/s3...) while((s32[]{:T(128)}, f32[2,512,512]{2,1,0:T(8,128)}, ...), condition=%wide.region_5.6_spmd.clone, body=%wide.region_3.5_spmd.clone.sunk | while | flops 69340160 | bytes 26769152 | solution.py:72
  492.4 39.2 %all-reduce = (f32[8,64]{1,0:T(8,128)S(1)}, f32[8,2]{0,1:T(2,128)S(1)}) all-reduce(f32[8,64]{1,0:T(8,128)S(1)} %bitcast.220, f32[8,2]{0,1:T(2,128)S(1)} %copy.29), channel_id=1, replica_groups=mesh['outer'=2,'nodes'=16] {'outer','nodes'}, use_global_device_ids=true, to_apply=%region_8.9 | all-reduce | flops 528 | bytes 4224 | tf_op jit(solution)/shard_map/psum | solution.py:111
  554.3 28.0 %all-to-all-done.1 = f32[16,32,512]{2,1,0:T(8,128)} async-done(((f32[16,32,512]{2,1,0:T(8,128)}), f32[16,32,512]{2,1,0:T(8,128)}, u32[]{:S(2)}, u32[]{:S(2)}) %all-to-all-start.1) | async-done | bytes 1048608 | tf_op jit(solution)/shard_map/all_to_all | solution.py:127
  587.0 119.7 %all-reduce.5.cloned.1.call-done = f32[512,2560]{0,1:T(8,128)} async-done(((f32[512,2560]{0,1:T(8,128)}), f32[512,2560]{0,1:T(8,128)}) %all-reduce.5.cloned.1.call-update) | async-done | bytes 5242896 | tf_op jit(solution)/shard_map/psum | solution.py:143
  (399 shorter events, 200.3 us)
Async XLA Ops:
  7.2 69.6 %copy-start = (bf16[2,512,512]{2,1,0:T(8,128)(2,1)S(1)}, bf16[2,512,512]{2,1,0:T(8,128)(2,1)}, u32[]{:S(2)}) copy-start(bf16[2,512,512]{2,1,0:T(8,128)(2,1)} %param.19) | copy-start | bytes 3145732
  8.1 12.2 %copy-start.10 = (f32[512,512]{1,0:T(8,128)S(1)}, f32[512,512]{1,0:T(8,128)}, u32[]{:S(2)}) copy-start(f32[512,512]{1,0:T(8,128)} %param.25) | copy-start | bytes 3145732
  11.9 201.4 %all-to-all-start = ((bf16[16,32,512]{2,1,0:T(8,128)(2,1)}), bf16[16,32,512]{2,1,0:T(8,128)(2,1)S(1)}, u32[]{:S(2)}, u32[]{:S(2)}) async-start(bf16[16,32,512]{2,1,0:T(8,128)(2,1)} %bitcast.32), calls=%async_computation | async-start | bytes 1048576 | tf_op jit(solution)/shard_map/all_to_all | solution.py:52
  20.2 184.5 %all-reduce.7.cloned.1.call-start = ((), (), s32[]{:S(2)}) async-start(), calls=%async_computation.3 | async-start | bytes 1048576 | tf_op jit(solution)/shard_map/psum | solution.py:62
  21.6 4.5 copy-start.6
  28.8 180.8 %copy-start.8 = (f32[512,512]{0,1:T(8,128)}, f32[512,512]{0,1:T(8,128)S(1)}, u32[]{:S(2)}) copy-start(f32[512,512]{0,1:T(8,128)S(1)} %get-tuple-element.188) | copy-start | bytes 3145732
  71.4 3.5 copy-start.11
  76.7 3.4 copy-start.28
  76.7 3.4 copy-start.27
  76.7 629.9 %all-reduce.5.cloned.1.call-start = ((), (), s32[]{:S(2)}) async-start(), calls=%async_computation.2 | async-start | bytes 10485760 | tf_op jit(solution)/shard_map/psum | solution.py:143
  204.8 3.8 copy-start.12
  204.8 4.8 copy-start.21
  488.3 43.3 %copy-start.9 = (f32[512,512]{0,1:T(8,128)S(1)}, f32[512,512]{0,1:T(8,128)}, u32[]{:S(2)}) copy-start(f32[512,512]{0,1:T(8,128)} %copy-done.8) | copy-start | bytes 3145732
  492.4 41.5 %copy-start.7 = (bf16[512,512]{1,0:T(8,128)(2,1)S(1)}, bf16[512,512]{1,0:T(8,128)(2,1)}, u32[]{:S(2)}) copy-start(bf16[512,512]{1,0:T(8,128)(2,1)} %param.15) | copy-start | bytes 1572868
  492.4 41.5 %copy-start.22 = (bf16[8,64,512]{2,1,0:T(8,128)(2,1)S(1)}, bf16[8,64,512]{2,1,0:T(8,128)(2,1)}, u32[]{:S(2)}) copy-start(bf16[8,64,512]{2,1,0:T(8,128)(2,1)} %convolution_convert_fusion) | copy-start | bytes 1572868
  540.2 6.7 copy-start.26
  541.3 8.9 %copy-start.3 = (f32[2,512,512]{2,1,0:T(8,128)S(1)}, f32[2,512,512]{2,1,0:T(8,128)}, u32[]{:S(2)}) copy-start(f32[2,512,512]{2,1,0:T(8,128)} %get-tuple-element.92) | copy-start | bytes 6291460
  541.3 41.0 %all-to-all-start.1 = ((f32[16,32,512]{2,1,0:T(8,128)}), f32[16,32,512]{2,1,0:T(8,128)}, u32[]{:S(2)}, u32[]{:S(2)}) async-start(f32[16,32,512]{2,1,0:T(8,128)} %bitcast.203), calls=%async_computation.1 | async-start | bytes 2097152 | tf_op jit(solution)/shard_map/all_to_all | solution.py:127
  550.1 3.1 copy-start.16
  550.1 3.1 copy-start.18
  550.1 3.1 copy-start.23
  550.1 3.1 copy-start.25
  550.2 3.1 copy-start.31
  587.0 122.8 %copy-start.5 = (f32[512,512]{1,0:T(8,128)}, f32[512,512]{1,0:T(8,128)S(1)}, u32[]{:S(2)}) copy-start(f32[512,512]{1,0:T(8,128)S(1)} %scatter_fusion) | copy-start | bytes 3145732
  (33 other events, 55.1 us)
Sparse Core Ops, SparseCore 0:
  76.8 127.9 all-reduce.6
  538.8 167.7 all-reduce.4
where the time goes:
time: 731 us; the launch traced here: 728 us
  waiting for transfers between devices  269 us (37%)
  matrix products  125 us (17%)
  local copies, waits for them, and re-layouts  118 us (16%)
  other arithmetic  107 us (15%)
  blocking collectives  79.9 us (11%)
  between operations  14.3 us (2%)
  starting transfers between devices  14.1 us (2%)
    psum x1, waiting for transfers between devices, per_device(): kv_sum, ks_sum = lax.psum((kv_part, ks_part), ('outer', 'nodes'))  122 us
    psum x1, waiting for transfers between devices, per_device(): lax.psum(jnp.concatenate([feat_part, basis_part.reshape(feat_width, -1)],...  120 us
    dot_general x8, matrix products, backward_step(): jnp.einsum('b,bmd->md', coef_row, basis_grad, precision=precise)  89.1 us
    scatter-add x8, other arithmetic, backward_step(): jax.ops.segment_sum(moved, sources.reshape(-1), num_segments=table_rows)  66.2 us
    psum x1, blocking collectives, per_device(): kv_sum, ks_sum = lax.psum((kv_part, ks_part), ('outer', 'nodes'))  40.6 us
    psum x1, blocking collectives, per_device(): lax.psum((dkv_part, dks_part, coef_part), ('outer', 'nodes'))  39.2 us
    gather x16, local copies, waits for them, and re-layouts, tile_rows(): picked = halo_table[sources]  31.5 us
    while x48, local copies, waits for them, and re-layouts  30.5 us
  transfers between devices with their start and end apart: 4, of which 3 were waited for; matrix products, arithmetic and copies ran while one was open for 6% of the time, Pallas kernels for 0%

commit v1 on v0

v1 whole, which is shorter than its diff:
```python
import functools
import math

import jax
import jax.numpy as jnp
from jax import lax
from jax.experimental import pallas as pl
from jax.experimental.pallas import tpu as pltpu
from jax.sharding import PartitionSpec as P

HEAD_DIM = 64
TILE = 128
LANES = 128

f32 = jnp.float32
bf16 = jnp.bfloat16
NN = (((1,), (0,)), ((), ()))
NT = (((1,), (1,)), ((), ()))
TN = (((0,), (0,)), ((), ()))

VMEM = pl.BlockSpec(memory_space=pltpu.VMEM)
SMEM = pl.BlockSpec(memory_space=pltpu.SMEM)


def mm(a, b, dims=NN):
    return lax.dot_general(a, b, dims, preferred_element_type=f32)


def split(x):
    high = x.astype(bf16)
    return high, (x - high.astype(f32)).astype(bf16)


def mm_exact_right(a, b, dims=NN):
    high, low = split(a)
    return mm(high, b, dims) + mm(low, b, dims)


def mm_wide(a, b, dims=NN):
    ah, al = split(a)
    bh, bl = split(b)
    return mm(ah, bh, dims) + (mm(ah, bl, dims) + mm(al, bh, dims))


def call(body, out_shape, n_smem, n_vmem, scratch=()):
    return pl.pallas_call(
        body,
        out_shape=out_shape,
        in_specs=[SMEM] * n_smem + [VMEM] * n_vmem,
        out_specs=jax.tree.map(lambda _: VMEM, out_shape),
        scratch_shapes=list(scratch),
        compiler_params=pltpu.CompilerParams(vmem_limit_bytes=56 * 1024 * 1024),
    )


def iota(shape, dim):
    return lax.broadcasted_iota(jnp.int32, shape, dim)


def one_hot_rows(index_row, count):
    return jnp.where(iota((count, index_row.shape[1]), 0) == index_row, 1.0, 0.0).astype(bf16)


def head_mask():
    return (iota((LANES, LANES), 0) < HEAD_DIM) == (iota((LANES, LANES), 1) < HEAD_DIM)


def block_diagonal(packed):
    return jnp.where(head_mask(), jnp.concatenate([packed, packed], axis=0), 0.0)


def pack_diagonal(full):
    left = iota((HEAD_DIM, LANES), 1) < HEAD_DIM
    return jnp.where(left, full[:HEAD_DIM], full[HEAD_DIM:])


def store_summary(me, pair, pairs, packed, row, mine_ref, theirs_ref):
    half = pairs // 2
    at = (pair % half) * LANES
    side = pair // half
    tail = jnp.where(iota((8, LANES), 0) == 0, row, 0.0)

    @pl.when(me == side)
    def _():
        mine_ref[0:HEAD_DIM, at : at + LANES] = packed
        mine_ref[HEAD_DIM : HEAD_DIM + 8, at : at + LANES] = tail

    @pl.when(me != side)
    def _():
        theirs_ref[0:HEAD_DIM, at : at + LANES] = packed
        theirs_ref[HEAD_DIM : HEAD_DIM + 8, at : at + LANES] = tail


def load_summary(me, pair, pairs, mine_ref, theirs_ref):
    half = pairs // 2
    at = (pair % half) * LANES
    both = jnp.where(
        me == pair // half, mine_ref[:, at : at + LANES], theirs_ref[:, at : at + LANES]
    )
    return both[:HEAD_DIM], both[HEAD_DIM : HEAD_DIM + 1]


def gather_kernel(send_ref, features_ref, out_ref):
    pick = one_hot_rows(send_ref[...], features_ref.shape[0])
    out_ref[...] = mm(pick, features_ref[...], TN).astype(bf16)


def project_kernel(me_ref, features_ref, wq_ref, wk_ref, wv_ref, eq_ref, ek_ref, v_ref, mine_ref, theirs_ref):
    me = me_ref[0]
    features = features_ref[...]
    pairs = features.shape[1] // LANES
    ek_ref[...] = jnp.exp(mm(features, wk_ref[...]))
    v_ref[...] = mm(features, wv_ref[...])
    for p in range(pairs):
        at = slice(p * LANES, (p + 1) * LANES)
        key = ek_ref[:, at]
        full = mm_wide(key, v_ref[:, at], TN)
        store_summary(
            me, p, pairs, pack_diagonal(full), jnp.sum(key, axis=0, keepdims=True), mine_ref, theirs_ref
        )
    eq_ref[...] = jnp.exp(mm(features, wq_ref[...]))


def attend_kernel(
    me_ref, eq_ref, cot_ref, sum_mine_ref, sum_theirs_ref, att_ref, qblock_ref, mine_ref, theirs_ref
):
    me = me_ref[0]
    pairs = eq_ref.shape[1] // LANES
    same_head = jnp.where(head_mask(), 1.0, 0.0).astype(bf16)
    for p in range(pairs):
        at = slice(p * LANES, (p + 1) * LANES)
        kv, ks = load_summary(me, p, pairs, sum_mine_ref, sum_theirs_ref)
        kv = block_diagonal(kv)
        query = eq_ref[:, at]
        cot = cot_ref[:, at]
        inverse = 1.0 / mm_exact_right(query * ks, same_head)
        attended = mm_wide(query, kv) * inverse
        att_ref[:, at] = attended
        num_grad = cot * inverse
        den_grad = -mm_exact_right(cot * attended, same_head) * inverse
        full = mm_wide(query, num_grad, TN)
        row = jnp.sum(query * den_grad, axis=0, keepdims=True)
        store_summary(me, p, pairs, pack_diagonal(full), row, mine_ref, theirs_ref)
        query_side = mm_wide(num_grad, kv, NT) + den_grad * ks
        qblock_ref[:, at] = (query_side * query).astype(bf16)


def key_kernel(
    me_ref, ek_ref, v_ref, features_ref, sum_mine_ref, sum_theirs_ref, kblock_ref, vblock_ref, mine_ref, theirs_ref
):
    me = me_ref[0]
    pairs = ek_ref.shape[1] // LANES
    for p in range(pairs):
        at = slice(p * LANES, (p + 1) * LANES)
        dkv, dks = load_summary(me, p, pairs, sum_mine_ref, sum_theirs_ref)
        dkv = block_diagonal(dkv)
        key = ek_ref[:, at]
        key_side = mm_wide(v_ref[:, at], dkv, NT) + dks
        kblock_ref[:, at] = (key_side * key).astype(bf16)
        vblock_ref[:, at] = mm_wide(key, dkv).astype(bf16)
    store_halves(me, mm(features_ref[...], kblock_ref[...], TN), mine_ref, theirs_ref, slice(None))


def store_halves(me, whole, mine_ref, theirs_ref, at):
    rows = whole.shape[0] // 2
    low, high = whole[:rows], whole[rows:]
    mine_ref[:, at] = jnp.where(me == 0, low, high)
    theirs_ref[:, at] = jnp.where(me == 0, high, low).astype(bf16)


def input_grad_kernel(
    send_ref, qblock_ref, kblock_ref, vblock_ref, wq_ref, wk_ref, wv_ref, own_ref, returned_ref, out_ref
):
    total = mm(qblock_ref[...], wq_ref[...], NT) + mm(kblock_ref[...], wk_ref[...], NT)
    total += mm(vblock_ref[...], wv_ref[...], NT) + own_ref[...]
    out_ref[...] = total + mm(one_hot_rows(send_ref[...], out_ref.shape[0]), returned_ref[...])


def early_weight_kernel(me_ref, features_ref, qblock_ref, ek_ref, mine_ref, theirs_ref):
    me = me_ref[0]
    features = features_ref[...]
    width = features.shape[1]
    store_halves(me, mm(features, qblock_ref[...], TN), mine_ref, theirs_ref, slice(0, width))
    high, low = split(ek_ref[...])
    store_halves(
        me, mm(features, high, TN) + mm(features, low, TN), mine_ref, theirs_ref, slice(width, 2 * width)
    )


def incidence_kernel(count_ref, coef_ref, src_ref, dst_ref, high_ref, low_ref, hit_ref, rows_ref):
    relations, tiles, slots = src_ref.shape
    basis_count, nodes, table_rows = high_ref.shape
    for t in range(tiles):
        picks = []
        for r in range(relations):
            live = iota((TILE, slots), 1) < count_ref[r, t]
            hit = jnp.where(
                (iota((TILE, slots), 0) == dst_ref[r, t : t + 1, :]) & live, 1.0, 0.0
            )
            degree = jnp.maximum(jnp.sum(hit, axis=1, keepdims=True), 1.0)
            hit = hit / degree
            at = slice(r * slots, (r + 1) * slots)
            hit_ref[t, :, at] = hit
            for b in range(basis_count):
                rows_ref[b * TILE : (b + 1) * TILE, at] = hit * coef_ref[r, b]
            picks.append(one_hot_rows(src_ref[r, t : t + 1, :], table_rows))
        pick = jnp.concatenate(picks, axis=1)
        high, low = split(rows_ref[...])
        mixed = mm(high, pick, NT) + mm(low, pick, NT)
        high, low = split(mixed)
        for b in range(basis_count):
            high_ref[b, t * TILE : (t + 1) * TILE, :] = high[b * TILE : (b + 1) * TILE]
            low_ref[b, t * TILE : (t + 1) * TILE, :] = low[b * TILE : (b + 1) * TILE]


def convolve_kernel(
    me_ref, high_ref, low_ref, own_ref, halo_ref, bases_ref, cot_ref, conv_ref, mine_ref, theirs_ref
):
    me = me_ref[0]
    basis_count, nodes, _ = high_ref.shape
    width = own_ref.shape[1]
    cot = cot_ref[...].astype(bf16)
    own, halo = own_ref[...], halo_ref[...]
    conv = None
    for b in range(basis_count):
        basis_in = (
            mm(high_ref[b, :, :nodes], own)
            + mm(low_ref[b, :, :nodes], own)
            + mm(high_ref[b, :, nodes:], halo)
            + mm(low_ref[b, :, nodes:], halo)
        ).astype(bf16)
        part = mm(basis_in, bases_ref[b])
        conv = part if conv is None else conv + part
        store_halves(me, mm(basis_in, cot, TN), mine_ref, theirs_ref, slice(b * width, (b + 1) * width))
    conv_ref[...] = conv


def basis_grad_kernel(bases_ref, cot_ref, high_ref, low_ref, out_ref, own_ref, halo_ref):
    basis_count, nodes, _ = high_ref.shape
    cot = cot_ref[...].astype(bf16)
    total = None
    for b in range(basis_count):
        grad = mm(cot, bases_ref[b], NT)
        out_ref[b] = grad
        grad_high, grad_low = split(grad)
        part = mm(high_ref[b], grad_high, TN) + mm(high_ref[b], grad_low, TN) + mm(low_ref[b], grad_high, TN)
        total = part if total is None else total + part
    own_ref[...] = total[:nodes]
    halo_ref[...] = total[nodes:].astype(bf16)


def coef_kernel(src_ref, hit_ref, grad_ref, own_ref, halo_ref, out_ref):
    relations, tiles, slots = src_ref.shape
    basis_count, nodes, width = grad_ref.shape
    table_rows = nodes + halo_ref.shape[0]
    table = jnp.concatenate([own_ref[...], halo_ref[...]], axis=0)
    sums = jnp.zeros((basis_count, relations * slots), f32)
    for t in range(tiles):
        grads = jnp.concatenate([grad_ref[b, t * TILE : (t + 1) * TILE, :] for b in range(basis_count)], axis=0)
        high, low = split(grads)
        dots = mm(high, table, NT) + mm(low, table, NT)
        pick = jnp.concatenate([one_hot_rows(src_ref[r, t : t + 1, :], table_rows) for r in range(relations)], axis=1)
        high, low = split(dots)
        edge = mm(high, pick) + mm(low, pick)
        hit = hit_ref[t]
        sums += jnp.concatenate(
            [jnp.sum(edge[b * TILE : (b + 1) * TILE] * hit, axis=0, keepdims=True) for b in range(basis_count)], axis=0
        )
    row, lane = iota((8, LANES), 0), iota((8, LANES), 1)
    total = jnp.zeros((8, LANES), f32)
    for r in range(relations):
        part = jnp.sum(sums[:, r * slots : (r + 1) * slots], axis=1, keepdims=True)
        for b in range(basis_count):
            total = jnp.where((row == r) & (lane == b), part[b : b + 1, :], total)
    out_ref[...] = total


def add_kernel(a_ref, b_ref, out_ref):
    out_ref[...] = a_ref[...] + b_ref[...]


def finish_kernel(me_ref, mine_ref, theirs_ref, *out_refs, scale):
    me = me_ref[0]
    rows = mine_ref.shape[0]
    at = 0
    for out_ref in out_refs:
        for i in range(out_ref.shape[0]):
            width = out_ref.shape[2]
            a = mine_ref[:, at : at + width].astype(f32) * scale
            b = theirs_ref[:, at : at + width].astype(f32) * scale
            out_ref[i, :rows, :] = jnp.where(me == 0, a, b)
            out_ref[i, rows:, :] = jnp.where(me == 0, b, a)
            at += width


def value_finish_kernel(me_ref, sum_mine_ref, sum_theirs_ref, mine_ref, theirs_ref, out_ref, *, scale):
    me = me_ref[0]
    rows, width = mine_ref.shape
    pairs = width // LANES
    for p in range(pairs):
        at = slice(p * LANES, (p + 1) * LANES)
        dkv, _ = load_summary(me, p, pairs, sum_mine_ref, sum_theirs_ref)
        dkv = block_diagonal(dkv)
        a = mm_exact_left(mine_ref[:, at], dkv) * scale
        b = mm_exact_left(theirs_ref[:, at], dkv) * scale
        out_ref[:rows, at] = jnp.where(me == 0, a, b)
        out_ref[rows:, at] = jnp.where(me == 0, b, a)


def mm_exact_left(a, b, dims=NN):
    high, low = split(b)
    return mm(a, high, dims) + mm(a, low, dims)


def swap_cores(x):
    return lax.ppermute(x, "outer", [(0, 1), (1, 0)])


def all_nodes_sum(x, nodes):
    step = 1
    while step < nodes:
        x = x + lax.ppermute(x, "nodes", [(i, i ^ step) for i in range(nodes)])
        step *= 2
    return x


def reduce_wide(mine, theirs, nodes):
    rows, width = mine.shape
    half = (mine + swap_cores(theirs).astype(f32)).astype(bf16)
    parts = lax.all_to_all(
        half.reshape(nodes, rows // nodes, width), "nodes", split_axis=0, concat_axis=0, tiled=True
    )
    part = jnp.sum(parts.astype(f32), axis=0).astype(bf16)
    whole = lax.all_to_all(
        jnp.broadcast_to(part[None], parts.shape), "nodes", split_axis=0, concat_axis=0, tiled=True
    )
    return whole.reshape(rows, width)


def per_device(
    features, w_query, w_key, w_value, bases, rel_coef, send_rows, tile_src, tile_dst, tile_count, cotangent
):
    rows, width = features.shape
    nodes = lax.axis_size("nodes")
    scale = 1.0 / math.sqrt(rows * nodes * lax.axis_size("outer"))
    basis_count = bases.shape[0]
    slots = send_rows.shape[2]
    halo_rows = nodes * slots
    table_rows = rows + halo_rows
    me = lax.axis_index("outer").astype(jnp.int32).reshape(1)
    send = send_rows.reshape(1, halo_rows)
    src, dst, count = tile_src[0], tile_dst[0], tile_count[0]
    relations, tiles, cap = src.shape

    def shape(*dims, dtype=f32):
        return jax.ShapeDtypeStruct(dims, dtype)

    outgoing = call(gather_kernel, shape(halo_rows, width, dtype=bf16), 0, 2)(send, features)
    halo = lax.all_to_all(
        outgoing.reshape(nodes, slots, width), "nodes", split_axis=0, concat_axis=0, tiled=True
    ).reshape(halo_rows, width)

    summary = shape(HEAD_DIM + 8, width // 2)
    square = shape(rows, width)
    exp_query, exp_key, values, kv_mine, kv_theirs = call(
        project_kernel, (square, square, square, summary, summary), 1, 4
    )(me, features, w_query, w_key, w_value)
    kv_mine = all_nodes_sum(kv_mine + swap_cores(kv_theirs), nodes)
    kv_theirs = swap_cores(kv_mine)

    incidence = shape(basis_count, rows, table_rows, dtype=bf16)
    high, low, hits = call(
        incidence_kernel,
        (incidence, incidence, shape(tiles, TILE, relations * cap)),
        2,
        2,
        [pltpu.VMEM((basis_count * TILE, relations * cap), f32)],
    )(count, rel_coef, src, dst)

    attended, qblock, dkv_mine, dkv_theirs = call(
        attend_kernel, (square, shape(rows, width, dtype=bf16), summary, summary), 1, 4
    )(me, exp_query, cotangent, kv_mine, kv_theirs)
    dkv_mine = all_nodes_sum(dkv_mine + swap_cores(dkv_theirs), nodes)
    dkv_theirs = swap_cores(dkv_mine)

    def halves(n):
        return shape(width // 2, n * width), shape(width // 2, n * width, dtype=bf16)

    conv_out, bases_mine, bases_theirs = call(convolve_kernel, (square, *halves(basis_count)), 1, 6)(
        me, high, low, features, halo, bases, cotangent
    )
    layer_out = call(add_kernel, square, 0, 2)(attended, conv_out)
    basis_grad, own_grad, halo_grad = call(
        basis_grad_kernel, (shape(basis_count, rows, width), square, shape(halo_rows, width, dtype=bf16)), 0, 4
    )(bases, cotangent, high, low)
    returned = lax.all_to_all(
        halo_grad.reshape(nodes, slots, width), "nodes", split_axis=0, concat_axis=0, tiled=True
    ).reshape(halo_rows, width)
    bases_mine = reduce_wide(bases_mine, bases_theirs, nodes)
    bases_theirs = swap_cores(bases_mine)

    early_mine, early_theirs = call(early_weight_kernel, halves(2), 1, 3)(me, features, qblock, exp_key)
    early_mine = reduce_wide(early_mine, early_theirs, nodes)
    early_theirs = swap_cores(early_mine)

    coef_part = call(coef_kernel, shape(8, LANES), 0, 5)(src, hits, basis_grad, features, halo)
    coef_sum = coef_part + swap_cores(coef_part)
    coef_sum = all_nodes_sum(coef_sum, nodes)

    half_block = shape(rows, width, dtype=bf16)
    kblock, vblock, key_mine, key_theirs = call(key_kernel, (half_block, half_block, *halves(1)), 1, 5)(
        me, exp_key, values, features, dkv_mine, dkv_theirs
    )
    key_mine = reduce_wide(key_mine, key_theirs, nodes)
    key_theirs = swap_cores(key_mine)

    grad_x = call(input_grad_kernel, square, 0, 9)(
        send, qblock, kblock, vblock, w_query, w_key, w_value, own_grad, returned
    )

    finish = functools.partial(finish_kernel, scale=scale)
    bases_grad = call(finish, (shape(basis_count, width, width),), 1, 2)(me, bases_mine, bases_theirs)[0]
    query_grad = call(finish, (shape(1, width, width),), 1, 2)(
        me, early_mine[:, :width], early_theirs[:, :width]
    )[0][0]
    value_grad = call(functools.partial(value_finish_kernel, scale=scale), shape(width, width), 1, 4)(
        me, dkv_mine, dkv_theirs, early_mine[:, width:], early_theirs[:, width:]
    )
    key_grad = call(finish, (shape(1, width, width),), 1, 2)(me, key_mine, key_theirs)[0][0]
    coef_grad = coef_sum[:relations, :basis_count] * scale
    return layer_out, grad_x, query_grad, key_grad, value_grad, bases_grad, coef_grad


def solution(mesh):
    both = ("outer", "nodes")
    in_specs = (
        P(both, None),
        P(),
        P(),
        P(),
        P(),
        P(),
        P(both, None, None),
        P(both, None, None, None),
        P(both, None, None, None),
        P(both, None, None),
        P(both, None),
    )
    out_specs = (P(both, None), P(both, None), P(), P(), P(), P(), P())
    return jax.shard_map(per_device, mesh=mesh, in_specs=in_specs, out_specs=out_specs, check_vma=False)
```

time: 731 us -> 246 us (0.34)
  waiting for transfers between devices: 269 us -> 85.2 us
  matrix products: 125 us -> 0 us
  local copies, waits for them, and re-layouts: 118 us -> 10.2 us
  other arithmetic: 107 us -> 6.71 us
  blocking collectives: 79.9 us -> 0 us
  Pallas kernels: 0 us -> 74.3 us
  starting transfers between devices: 14.1 us -> 66.8 us
  between operations: 14.3 us -> 0.92 us
    psum x2 -> x0, waiting for transfers between devices: 241 us -> none  [the longest x1 122 us: per_device(): kv_sum, ks_sum = lax.psum((kv_part, ks_part), ('outer', 'nodes'))]
    dot_general x38 -> x0, matrix products: 125 us -> none  [the longest x8 89.1 us: backward_step(): jnp.einsum('b,bmd->md', coef_row, basis_grad, precision=precise)]
    psum x2 -> x0, blocking collectives: 79.9 us -> none  [the longest x1 40.6 us: per_device(): kv_sum, ks_sum = lax.psum((kv_part, ks_part), ('outer', 'nodes'))]
    pallas_call x0 -> x15, Pallas kernels: none -> 74.3 us  [the longest x1 11.3 us: per_device(): call(coef_kernel, shape(8, LANES), 0, 5)]
    scatter-add x9 -> x0, other arithmetic: 70.8 us -> none  [the longest x8 66.2 us: backward_step(): jax.ops.segment_sum(moved, sources.reshape(-1), num_segments=table_rows)]
    gather x17 -> x0, local copies, waits for them, and re-layouts: 35.4 us -> none  [the longest x16 31.5 us: tile_rows(): picked = halo_table[sources]]
    ppermute x0 -> x23, waiting for transfers between devices: none -> 33.9 us  [the longest x12 28.6 us: all_nodes_sum(): x = x + lax.ppermute(x, 'nodes', [(i, i ^ step) for i in range(nodes)])]
    while x50 -> x0, local copies, waits for them, and re-layouts: 33.5 us -> none
  transfers between devices with their start and end apart: 4 -> 31, of which waited for: 3 -> 20; matrix products, arithmetic and copies ran while one was open for 6% -> 5% of each run, Pallas kernels for 0% -> 28%
where the time goes in v1:
time: 246 us; the launch traced here: 244 us
  waiting for transfers between devices  85.2 us (35%)
  Pallas kernels  74.3 us (30%)
  starting transfers between devices  66.8 us (27%)
  local copies, waits for them, and re-layouts  10.2 us (4%)
  other arithmetic  6.71 us (3%)
    all_to_all x3, waiting for transfers between devices, reduce_wide(): lax.all_to_all(half.reshape(nodes, rows // nodes, width), 'nodes', split_...  30.2 us
    ppermute x12, waiting for transfers between devices, all_nodes_sum(): x = x + lax.ppermute(x, 'nodes', [(i, i ^ step) for i in range(nodes)])  28.6 us
    ppermute x12, starting transfers between devices, all_nodes_sum(): x = x + lax.ppermute(x, 'nodes', [(i, i ^ step) for i in range(nodes)])  25.6 us
    all_to_all x3, waiting for transfers between devices, reduce_wide(): lax.all_to_all(jnp.broadcast_to(part[None], parts.shape), 'nodes', split_...  21.1 us
    all_to_all x3, starting transfers between devices, reduce_wide(): lax.all_to_all(half.reshape(nodes, rows // nodes, width), 'nodes', split_...  13.4 us
    all_to_all x3, starting transfers between devices, reduce_wide(): lax.all_to_all(jnp.broadcast_to(part[None], parts.shape), 'nodes', split_...  11.6 us
    pallas_call x1, Pallas kernels, per_device(): call(coef_kernel, shape(8, LANES), 0, 5)  11.3 us
    pallas_call x1, Pallas kernels, per_device(): call(incidence_kernel, (incidence, incidence, shape(tiles, TILE, relation...  9.42 us
  transfers between devices with their start and end apart: 31, of which 20 were waited for; matrix products, arithmetic and copies ran while one was open for 5% of the time, Pallas kernels for 28%

profile of v1, /device:TPU:0, one launch (start us, length us, event | category | flops | bytes accessed | tf_op | source)
XLA Modules:
  0.0 244.2 jit_solution(13865721737911768636)
XLA Ops:
  4.3 8.4 %all-to-all-start = ((bf16[16,32,512]{2,1,0:T(8,128)(2,1)}), bf16[16,32,512]{2,1,0:T(8,128)(2,1)S(1)}, u32[]{:S(2)}, u32[]{:S(2)}) async-start(bf16[16,32,512]{2,1,0:T(8,128)(2,1)} %bitcast.20), calls=%async_computation | async-start | bytes 1048576 | tf_op jit(solution)/shard_map/all_to_all | solution.py:359
  12.8 5.1 %shard_map.162 = (f32[512,512]{1,0:T(8,128)}, f32[512,512]{1,0:T(8,128)}, f32[512,512]{1,0:T(8,128)}, f32[72,256]{1,0:T(8,128)}, f32[72,256]{1,0:T(8,128)}) custom-call(s32[1]{0:T(128)} %bitcast.me_ref, bf16[512,512]{1,0:T(8,128)(2,1)} %own_ref.3, bf16[512,512]{1,0:T(8,128)(2,1)} %wq_ref.3, bf16[512,512]{1,0:T(8,128)(2,1)} %wk_ref.3, bf16[512,512]{1,0:T(8,128)(2,1)} %wv_ref.3), custom_call_target="tpu_custom_call" | custom-call | tf_op jit(solution)/shard_map/pallas_call | solution.py:365
  22.3 3.7 %collective-permute-done.1 = f32[72,256]{1,0:T(8,128)S(1)} collective-permute-done((f32[72,256]{1,0:T(8,128)S(1)}, f32[72,256]{1,0:T(8,128)S(1)}, u32[]{:S(2)}, u32[]{:S(2)}) %collective-permute-start.1) | collective-permute-done | bytes 73760 | tf_op jit(solution)/shard_map/ppermute | solution.py:322
  42.3 9.4 %shard_map.164 = (bf16[2,512,1024]{2,1,0:T(8,128)(2,1)}, bf16[2,512,1024]{2,1,0:T(8,128)(2,1)}, f32[4,128,1024]{2,1,0:T(8,128)}) custom-call(s32[8,4]{1,0:T(8,128)} %copy.18.count_ref, f32[8,2]{1,0:T(8,128)} %copy.19.coef_ref, s32[8,4,128]{2,1,0:T(4,128)} %bitcast.29, s32[8,4,128]{2,1,0:T(4,128)} %bitcast.31), custom_call_target="tpu_custom_call" | custom-call | tf_op jit(solution)/shard_map/pallas_call | solution.py:372
  51.8 8.1 %shard_map.169 = (f32[2,512,512]{2,1,0:T(8,128)}, f32[512,512]{1,0:T(8,128)}, bf16[512,512]{1,0:T(8,128)(2,1)}) custom-call(bf16[2,512,512]{2,1,0:T(8,128)(2,1)} %bases_ref.3, f32[512,512]{1,0:T(8,128)} %cot_ref.5, bf16[2,512,1024]{2,1,0:T(8,128)(2,1)} %get-tuple-element.35.high_ref, bf16[2,512,1024]{2,1,0:T(8,128)(2,1)} %get-tuple-element.36.low_ref), custom_call_target="tpu_custom_call" | custom-call | tf_op jit(solution)/shard_map/pallas_call | solution.py:393
  59.8 6.1 %all-to-all-start.1 = ((bf16[16,32,512]{2,1,0:T(8,128)(2,1)}), bf16[16,32,512]{2,1,0:T(8,128)(2,1)S(1)}, u32[]{:S(2)}, u32[]{:S(2)}) async-start(bf16[16,32,512]{2,1,0:T(8,128)(2,1)} %bitcast.28), calls=%async_computation.1 | async-start | bytes 1048576 | tf_op jit(solution)/shard_map/all_to_all | solution.py:396
  66.6 5.8 %shard_map.163 = (f32[512,512]{1,0:T(8,128)}, bf16[512,512]{1,0:T(8,128)(2,1)}, f32[72,256]{1,0:T(8,128)}, f32[72,256]{1,0:T(8,128)}) custom-call(s32[1]{0:T(128)} %bitcast.me_ref, f32[512,512]{1,0:T(8,128)} %get-tuple-element.31.eq_ref, f32[512,512]{1,0:T(8,128)} %cot_ref.5, f32[72,256]{1,0:T(8,128)} %copy-done.9, f32[72,256]{1,0:T(8,128)} %copy-done.11), custom_call_target="tpu_custom_call" | custom-call | tf_op jit(solution)/shard_map/pallas_call | solution.py:380
  76.8 3.4 %collective-permute-done.7 = f32[72,256]{1,0:T(8,128)S(1)} collective-permute-done((f32[72,256]{1,0:T(8,128)S(1)}, f32[72,256]{1,0:T(8,128)S(1)}, u32[]{:S(2)}, u32[]{:S(2)}) %collective-permute-start.7) | collective-permute-done | bytes 73760 | tf_op jit(solution)/shard_map/ppermute | solution.py:322
  96.9 4.0 %shard_map.168 = (bf16[512,512]{1,0:T(8,128)(2,1)}, bf16[512,512]{1,0:T(8,128)(2,1)}, f32[256,512]{1,0:T(8,128)}, bf16[256,512]{1,0:T(8,128)(2,1)}) custom-call(s32[1]{0:T(128)} %bitcast.me_ref, f32[512,512]{1,0:T(8,128)} %get-tuple-element.39.ek_ref, f32[512,512]{1,0:T(8,128)} %get-tuple-element.40.v_ref, bf16[512,512]{1,0:T(8,128)(2,1)} %own_ref.3, ...), custom_call_target="tpu_custom_call" | custom-call | tf_op jit(solution)/shard_map/pallas_call | solution.py:411
  101.0 3.7 %shard_map.171 = (f32[256,1024]{1,0:T(8,128)}, bf16[256,1024]{1,0:T(8,128)(2,1)}) custom-call(s32[1]{0:T(128)} %bitcast.me_ref, bf16[512,512]{1,0:T(8,128)(2,1)} %own_ref.3, bf16[512,512]{1,0:T(8,128)(2,1)} %get-tuple-element.38.qblock_ref, f32[512,512]{1,0:T(8,128)} %get-tuple-element.39.ek_ref), custom_call_target="tpu_custom_call" | custom-call | tf_op jit(solution)/shard_map/pallas_call | solution.py:402
  105.9 6.2 %all-to-all-start.4 = ((bf16[16,16,512]{2,1,0:T(8,128)(2,1)}), bf16[16,16,512]{2,1,0:T(8,128)(2,1)S(1)}, u32[]{:S(2)}, u32[]{:S(2)}) async-start(bf16[16,16,512]{2,1,0:T(8,128)(2,1)} %bitcast.11), calls=%async_computation.4 | async-start | bytes 524288 | tf_op jit(solution)/shard_map/all_to_all | solution.py:330
  113.1 9.2 %all-to-all-done.4 = bf16[16,16,512]{2,1,0:T(8,128)(2,1)S(1)} async-done(((bf16[16,16,512]{2,1,0:T(8,128)(2,1)}), bf16[16,16,512]{2,1,0:T(8,128)(2,1)S(1)}, u32[]{:S(2)}, u32[]{:S(2)}) %all-to-all-start.4) | async-done | bytes 262176 | tf_op jit(solution)/shard_map/all_to_all | solution.py:330
  122.3 3.6 %all-to-all-start.2 = ((bf16[16,16,1024]{2,1,0:T(8,128)(2,1)}), bf16[16,16,1024]{2,1,0:T(8,128)(2,1)S(1)}, u32[]{:S(2)}, u32[]{:S(2)}) async-start(bf16[16,16,1024]{2,1,0:T(8,128)(2,1)} %bitcast.8), calls=%async_computation.2 | async-start | bytes 1048576 | tf_op jit(solution)/shard_map/all_to_all | solution.py:330
  125.9 7.8 %shard_map.166 = (f32[512,512]{1,0:T(8,128)}, f32[256,1024]{1,0:T(8,128)}, bf16[256,1024]{1,0:T(8,128)(2,1)}) custom-call(s32[1]{0:T(128)} %bitcast.me_ref, bf16[2,512,1024]{2,1,0:T(8,128)(2,1)} %get-tuple-element.35.high_ref, bf16[2,512,1024]{2,1,0:T(8,128)(2,1)} %get-tuple-element.36.low_ref, bf16[512,512]{1,0:T(8,128)(2,1)} %own_ref.3, ...), custom_call_target="tpu_custom_call" | custom-call | tf_op jit(solution)/shard_map/pallas_call | solution.py:389
  133.8 6.8 %all-to-all-done.2 = bf16[16,16,1024]{2,1,0:T(8,128)(2,1)S(1)} async-done(((bf16[16,16,1024]{2,1,0:T(8,128)(2,1)}), bf16[16,16,1024]{2,1,0:T(8,128)(2,1)S(1)}, u32[]{:S(2)}, u32[]{:S(2)}) %all-to-all-start.2) | async-done | bytes 524320 | tf_op jit(solution)/shard_map/all_to_all | solution.py:330
  141.3 3.9 %all-to-all-start.5 = ((bf16[16,16,512]{2,1,0:T(8,128)(2,1)}), bf16[16,16,512]{2,1,0:T(8,128)(2,1)S(1)}, u32[]{:S(2)}, u32[]{:S(2)}) async-start(bf16[16,16,512]{2,1,0:T(8,128)(2,1)} %broadcast_in_dim.7), calls=%async_computation.5 | async-start | bytes 524288 | tf_op jit(solution)/shard_map/all_to_all | solution.py:334
  147.4 6.9 %all-to-all-done.5 = bf16[16,16,512]{2,1,0:T(8,128)(2,1)S(1)} async-done(((bf16[16,16,512]{2,1,0:T(8,128)(2,1)}), bf16[16,16,512]{2,1,0:T(8,128)(2,1)S(1)}, u32[]{:S(2)}, u32[]{:S(2)}) %all-to-all-start.5) | async-done | bytes 262176 | tf_op jit(solution)/shard_map/all_to_all | solution.py:334
  154.3 3.6 %all-to-all-start.6 = ((bf16[16,16,1024]{2,1,0:T(8,128)(2,1)}), bf16[16,16,1024]{2,1,0:T(8,128)(2,1)S(1)}, u32[]{:S(2)}, u32[]{:S(2)}) async-start(bf16[16,16,1024]{2,1,0:T(8,128)(2,1)} %bitcast.14), calls=%async_computation.6 | async-start | bytes 1048576 | tf_op jit(solution)/shard_map/all_to_all | solution.py:330
  158.0 14.2 %all-to-all-done.6 = bf16[16,16,1024]{2,1,0:T(8,128)(2,1)S(1)} async-done(((bf16[16,16,1024]{2,1,0:T(8,128)(2,1)}), bf16[16,16,1024]{2,1,0:T(8,128)(2,1)S(1)}, u32[]{:S(2)}, u32[]{:S(2)}) %all-to-all-start.6) | async-done | bytes 524320 | tf_op jit(solution)/shard_map/all_to_all | solution.py:330
  173.1 3.8 %all-to-all-start.3 = ((bf16[16,16,1024]{2,1,0:T(8,128)(2,1)}), bf16[16,16,1024]{2,1,0:T(8,128)(2,1)S(1)}, u32[]{:S(2)}, u32[]{:S(2)}) async-start(bf16[16,16,1024]{2,1,0:T(8,128)(2,1)} %broadcast_in_dim.6), calls=%async_computation.3 | async-start | bytes 1048576 | tf_op jit(solution)/shard_map/all_to_all | solution.py:334
  177.0 14.2 %all-to-all-done.3 = bf16[16,16,1024]{2,1,0:T(8,128)(2,1)S(1)} async-done(((bf16[16,16,1024]{2,1,0:T(8,128)(2,1)}), bf16[16,16,1024]{2,1,0:T(8,128)(2,1)S(1)}, u32[]{:S(2)}, u32[]{:S(2)}) %all-to-all-start.3) | async-done | bytes 524320 | tf_op jit(solution)/shard_map/all_to_all | solution.py:334
  192.0 3.9 %all-to-all-start.7 = ((bf16[16,16,1024]{2,1,0:T(8,128)(2,1)}), bf16[16,16,1024]{2,1,0:T(8,128)(2,1)S(1)}, u32[]{:S(2)}, u32[]{:S(2)}) async-start(bf16[16,16,1024]{2,1,0:T(8,128)(2,1)} %broadcast_in_dim.8), calls=%async_computation.7 | async-start | bytes 1048576 | tf_op jit(solution)/shard_map/all_to_all | solution.py:334
  196.5 11.3 %shard_map.176 = f32[8,128]{1,0:T(8,128)} custom-call(s32[8,4,128]{2,1,0:T(4,128)} %bitcast.30, f32[4,128,1024]{2,1,0:T(8,128)} %get-tuple-element.53.hit_ref, f32[2,512,512]{2,1,0:T(8,128)} %get-tuple-element.54.grad_ref, bf16[512,512]{1,0:T(8,128)(2,1)} %own_ref.3, bf16[512,512]{1,0:T(8,128)(2,1)} %bitcast.17), custom_call_target="tpu_custom_call" | custom-call | tf_op jit(solution)/shard_map/pallas_call | solution.py:406
  226.1 4.6 %shard_map.170 = f32[512,512]{1,0:T(8,128)} custom-call(s32[1,512]{1,0:T(1,128)} %reshape.54.send_ref, bf16[512,512]{1,0:T(8,128)(2,1)} %get-tuple-element.38.qblock_ref, bf16[512,512]{1,0:T(8,128)(2,1)} %get-tuple-element.43.kblock_ref, bf16[512,512]{1,0:T(8,128)(2,1)} %get-tuple-element.44.vblock_ref, bf16[512,512]{1,0:T(8,128)(2,1)} %wq_ref.3, ...), custom_call_target="tpu_custom_call" | custom-call | tf_op jit(solution)/shard_map/pallas_call | solution.py:417
  (112 shorter events, 85.4 us)
Async XLA Ops:
  4.3 55.5 %all-to-all-start = ((bf16[16,32,512]{2,1,0:T(8,128)(2,1)}), bf16[16,32,512]{2,1,0:T(8,128)(2,1)S(1)}, u32[]{:S(2)}, u32[]{:S(2)}) async-start(bf16[16,32,512]{2,1,0:T(8,128)(2,1)} %bitcast.20), calls=%async_computation | async-start | bytes 1048576 | tf_op jit(solution)/shard_map/all_to_all | solution.py:359
  20.3 5.7 %collective-permute-start.1 = (f32[72,256]{1,0:T(8,128)S(1)}, f32[72,256]{1,0:T(8,128)S(1)}, u32[]{:S(2)}, u32[]{:S(2)}) collective-permute-start(f32[72,256]{1,0:T(8,128)S(1)} %add.54), channel_id=1, source_target_pairs={{0,1},{1,0},{2,3},{3,2},{4,5},{5,4},{6,7},{7,6},{8,9},{9,8},{10,11... | collective-permute-start | bytes 221192 | tf_op jit(solution)/shard_map/ppermute | solution.py:322
  26.0 4.4 %collective-permute-start.2 = (f32[72,256]{1,0:T(8,128)S(1)}, f32[72,256]{1,0:T(8,128)S(1)}, u32[]{:S(2)}, u32[]{:S(2)}) collective-permute-start(f32[72,256]{1,0:T(8,128)S(1)} %add.55), channel_id=1, source_target_pairs={{0,2},{1,3},{2,0},{3,1},{4,6},{5,7},{6,4},{7,5},{8,10},{9,11},{10,... | collective-permute-start | bytes 221192 | tf_op jit(solution)/shard_map/ppermute | solution.py:322
  30.4 5.1 %collective-permute-start.3 = (f32[72,256]{1,0:T(8,128)S(1)}, f32[72,256]{1,0:T(8,128)S(1)}, u32[]{:S(2)}, u32[]{:S(2)}) collective-permute-start(f32[72,256]{1,0:T(8,128)S(1)} %add.56), channel_id=1, source_target_pairs={{0,4},{1,5},{2,6},{3,7},{4,0},{5,1},{6,2},{7,3},{8,12},{9,13},{10,... | collective-permute-start | bytes 221192 | tf_op jit(solution)/shard_map/ppermute | solution.py:322
  35.6 5.3 %collective-permute-start.4 = (f32[72,256]{1,0:T(8,128)S(1)}, f32[72,256]{1,0:T(8,128)S(1)}, u32[]{:S(2)}, u32[]{:S(2)}) collective-permute-start(f32[72,256]{1,0:T(8,128)S(1)} %add.57), channel_id=1, source_target_pairs={{0,8},{1,9},{2,10},{3,11},{4,12},{5,13},{6,14},{7,15},{8,0},{9,1},... | collective-permute-start | bytes 221192 | tf_op jit(solution)/shard_map/ppermute | solution.py:322
  40.9 25.1 %collective-permute-start.5 = (f32[72,256]{1,0:T(8,128)S(1)}, f32[72,256]{1,0:T(8,128)S(1)}, u32[]{:S(2)}, u32[]{:S(2)}) collective-permute-start(f32[72,256]{1,0:T(8,128)S(1)} %add.58.sum_mine_ref), channel_id=1, source_target_pairs={{0,16},{16,0},{1,17},{17,1},{2,18},{18,2},{3,19},{19,3},{4,20},{20... | collective-permute-start | bytes 221192 | tf_op jit(solution)/shard_map/ppermute | solution.py:316
  59.8 46.0 %all-to-all-start.1 = ((bf16[16,32,512]{2,1,0:T(8,128)(2,1)}), bf16[16,32,512]{2,1,0:T(8,128)(2,1)S(1)}, u32[]{:S(2)}, u32[]{:S(2)}) async-start(bf16[16,32,512]{2,1,0:T(8,128)(2,1)} %bitcast.28), calls=%async_computation.1 | async-start | bytes 1048576 | tf_op jit(solution)/shard_map/all_to_all | solution.py:396
  74.9 5.4 %collective-permute-start.7 = (f32[72,256]{1,0:T(8,128)S(1)}, f32[72,256]{1,0:T(8,128)S(1)}, u32[]{:S(2)}, u32[]{:S(2)}) collective-permute-start(f32[72,256]{1,0:T(8,128)S(1)} %add.59), channel_id=1, source_target_pairs={{0,1},{1,0},{2,3},{3,2},{4,5},{5,4},{6,7},{7,6},{8,9},{9,8},{10,11... | collective-permute-start | bytes 221192 | tf_op jit(solution)/shard_map/ppermute | solution.py:322
  80.3 4.4 %collective-permute-start.8 = (f32[72,256]{1,0:T(8,128)S(1)}, f32[72,256]{1,0:T(8,128)S(1)}, u32[]{:S(2)}, u32[]{:S(2)}) collective-permute-start(f32[72,256]{1,0:T(8,128)S(1)} %add.60), channel_id=1, source_target_pairs={{0,2},{1,3},{2,0},{3,1},{4,6},{5,7},{6,4},{7,5},{8,10},{9,11},{10,... | collective-permute-start | bytes 221192 | tf_op jit(solution)/shard_map/ppermute | solution.py:322
  84.7 4.9 %collective-permute-start.9 = (f32[72,256]{1,0:T(8,128)S(1)}, f32[72,256]{1,0:T(8,128)S(1)}, u32[]{:S(2)}, u32[]{:S(2)}) collective-permute-start(f32[72,256]{1,0:T(8,128)S(1)} %add.61), channel_id=1, source_target_pairs={{0,4},{1,5},{2,6},{3,7},{4,0},{5,1},{6,2},{7,3},{8,12},{9,13},{10,... | collective-permute-start | bytes 221192 | tf_op jit(solution)/shard_map/ppermute | solution.py:322
  89.6 5.3 %collective-permute-start.10 = (f32[72,256]{1,0:T(8,128)S(1)}, f32[72,256]{1,0:T(8,128)S(1)}, u32[]{:S(2)}, u32[]{:S(2)}) collective-permute-start(f32[72,256]{1,0:T(8,128)S(1)} %add.62), channel_id=1, source_target_pairs={{0,8},{1,9},{2,10},{3,11},{4,12},{5,13},{6,14},{7,15},{8,0},{9,1},... | collective-permute-start | bytes 221192 | tf_op jit(solution)/shard_map/ppermute | solution.py:322
  100.9 4.2 %collective-permute-start.14 = (bf16[256,512]{1,0:T(8,128)(2,1)}, bf16[256,512]{1,0:T(8,128)(2,1)S(1)}, u32[]{:S(2)}, u32[]{:S(2)}) collective-permute-start(bf16[256,512]{1,0:T(8,128)(2,1)} %get-tuple-element.50), channel_id=1, source_target_pairs={{0,16},{16,0},{1,17},{17,1},{2,18},{18,2},{3,19},{19,3},{4,20},{20... | collective-permute-start | bytes 786440 | tf_op jit(solution)/shard_map/ppermute | solution.py:316
  104.7 7.4 %collective-permute-start.12 = (bf16[256,1024]{1,0:T(8,128)(2,1)}, bf16[256,1024]{1,0:T(8,128)(2,1)S(1)}, u32[]{:S(2)}, u32[]{:S(2)}) collective-permute-start(bf16[256,1024]{1,0:T(8,128)(2,1)} %get-tuple-element.48), channel_id=1, source_target_pairs={{0,16},{16,0},{1,17},{17,1},{2,18},{18,2},{3,19},{19,3},{4,20},{20... | collective-permute-start | bytes 1572872 | tf_op jit(solution)/shard_map/ppermute | solution.py:316
  105.9 16.4 %all-to-all-start.4 = ((bf16[16,16,512]{2,1,0:T(8,128)(2,1)}), bf16[16,16,512]{2,1,0:T(8,128)(2,1)S(1)}, u32[]{:S(2)}, u32[]{:S(2)}) async-start(bf16[16,16,512]{2,1,0:T(8,128)(2,1)} %bitcast.11), calls=%async_computation.4 | async-start | bytes 524288 | tf_op jit(solution)/shard_map/all_to_all | solution.py:330
  122.3 18.3 %all-to-all-start.2 = ((bf16[16,16,1024]{2,1,0:T(8,128)(2,1)}), bf16[16,16,1024]{2,1,0:T(8,128)(2,1)S(1)}, u32[]{:S(2)}, u32[]{:S(2)}) async-start(bf16[16,16,1024]{2,1,0:T(8,128)(2,1)} %bitcast.8), calls=%async_computation.2 | async-start | bytes 1048576 | tf_op jit(solution)/shard_map/all_to_all | solution.py:330
  133.7 11.5 %collective-permute-start.16 = (bf16[256,1024]{1,0:T(8,128)(2,1)}, bf16[256,1024]{1,0:T(8,128)(2,1)S(1)}, u32[]{:S(2)}, u32[]{:S(2)}) collective-permute-start(bf16[256,1024]{1,0:T(8,128)(2,1)} %get-tuple-element.52), channel_id=1, source_target_pairs={{0,16},{16,0},{1,17},{17,1},{2,18},{18,2},{3,19},{19,3},{4,20},{20... | collective-permute-start | bytes 1572872 | tf_op jit(solution)/shard_map/ppermute | solution.py:316
  141.3 13.0 %all-to-all-start.5 = ((bf16[16,16,512]{2,1,0:T(8,128)(2,1)}), bf16[16,16,512]{2,1,0:T(8,128)(2,1)S(1)}, u32[]{:S(2)}, u32[]{:S(2)}) async-start(bf16[16,16,512]{2,1,0:T(8,128)(2,1)} %broadcast_in_dim.7), calls=%async_computation.5 | async-start | bytes 524288 | tf_op jit(solution)/shard_map/all_to_all | solution.py:334
  154.3 17.9 %all-to-all-start.6 = ((bf16[16,16,1024]{2,1,0:T(8,128)(2,1)}), bf16[16,16,1024]{2,1,0:T(8,128)(2,1)S(1)}, u32[]{:S(2)}, u32[]{:S(2)}) async-start(bf16[16,16,1024]{2,1,0:T(8,128)(2,1)} %bitcast.14), calls=%async_computation.6 | async-start | bytes 1048576 | tf_op jit(solution)/shard_map/all_to_all | solution.py:330
  173.1 18.1 %all-to-all-start.3 = ((bf16[16,16,1024]{2,1,0:T(8,128)(2,1)}), bf16[16,16,1024]{2,1,0:T(8,128)(2,1)S(1)}, u32[]{:S(2)}, u32[]{:S(2)}) async-start(bf16[16,16,1024]{2,1,0:T(8,128)(2,1)} %broadcast_in_dim.6), calls=%async_computation.3 | async-start | bytes 1048576 | tf_op jit(solution)/shard_map/all_to_all | solution.py:334
  192.0 38.6 %all-to-all-start.7 = ((bf16[16,16,1024]{2,1,0:T(8,128)(2,1)}), bf16[16,16,1024]{2,1,0:T(8,128)(2,1)S(1)}, u32[]{:S(2)}, u32[]{:S(2)}) async-start(bf16[16,16,1024]{2,1,0:T(8,128)(2,1)} %broadcast_in_dim.8), calls=%async_computation.7 | async-start | bytes 1048576 | tf_op jit(solution)/shard_map/all_to_all | solution.py:334
  195.9 39.2 %collective-permute-start.13 = (bf16[256,1024]{1,0:T(8,128)(2,1)S(1)}, bf16[256,1024]{1,0:T(8,128)(2,1)S(1)}, u32[]{:S(2)}, u32[]{:S(2)}) collective-permute-start(bf16[256,1024]{1,0:T(8,128)(2,1)S(1)} %bitcast.18), channel_id=1, source_target_pairs={{0,16},{16,0},{1,17},{17,1},{2,18},{18,2},{3,19},{19,3},{4,20},{20... | collective-permute-start | bytes 1572872 | tf_op jit(solution)/shard_map/ppermute | solution.py:316
  196.0 35.4 %collective-permute-start.15 = (bf16[256,512]{1,0:T(8,128)(2,1)S(1)}, bf16[256,512]{1,0:T(8,128)(2,1)S(1)}, u32[]{:S(2)}, u32[]{:S(2)}) collective-permute-start(bf16[256,512]{1,0:T(8,128)(2,1)S(1)} %bitcast.26), channel_id=1, source_target_pairs={{0,16},{16,0},{1,17},{17,1},{2,18},{18,2},{3,19},{19,3},{4,20},{20... | collective-permute-start | bytes 786440 | tf_op jit(solution)/shard_map/ppermute | solution.py:316
  220.6 10.0 %collective-permute-start.22 = (f32[8,128]{1,0:T(8,128)S(1)}, f32[8,128]{1,0:T(8,128)S(1)}, u32[]{:S(2)}, u32[]{:S(2)}) collective-permute-start(f32[8,128]{1,0:T(8,128)S(1)} %add.70), channel_id=1, source_target_pairs={{0,8},{1,9},{2,10},{3,11},{4,12},{5,13},{6,14},{7,15},{8,0},{9,1},... | collective-permute-start | bytes 12296 | tf_op jit(solution)/shard_map/ppermute | solution.py:322
  230.7 9.9 %collective-permute-start.17 = (bf16[256,1024]{1,0:T(8,128)(2,1)S(1)}, bf16[256,1024]{1,0:T(8,128)(2,1)S(1)}, u32[]{:S(2)}, u32[]{:S(2)}) collective-permute-start(bf16[256,1024]{1,0:T(8,128)(2,1)S(1)} %bitcast.21), channel_id=1, source_target_pairs={{0,16},{16,0},{1,17},{17,1},{2,18},{18,2},{3,19},{19,3},{4,20},{20... | collective-permute-start | bytes 1572872 | tf_op jit(solution)/shard_map/ppermute | solution.py:316
  (21 other events, 237.2 us)

commit v2 on v0

v2 whole, which is shorter than its diff:
```python
import functools
import math

import jax
import jax.numpy as jnp
from jax import lax
from jax.experimental import pallas as pl
from jax.experimental.pallas import tpu as pltpu
from jax.sharding import PartitionSpec as P

HEAD_DIM = 64
TILE = 128
LANES = 128

f32 = jnp.float32
bf16 = jnp.bfloat16
NN = (((1,), (0,)), ((), ()))
NT = (((1,), (1,)), ((), ()))
TN = (((0,), (0,)), ((), ()))

VMEM = pl.BlockSpec(memory_space=pltpu.VMEM)
SMEM = pl.BlockSpec(memory_space=pltpu.SMEM)


def shape(*dims, dtype=f32):
    return jax.ShapeDtypeStruct(dims, dtype)


def call(body, outs, scalars, arrays, after=(), megabytes=8, far=(), us=0.3):
    n_in, n_after, n_far = len(scalars) + len(arrays), len(after), len(far)

    def kernel(*refs):
        outs_at = n_in + n_after + n_far
        sources, given = refs[n_in + n_after : outs_at], refs[outs_at : outs_at + len(outs)]
        targets, sems = refs[outs_at + len(outs) : outs_at + len(outs) + n_far], refs[-1]
        moves = [pltpu.make_async_copy(sources[i], targets[i], sems.at[i]) for i in range(n_far)]
        for move in moves:
            move.start()
        for move in moves:
            move.wait()
        body(*refs[:n_in], *targets, *given)

    scratch = [pltpu.VMEM(x.shape, x.dtype) for x in far]
    return pl.pallas_call(
        kernel,
        out_shape=list(outs),
        in_specs=[SMEM] * len(scalars)
        + [VMEM] * (len(arrays) + n_after)
        + [pl.BlockSpec(memory_space=pltpu.HBM)] * n_far,
        out_specs=[VMEM] * len(outs),
        scratch_shapes=scratch + ([pltpu.SemaphoreType.DMA((n_far,))] if n_far else []),
        compiler_params=pltpu.CompilerParams(vmem_limit_bytes=megabytes * 1024 * 1024),
        cost_estimate=pl.CostEstimate(
            flops=int(us * 1.1e9),
            bytes_accessed=sum(x.size * x.dtype.itemsize for x in (*arrays, *far)),
            transcendentals=0,
        ),
    )(*scalars, *arrays, *after, *far)


def on_core_zero(place_ref):
    return place_ref[0:1, 0:1] == 0


def bit_is_zero(place_ref, bit):
    return place_ref[1 + bit : 2 + bit, 0:1] == 0


def mm(a, b, dims=NN):
    return lax.dot_general(a, b, dims, preferred_element_type=f32)


def split(x):
    high = x.astype(bf16)
    return high, (x - high.astype(f32)).astype(bf16)


def mm_exact_right(a, b, dims=NN):
    high, low = split(a)
    return mm(high, b, dims) + mm(low, b, dims)


def mm_exact_left(a, b, dims=NN):
    high, low = split(b)
    return mm(a, high, dims) + mm(a, low, dims)


def mm_wide(a, b, dims=NN):
    ah, al = split(a)
    bh, bl = split(b)
    return mm(ah, bh, dims) + (mm(ah, bl, dims) + mm(al, bh, dims))


def iota(dims, axis):
    return lax.broadcasted_iota(jnp.int32, dims, axis)


def one_hot_rows(index_row, count):
    return jnp.where(iota((count, index_row.shape[1]), 0) == index_row, 1.0, 0.0).astype(bf16)


def head_mask():
    return (iota((LANES, LANES), 0) < HEAD_DIM) == (iota((LANES, LANES), 1) < HEAD_DIM)


def block_diagonal(packed):
    return jnp.where(head_mask(), jnp.concatenate([packed, packed], axis=0), 0.0)


def pack_diagonal(full):
    left = iota((HEAD_DIM, LANES), 1) < HEAD_DIM
    return jnp.where(left, full[:HEAD_DIM], full[HEAD_DIM:])


def store_summary(place_ref, packed, rows, mine_ref, theirs_ref, extra=None):
    zero = on_core_zero(place_ref)
    half = len(packed) // 2
    first = iota((8, LANES), 0) == 0
    if extra is not None:
        at = slice(HEAD_DIM + 8, HEAD_DIM + 16)
        mine_ref[at, :] = jnp.zeros((8, mine_ref.shape[1]), f32)
        theirs_ref[at, :] = jnp.zeros((8, mine_ref.shape[1]), f32)
        mine_ref[at, :LANES] = jnp.where(zero, extra, 0.0)
        theirs_ref[at, :LANES] = jnp.where(zero, 0.0, extra)
    for p in range(half):
        at = slice(p * LANES, (p + 1) * LANES)
        low = jnp.concatenate([packed[p], jnp.where(first, rows[p], 0.0)], axis=0)
        high = jnp.concatenate([packed[p + half], jnp.where(first, rows[p + half], 0.0)], axis=0)
        mine_ref[: HEAD_DIM + 8, at] = jnp.where(zero, low, high)
        theirs_ref[: HEAD_DIM + 8, at] = jnp.where(zero, high, low)


def load_summary(place_ref, pair, pairs, mine_ref, theirs_ref):
    half = pairs // 2
    at = slice(pair % half * LANES, (pair % half + 1) * LANES)
    low, high = (mine_ref, theirs_ref) if pair < half else (theirs_ref, mine_ref)
    both = jnp.where(on_core_zero(place_ref), low[:, at], high[:, at])
    return both[:HEAD_DIM], both[HEAD_DIM : HEAD_DIM + 1]


def store_halves(place_ref, whole, mine_ref, theirs_ref, at):
    zero = on_core_zero(place_ref)
    rows = whole.shape[0] // 2
    low, high = whole[:rows], whole[rows:]
    mine_ref[:, at] = jnp.where(zero, low, high)
    theirs_ref[:, at] = jnp.where(zero, high, low).astype(bf16)


def send_row(send_ref):
    return jnp.concatenate([send_ref[p : p + 1, :] for p in range(send_ref.shape[0])], axis=1)


def gather_kernel(send_ref, features_ref, out_ref):
    pick = one_hot_rows(send_row(send_ref), features_ref.shape[0])
    out_ref[...] = mm(pick, features_ref[...], TN).astype(bf16)


def project_kernel(
    place_ref, features_ref, wk_ref, wv_ref, wq_ref, ek_ref, v_ref, eq_ref, mine_ref, theirs_ref
):
    features = features_ref[...]
    pairs = features.shape[1] // LANES
    ek_ref[...] = jnp.exp(mm(features, wk_ref[...]))
    v_ref[...] = mm(features, wv_ref[...])
    packed, sums = [], []
    for p in range(pairs):
        at = slice(p * LANES, (p + 1) * LANES)
        key = ek_ref[:, at]
        packed.append(pack_diagonal(mm_wide(key, v_ref[:, at], TN)))
        sums.append(jnp.sum(key, axis=0, keepdims=True))
    store_summary(place_ref, packed, sums, mine_ref, theirs_ref)
    eq_ref[...] = jnp.exp(mm(features, wq_ref[...]))


def attend_kernel(
    place_ref,
    eq_ref,
    cot_ref,
    sum_mine_ref,
    sum_theirs_ref,
    coef_ref,
    att_ref,
    num_ref,
    den_ref,
    mine_ref,
    theirs_ref,
):
    pairs = eq_ref.shape[1] // LANES
    same_head = jnp.where(head_mask(), 1.0, 0.0).astype(bf16)
    packed, sums = [], []
    for p in range(pairs):
        at = slice(p * LANES, (p + 1) * LANES)
        kv, ks = load_summary(place_ref, p, pairs, sum_mine_ref, sum_theirs_ref)
        kv = block_diagonal(kv)
        query = eq_ref[:, at]
        cot = cot_ref[:, at]
        inverse = 1.0 / mm_exact_right(query * ks, same_head)
        attended = mm_wide(query, kv) * inverse
        att_ref[:, at] = attended
        num_grad = cot * inverse
        den_grad = -mm_exact_right(cot * attended, same_head) * inverse
        num_ref[:, at] = num_grad
        den_ref[:, at] = den_grad
        packed.append(pack_diagonal(mm_wide(query, num_grad, TN)))
        sums.append(jnp.sum(query * den_grad, axis=0, keepdims=True))
    store_summary(place_ref, packed, sums, mine_ref, theirs_ref, coef_ref[...])


def query_kernel(
    place_ref,
    eq_ref,
    num_ref,
    den_ref,
    sum_mine_ref,
    sum_theirs_ref,
    ek_ref,
    att_ref,
    *refs,
):
    *conv_refs, features_ref, qblock_ref, layer_ref, mine_ref, theirs_ref = refs
    rows, width = eq_ref.shape
    pairs = width // LANES
    for p in range(pairs):
        at = slice(p * LANES, (p + 1) * LANES)
        kv, ks = load_summary(place_ref, p, pairs, sum_mine_ref, sum_theirs_ref)
        kv = block_diagonal(kv)
        query_side = mm_wide(num_ref[:, at], kv, NT) + den_ref[:, at] * ks
        qblock_ref[:, at] = (query_side * eq_ref[:, at]).astype(bf16)
    features = features_ref[...]
    store_halves(place_ref, mm(features, qblock_ref[...], TN), mine_ref, theirs_ref, slice(0, width))
    whole = mm_exact_left(features, ek_ref[...], TN)
    store_halves(place_ref, whole, mine_ref, theirs_ref, slice(width, 2 * width))
    for t, conv_ref in enumerate(conv_refs):
        at = slice(t * TILE, (t + 1) * TILE)
        layer_ref[at, :] = att_ref[at, :] + conv_ref[...]


def key_kernel(
    place_ref, ek_ref, v_ref, sum_mine_ref, sum_theirs_ref, features_ref, kblock_ref, mine_ref, theirs_ref
):
    pairs = ek_ref.shape[1] // LANES
    for p in range(pairs):
        at = slice(p * LANES, (p + 1) * LANES)
        dkv, dks = load_summary(place_ref, p, pairs, sum_mine_ref, sum_theirs_ref)
        key_side = mm_wide(v_ref[:, at], block_diagonal(dkv), NT) + dks
        kblock_ref[:, at] = (key_side * ek_ref[:, at]).astype(bf16)
    store_halves(place_ref, mm(features_ref[...], kblock_ref[...], TN), mine_ref, theirs_ref, slice(None))


def returned_kernel(send_ref, table_ref, returned_ref, out_ref):
    rows = out_ref.shape[0]
    out_ref[...] = table_ref[:rows, :] + mm(one_hot_rows(send_row(send_ref), rows), returned_ref[...])


def input_grad_kernel(
    place_ref,
    qblock_ref,
    kblock_ref,
    ek_ref,
    sum_mine_ref,
    sum_theirs_ref,
    graph_ref,
    wq_ref,
    wk_ref,
    wv_ref,
    out_ref,
):
    pairs = ek_ref.shape[1] // LANES
    blocks = []
    for p in range(pairs):
        at = slice(p * LANES, (p + 1) * LANES)
        dkv, _ = load_summary(place_ref, p, pairs, sum_mine_ref, sum_theirs_ref)
        blocks.append(mm_wide(ek_ref[:, at], block_diagonal(dkv)).astype(bf16))
    total = mm(qblock_ref[...], wq_ref[...], NT) + mm(kblock_ref[...], wk_ref[...], NT)
    out_ref[...] = total + mm(jnp.concatenate(blocks, axis=1), wv_ref[...], NT) + graph_ref[...]


def tile_hits(count_ref, dst_ref, r, tile):
    slots = dst_ref.shape[2]
    live = iota((TILE, slots), 1) < count_ref[r, tile]
    target = iota((TILE, slots), 0) == dst_ref[r, tile : tile + 1, :]
    hit = jnp.where(target & live, 1.0, 0.0)
    return hit / jnp.maximum(jnp.sum(hit, axis=1, keepdims=True), 1.0)


def tile_incidence(count_ref, coef_ref, dst_ref, tile):
    basis_count = coef_ref.shape[1]
    hits, scaled = [], [[] for _ in range(basis_count)]
    for r in range(dst_ref.shape[0]):
        hit = tile_hits(count_ref, dst_ref, r, tile)
        hits.append(hit)
        for b in range(basis_count):
            scaled[b].append(hit * coef_ref[r, b])
    high, low = split(jnp.concatenate([jnp.concatenate(part, axis=1) for part in scaled], axis=0))
    return jnp.concatenate(hits, axis=1), jnp.concatenate([high, low], axis=0)


def backward_kernel(count_ref, coef_ref, src_ref, dst_ref, grad_ref, *refs, tile):
    table_ref = refs[-1]
    _, scaled = tile_incidence(count_ref, coef_ref, dst_ref, tile)
    picks = [one_hot_rows(src_ref[r, tile : tile + 1, :], table_ref.shape[0]) for r in range(src_ref.shape[0])]
    grad = grad_ref[tile].astype(bf16)
    moved = mm(scaled, jnp.concatenate([grad, grad], axis=0), TN).astype(bf16)
    table = mm(jnp.concatenate(picks, axis=1), moved)
    table_ref[...] = table if tile == 0 else table + refs[0][...]


def one_hot_columns(index_row, count):
    lanes = index_row.shape[1]
    column = jnp.broadcast_to(index_row.astype(f32), (LANES, lanes)).T.astype(jnp.int32)
    blocks = [jnp.where(iota((lanes, LANES), 1) + j == column, 1.0, 0.0) for j in range(0, count, LANES)]
    return jnp.concatenate(blocks, axis=1).astype(bf16)


def forward_kernel(count_ref, coef_ref, src_ref, dst_ref, grad_ref, own_ref, halo_ref, bases_ref, *refs, tile, last):
    basis_ref, conv_ref, sums_ref = refs[-3:]
    relations, _, slots = src_ref.shape
    basis_count = bases_ref.shape[0]
    wide = basis_count * TILE
    rows, halo_rows = own_ref.shape[0], halo_ref.shape[0]
    hit, scaled = tile_incidence(count_ref, coef_ref, dst_ref, tile)
    picks = [one_hot_columns(src_ref[r, tile : tile + 1, :], rows + halo_rows) for r in range(relations)]
    pick = jnp.concatenate(picks, axis=0)
    edge_rows = (mm(pick[:, :rows], own_ref[...]) + mm(pick[:, rows:], halo_ref[...])).astype(bf16)
    both = mm(scaled, edge_rows)
    both = (both[:wide] + both[wide:]).astype(bf16)
    conv = None
    for b in range(basis_count):
        basis_in = both[b * TILE : (b + 1) * TILE]
        basis_ref[b] = basis_in
        part = mm(basis_in, bases_ref[b])
        conv = part if conv is None else conv + part
    conv_ref[...] = conv

    dots = mm(jnp.concatenate(split(grad_ref[tile]), axis=0), edge_rows, NT)
    dots = dots[:wide] + dots[wide:]
    row, lane = iota((8, LANES), 0), iota((8, LANES), 1)
    total = jnp.zeros((8, LANES), f32)
    for b in range(basis_count):
        sums = jnp.sum(dots[b * TILE : (b + 1) * TILE] * hit, axis=0, keepdims=True)
        if tile > 0:
            sums += refs[0][b : b + 1, :]
        if not last:
            sums_ref[b : b + 1, :] = sums
            continue
        for r in range(relations):
            part = jnp.sum(sums[:, r * slots : (r + 1) * slots], axis=1, keepdims=True)
            total = jnp.where((row == r) & (lane == b), part, total)
    if last:
        sums_ref[...] = total


def ship_kernel(table_ref, out_ref):
    out_ref[...] = table_ref[table_ref.shape[0] - out_ref.shape[0] :, :].astype(bf16)


def bases_kernel(place_ref, *refs, parts, basis_count):
    cot_ref, mine_ref, theirs_ref = refs[parts:]
    width = cot_ref.shape[1]
    cot = cot_ref[...].astype(bf16)
    for b in range(basis_count):
        basis_in = jnp.concatenate([refs[i][b] for i in range(parts)], axis=0)
        at = slice(b * width, (b + 1) * width)
        store_halves(place_ref, mm(basis_in, cot, TN), mine_ref, theirs_ref, at)


def basis_grad_kernel(bases_ref, cot_ref, out_ref, *, tiles):
    cot = cot_ref[...].astype(bf16)
    for b in range(bases_ref.shape[0]):
        grad = mm(cot, bases_ref[b], NT)
        for t in range(tiles):
            out_ref[t, b * TILE : (b + 1) * TILE, :] = grad[t * TILE : (t + 1) * TILE]


def add_kernel(a_ref, b_ref, out_ref):
    out_ref[...] = a_ref[...] + b_ref[...]


def choose(place_ref, first_bit, blocks, index):
    bit = first_bit
    while len(blocks) > 1:
        zero = bit_is_zero(place_ref, bit)
        pairs = [(blocks[i], blocks[i + 1]) for i in range(0, len(blocks), 2)]
        if index % 2:
            blocks = [jnp.where(zero, high, low) for low, high in pairs]
        else:
            blocks = [jnp.where(zero, low, high) for low, high in pairs]
        index //= 2
        bit += 1
    return blocks[0]


def scatter_kernel(place_ref, *refs, first_bit, sources):
    keep_ref, *send_refs = refs[sum(sources) :]
    rows = keep_ref.shape[0]
    count = len(send_refs) + 1
    at = 0
    for n in sources:
        parts, refs = refs[:n], refs[n:]
        width = parts[0].shape[1]
        blocks = []
        for i in range(count):
            rows_at = slice(i * rows, (i + 1) * rows)
            total = parts[0][rows_at, :].astype(f32)
            for part in parts[1:]:
                total += part[rows_at, :].astype(f32)
            blocks.append(total)
        lanes = slice(at, at + width)
        keep_ref[:, lanes] = choose(place_ref, first_bit, blocks, 0)
        for k in range(1, count):
            send_refs[k - 1][:, lanes] = choose(place_ref, first_bit, blocks, k).astype(send_refs[k - 1].dtype)
        at += width


def total_kernel(*refs):
    out_ref = refs[-1]
    total = refs[0][...].astype(f32)
    for ref in refs[1:-1]:
        total += ref[...].astype(f32)
    out_ref[...] = total.astype(out_ref.dtype)


def join_kernel(place_ref, *refs, first_bit):
    out_ref = refs[-1]
    blocks = [ref[...] for ref in refs[:-1]]
    rows = blocks[0].shape[0]
    for i in range(len(blocks)):
        out_ref[i * rows : (i + 1) * rows, :] = choose(place_ref, first_bit, blocks, i)


def finish_kernel(place_ref, sum_mine_ref, sum_theirs_ref, mine_ref, theirs_ref, *refs, scale, basis_count):
    bases_ref, *outs = refs[:4]
    outs = [bases_ref.at[b] for b in range(basis_count)] + outs
    holds, sems = refs[4:-1], refs[-1]
    zero = on_core_zero(place_ref)
    rows = mine_ref.shape[0]
    width = holds[0].shape[1]
    moves = []
    for i, hold in enumerate(holds):
        for p in range(width // LANES):
            at = slice(p * LANES, (p + 1) * LANES)
            source = slice(i * width + p * LANES, i * width + (p + 1) * LANES)
            if i == basis_count + 1:
                dkv, _ = load_summary(place_ref, p, width // LANES, sum_mine_ref, sum_theirs_ref)
                dkv = block_diagonal(dkv)
                a = mm_exact_left(mine_ref[:, source], dkv) * scale
                b = mm_exact_left(theirs_ref[:, source], dkv) * scale
            else:
                a = mine_ref[:, source].astype(f32) * scale
                b = theirs_ref[:, source].astype(f32) * scale
            hold[:rows, at] = jnp.where(zero, a, b)
            hold[rows:, at] = jnp.where(zero, b, a)
        moves.append(pltpu.make_async_copy(hold, outs[i], sems.at[i]))
        moves[-1].start()
    for move in moves:
        move.wait()


def swap_cores(x):
    return lax.ppermute(x, "outer", [(0, 1), (1, 0)])


def swap_nodes(x, bit):
    nodes = lax.axis_size("nodes")
    return lax.ppermute(x, "nodes", [(i, i ^ (1 << bit)) for i in range(nodes)])


def sum_summary(mine, theirs, bits, beside):
    out = [shape(*mine.shape)]
    received = swap_cores(theirs)
    (mine,) = call(add_kernel, out, [], [mine, received], beside("core", mine))
    for bit in bits:
        received = swap_nodes(mine, bit)
        (mine,) = call(add_kernel, out, [], [mine, received], beside(bit, mine))
    return mine, swap_cores(mine), beside("back", mine)


def exchange(sends, first_bit):
    nodes = lax.axis_size("nodes")
    return [
        lax.ppermute(x, "nodes", [(i, i ^ (k << first_bit)) for i in range(nodes)])
        for k, x in enumerate(sends, start=1)
    ]


def per_device(
    features, w_query, w_key, w_value, bases, rel_coef, send_rows, tile_src, tile_dst, tile_count, cotangent
):
    rows, width = features.shape
    nodes = lax.axis_size("nodes")
    scale = 1.0 / math.sqrt(rows * nodes * lax.axis_size("outer"))
    basis_count = bases.shape[0]
    slots = send_rows.shape[2]
    halo_rows = nodes * slots
    table_rows = rows + halo_rows
    core, node = lax.axis_index("outer"), lax.axis_index("nodes")
    place = jnp.stack([core] + [(node >> bit) & 1 for bit in range(7)]).astype(jnp.int32)
    place = jnp.broadcast_to(place[:, None], (8, LANES))
    send, src, dst, count = send_rows[0], tile_src[0], tile_dst[0], tile_count[0]
    relations, tiles, cap = src.shape
    bits = list(range(nodes.bit_length() - 1))
    y, z1, z2 = bits[-3:]

    square, square_half = shape(rows, width), shape(rows, width, dtype=bf16)
    summary = shape(HEAD_DIM + 8, width // 2)
    wide_summary = shape(HEAD_DIM + 16, width // 2)

    def halves(n):
        return shape(width // 2, n * width), shape(width // 2, n * width, dtype=bf16)

    (outgoing,) = call(gather_kernel, [shape(halo_rows, width, dtype=bf16)], [], [send], far=[features], us=1.4)
    halo = lax.all_to_all(
        outgoing.reshape(nodes, slots, width), "nodes", split_axis=0, concat_axis=0, tiled=True
    ).reshape(halo_rows, width)
    exp_key, values, exp_query, kv_mine, kv_theirs = call(
        project_kernel,
        [square, square, square, summary, summary],
        [],
        [place],
        far=[features, w_key, w_value, w_query],
        us=1.8,
    )

    kept = {}

    def run_basis_grad(x):
        (kept["grad"],) = call(
            functools.partial(basis_grad_kernel, tiles=tiles),
            [shape(tiles, basis_count * TILE, width)],
            [],
            [],
            [x],
            far=[bases, cotangent],
            us=1.1,
        )
        return kept["grad"]

    def run_backward(t, x):
        (kept["table"],) = call(
            functools.partial(backward_kernel, tile=t),
            [shape(table_rows, width)],
            [count, rel_coef],
            [src, dst, kept["grad"]] + ([kept["table"]] if t > 0 else []),
            [x],
            table_rows // 64,
            us=2.7,
        )
        return kept["table"]

    def run_forward(t, x):
        last = t == tiles - 1
        outs = [shape(basis_count, TILE, width, dtype=bf16), shape(TILE, width)]
        outs.append(shape(8, LANES) if last else shape(8, relations * cap))
        kept["basis", t], kept["conv", t], kept["coef"] = call(
            functools.partial(forward_kernel, tile=t, last=last),
            outs,
            [count, rel_coef],
            [src, dst, kept["grad"], features, halo, bases] + ([kept["coef"]] if t > 0 else []),
            [x],
            table_rows // 64,
            us=3.3,
        )
        return kept["coef"]

    def run_bases(x):
        kept["bases"] = call(
            functools.partial(bases_kernel, parts=tiles, basis_count=basis_count),
            halves(basis_count),
            [],
            [place, *[kept["basis", t] for t in range(tiles)], cotangent],
            [x],
            us=0.8,
        )
        return kept["bases"][1]

    def run_ship(x):
        (sent,) = call(ship_kernel, [shape(halo_rows, width, dtype=bf16)], [], [kept["table"]], [x])
        kept["returned"] = lax.all_to_all(
            sent.reshape(nodes, slots, width), "nodes", split_axis=0, concat_axis=0, tiled=True
        ).reshape(halo_rows, width)
        return sent

    backward = [functools.partial(run_backward, t) for t in range(tiles)]
    forward = [functools.partial(run_forward, t) for t in range(tiles)]
    first = {"core": [run_basis_grad], bits[0]: backward[:1], y: backward[1:2], z1: backward[2:3], z2: backward[3:]}
    first["back"] = [run_ship, *forward, run_bases]
    kv_mine, kv_theirs, after = sum_summary(
        kv_mine, kv_theirs, bits, lambda step, x: [run(x) for run in first.get(step, [])]
    )
    attended, num_grad, den_grad, dkv_mine, dkv_theirs = call(
        attend_kernel,
        [square, square, square, wide_summary, wide_summary],
        [],
        [place, exp_query, cotangent, kv_mine, kv_theirs, kept["coef"]],
        after,
        us=2.0,
    )

    plane, planes = nodes // 4, 4
    plane_rows = width // 2 // plane
    place_rows = plane_rows // planes
    early_width, whole_width = (basis_count + 2) * width, (basis_count + 3) * width

    def sends(n, rows, columns):
        return [shape(rows, columns)] + [shape(rows, columns, dtype=bf16 if rows >= 16 else f32)] * (n - 1)

    def run_returned(x):
        (kept["graph"],) = call(
            returned_kernel, [square], [], [send, kept["table"], kept["returned"]], [x], us=0.5
        )
        return kept["graph"]

    def run_query(x):
        operands = [exp_query, num_grad, den_grad, kv_mine, kv_theirs, exp_key, attended]
        operands += [kept["conv", t] for t in range(tiles)]
        kept["qblock"], kept["layer"], *kept["early"] = call(
            query_kernel,
            [square_half, square, *halves(2)],
            [],
            [place, *operands],
            [x],
            12,
            far=[features],
            us=2.7,
        )
        return kept["early"][1]

    def run_early(x):
        operands = []
        for mine, theirs in (kept["bases"], kept["early"]):
            operands += [mine, swap_cores(theirs)]
        kept["early own"], *out = call(
            functools.partial(scatter_kernel, first_bit=0, sources=[2, 2]),
            sends(plane, plane_rows, early_width),
            [],
            [place, *operands],
            [x],
            12,
        )
        kept["early received"] = exchange(out, 0)
        return kept["early own"]

    def run_early_sum(x):
        (kept["early own"],) = call(
            total_kernel,
            [shape(plane_rows, early_width)],
            [],
            [kept["early own"], *kept["early received"]],
            [x],
        )
        return kept["early own"]

    second = {"core": [run_query], bits[0]: [run_returned], y: [run_early], "back": [run_early_sum]}
    dkv_mine, dkv_theirs, after = sum_summary(
        dkv_mine, dkv_theirs, bits, lambda step, x: [run(x) for run in second.get(step, [])]
    )
    kblock, key_mine, key_theirs = call(
        key_kernel,
        [square_half, *halves(1)],
        [],
        [place, exp_key, values, dkv_mine, dkv_theirs],
        after,
        far=[features],
        us=1.1,
    )
    key_own, *out = call(
        functools.partial(scatter_kernel, first_bit=0, sources=[2]),
        sends(plane, plane_rows, width),
        [],
        [place, key_mine, swap_cores(key_theirs)],
    )
    received = exchange(out, 0)
    (grad_x,) = call(
        input_grad_kernel,
        [square],
        [],
        [place, kept["qblock"], kblock, exp_key, dkv_mine, dkv_theirs, kept["graph"]],
        [key_own],
        16,
        far=[w_query, w_key, w_value],
        us=3.5,
    )
    own, *out = call(
        functools.partial(scatter_kernel, first_bit=z1, sources=[1, plane]),
        sends(planes, place_rows, whole_width),
        [],
        [place, kept["early own"], key_own, *received],
    )
    total_type = bf16 if place_rows >= 16 else f32
    (own,) = call(
        total_kernel, [shape(place_rows, whole_width, dtype=total_type)], [], [own, *exchange(out, z1)]
    )
    (own,) = call(
        functools.partial(join_kernel, first_bit=z1),
        [shape(plane_rows, whole_width, dtype=total_type)],
        [],
        [place, own, *exchange([own] * (planes - 1), z1)],
    )
    own = own.astype(bf16)
    (own,) = call(
        functools.partial(join_kernel, first_bit=0),
        [shape(width // 2, whole_width, dtype=bf16)],
        [],
        [place, own, *exchange([own] * (plane - 1), 0)],
    )
    count_out = basis_count + 3
    bases_grad, query_grad, value_grad, key_grad = pl.pallas_call(
        functools.partial(finish_kernel, scale=scale, basis_count=basis_count),
        out_shape=[shape(basis_count, width, width)] + [shape(width, width)] * 3,
        in_specs=[VMEM] * 5,
        out_specs=[pl.BlockSpec(memory_space=pltpu.HBM)] * 4,
        scratch_shapes=[pltpu.VMEM((width, width), f32)] * count_out + [pltpu.SemaphoreType.DMA((count_out,))],
        compiler_params=pltpu.CompilerParams(vmem_limit_bytes=16 * 1024 * 1024),
    )(place, dkv_mine, dkv_theirs, own, swap_cores(own))
    coef_sum = jnp.where(core == 0, dkv_mine, dkv_theirs)[HEAD_DIM + 8 :, :]
    coef_grad = coef_sum[:relations, :basis_count] * scale
    return kept["layer"], grad_x, query_grad, key_grad, value_grad, bases_grad, coef_grad


def solution(mesh):
    both = ("outer", "nodes")
    in_specs = (
        P(both, None),
        P(),
        P(),
        P(),
        P(),
        P(),
        P(both, None, None),
        P(both, None, None, None),
        P(both, None, None, None),
        P(both, None, None),
        P(both, None),
    )
    out_specs = (P(both, None), P(both, None), P(), P(), P(), P(), P())
    return jax.shard_map(per_device, mesh=mesh, in_specs=in_specs, out_specs=out_specs, check_vma=False)
```

time: 731 us -> 164 us (0.22)
  waiting for transfers between devices: 269 us -> 37.6 us
  matrix products: 125 us -> 0 us
  other arithmetic: 107 us -> 0.01 us
  local copies, waits for them, and re-layouts: 118 us -> 23.7 us
  blocking collectives: 79.9 us -> 0 us
  Pallas kernels: 0 us -> 49.6 us
  starting transfers between devices: 14.1 us -> 50.5 us
  between operations: 14.3 us -> 1.32 us
    psum x2 -> x0, waiting for transfers between devices: 241 us -> none  [the longest x1 122 us: per_device(): kv_sum, ks_sum = lax.psum((kv_part, ks_part), ('outer', 'nodes'))]
    dot_general x38 -> x0, matrix products: 125 us -> none  [the longest x8 89.1 us: backward_step(): jnp.einsum('b,bmd->md', coef_row, basis_grad, precision=precise)]
    psum x2 -> x0, blocking collectives: 79.9 us -> none  [the longest x1 40.6 us: per_device(): kv_sum, ks_sum = lax.psum((kv_part, ks_part), ('outer', 'nodes'))]
    scatter-add x9 -> x0, other arithmetic: 70.8 us -> none  [the longest x8 66.2 us: backward_step(): jax.ops.segment_sum(moved, sources.reshape(-1), num_segments=table_rows)]
    pallas_call x0 -> x36, Pallas kernels: none -> 49.6 us  [the longest x35 45.5 us: call(): pl.pallas_call(kernel, out_shape=list(outs), in_specs=[SMEM] * len(scalar...]
    ppermute x0 -> x31, waiting for transfers between devices: none -> 37.6 us  [the longest x15 27.5 us: exchange(): lax.ppermute(x, 'nodes', [(i, i ^ k << first_bit) for i in range(nodes)])]
    gather x17 -> x0, local copies, waits for them, and re-layouts: 35.4 us -> none  [the longest x16 31.5 us: tile_rows(): picked = halo_table[sources]]
    ppermute x0 -> x31, starting transfers between devices: none -> 35.3 us  [the longest x15 19.5 us: exchange(): lax.ppermute(x, 'nodes', [(i, i ^ k << first_bit) for i in range(nodes)])]
  transfers between devices with their start and end apart: 4 -> 33, of which waited for: 3 -> 19; matrix products, arithmetic and copies ran while one was open for 6% -> 1% of each run, Pallas kernels for 0% -> 26%
where the time goes in v2:
time: 164 us; the launch traced here: 163 us
  starting transfers between devices  50.5 us (31%)
  Pallas kernels  49.6 us (30%)
  waiting for transfers between devices  37.6 us (23%)
  local copies, waits for them, and re-layouts  23.7 us (14%)
    pallas_call x35, Pallas kernels, call(): pl.pallas_call(kernel, out_shape=list(outs), in_specs=[SMEM] * len(scalar...  45.5 us
    ppermute x15, waiting for transfers between devices, exchange(): lax.ppermute(x, 'nodes', [(i, i ^ k << first_bit) for i in range(nodes)])  27.5 us
    unnamed x84, local copies, waits for them, and re-layouts  23.5 us
    ppermute x15, starting transfers between devices, exchange(): lax.ppermute(x, 'nodes', [(i, i ^ k << first_bit) for i in range(nodes)])  19.5 us
    ppermute x8, starting transfers between devices, swap_nodes(): return lax.ppermute(x, 'nodes', [(i, i ^ 1 << bit) for i in range(nodes)])  14.8 us
    all_to_all x1, starting transfers between devices, per_device(): lax.all_to_all(outgoing.reshape(nodes, slots, width), 'nodes', split_axis...  8.32 us
    ppermute x8, waiting for transfers between devices, swap_nodes(): return lax.ppermute(x, 'nodes', [(i, i ^ 1 << bit) for i in range(nodes)])  6.89 us
    all_to_all x1, starting transfers between devices, run_ship(): lax.all_to_all(sent.reshape(nodes, slots, width), 'nodes', split_axis=0,...  6.8 us
  transfers between devices with their start and end apart: 33, of which 19 were waited for; matrix products, arithmetic and copies ran while one was open for 1% of the time, Pallas kernels for 26%

profile of v2, /device:TPU:0, one launch (start us, length us, event | category | flops | bytes accessed | tf_op | source)
XLA Modules:
  0.0 162.7 jit_solution(8345348886779098388)
XLA Ops:
  3.8 8.3 %all-to-all-start = ((bf16[16,32,512]{2,1,0:T(8,128)(2,1)}), bf16[16,32,512]{2,1,0:T(8,128)(2,1)S(1)}, u32[]{:S(2)}, u32[]{:S(2)}) async-start(bf16[16,32,512]{2,1,0:T(8,128)(2,1)} %bitcast.12), calls=%async_computation | async-start | bytes 1048576 | tf_op jit(solution)/shard_map/all_to_all | solution.py:512
  22.4 2.0 %collective-permute-start.1 = (f32[72,256]{1,0:T(8,128)S(1)}, f32[72,256]{1,0:T(8,128)S(1)}, u32[]{:S(2)}, u32[]{:S(2)}) collective-permute-start(f32[72,256]{1,0:T(8,128)S(1)} %shard_map.164.refs_5_.refs_0_), channel_id=1, source_target_pairs={{0,1},{1,0},{2,3},{3,2},{4,5},{5,4},{6,7},{7,6},{8,9},{9,8},{10,11... | collective-permute-start | bytes 221192 | tf_op jit(solution)/shard_map/ppermute | solution.py:465
  24.5 2.7 %shard_map.165.refs_2_.refs_5_ = f32[1024,512]{1,0:T(8,128)S(1)} custom-call(s32[8,4]{1,0:T(8,128)S(1)} %copy.18.refs_0_, f32[8,2]{1,0:T(8,128)S(1)} %copy.19.refs_1_, s32[8,4,128]{2,1,0:T(4,128)S(1)} %bitcast.23, s32[8,4,128]{2,1,0:T(4,128)S(1)} %bitcast.31, f32[4,256,512]{2,1,0:T(8,128)S(1)} %shard_map.163.refs_2_.refs_4_, ...), custom_call_target="tpu_custom_call" | custom-call | flops 2969999872 | bytes 2129920 | tf_op jit(solution)/shard_map/pallas_call | solution.py:44
  29.6 2.7 %shard_map.167.refs_2_.refs_5_ = f32[1024,512]{1,0:T(8,128)S(1)} custom-call(s32[8,4]{1,0:T(8,128)S(1)} %copy.18.refs_0_, f32[8,2]{1,0:T(8,128)S(1)} %copy.19.refs_1_, s32[8,4,128]{2,1,0:T(4,128)S(1)} %bitcast.24, s32[8,4,128]{2,1,0:T(4,128)S(1)} %bitcast.32, f32[4,256,512]{2,1,0:T(8,128)S(1)} %shard_map.163.refs_2_.refs_4_, ...), custom_call_target="tpu_custom_call" | custom-call | flops 2969999872 | bytes 4227072 | tf_op jit(solution)/shard_map/pallas_call | solution.py:44
  34.1 2.7 %shard_map.169.refs_2_.refs_5_ = f32[1024,512]{1,0:T(8,128)S(1)} custom-call(s32[8,4]{1,0:T(8,128)S(1)} %copy.18.refs_0_, f32[8,2]{1,0:T(8,128)S(1)} %copy.19.refs_1_, s32[8,4,128]{2,1,0:T(4,128)S(1)} %bitcast.25, s32[8,4,128]{2,1,0:T(4,128)S(1)} %bitcast.33, f32[4,256,512]{2,1,0:T(8,128)S(1)} %shard_map.163.refs_2_.refs_4_, ...), custom_call_target="tpu_custom_call" | custom-call | flops 2969999872 | bytes 4227072 | tf_op jit(solution)/shard_map/pallas_call | solution.py:44
  38.8 2.7 %shard_map.171.refs_2_.refs_0_.refs_1_ = f32[1024,512]{1,0:T(8,128)S(1)} custom-call(s32[8,4]{1,0:T(8,128)S(1)} %copy.18.refs_0_, f32[8,2]{1,0:T(8,128)S(1)} %copy.19.refs_1_, s32[8,4,128]{2,1,0:T(4,128)S(1)} %bitcast.26, s32[8,4,128]{2,1,0:T(4,128)S(1)} %bitcast.34, f32[4,256,512]{2,1,0:T(8,128)S(1)} %shard_map.163.refs_2_.refs_4_, ...), custom_call_target="tpu_custom_call" | custom-call | flops 2969999872 | bytes 4227072 | tf_op jit(solution)/shard_map/pallas_call | solution.py:44
  43.1 6.8 %all-to-all-start.1 = ((bf16[16,32,512]{2,1,0:T(8,128)(2,1)}), bf16[16,32,512]{2,1,0:T(8,128)(2,1)S(1)}, u32[]{:S(2)}, u32[]{:S(2)}) async-start(bf16[16,32,512]{2,1,0:T(8,128)(2,1)} %bitcast.14), calls=%async_computation.1 | async-start | bytes 1048576 | tf_op jit(solution)/shard_map/all_to_all | solution.py:578
  53.8 3.4 %shard_map.174 = (bf16[2,128,512]{2,1,0:T(8,128)(2,1)S(1)}, f32[128,512]{1,0:T(8,128)S(1)}, f32[8,1024]{1,0:T(8,128)S(1)}) custom-call(s32[8,4]{1,0:T(8,128)S(1)} %copy.18.refs_0_, f32[8,2]{1,0:T(8,128)S(1)} %copy.19.refs_1_, s32[8,4,128]{2,1,0:T(4,128)S(1)} %bitcast.27, s32[8,4,128]{2,1,0:T(4,128)S(1)} %bitcast.35, f32[4,256,512]{2,1,0:T(8,128)S(1)} %copy-done.3, ...), custom_call_target="tpu_custom_call" | custom-call | flops 3630000128 | bytes 4227072 | tf_op jit(solution)/shard_map/pallas_call | solution.py:44
  57.1 3.4 %shard_map.175 = (bf16[2,128,512]{2,1,0:T(8,128)(2,1)S(1)}, f32[128,512]{1,0:T(8,128)S(1)}, f32[8,1024]{1,0:T(8,128)S(1)}) custom-call(s32[8,4]{1,0:T(8,128)S(1)} %copy.18.refs_0_, f32[8,2]{1,0:T(8,128)S(1)} %copy.19.refs_1_, s32[8,4,128]{2,1,0:T(4,128)S(1)} %bitcast.28, s32[8,4,128]{2,1,0:T(4,128)S(1)} %bitcast.36, f32[4,256,512]{2,1,0:T(8,128)S(1)} %copy-done.3, ...), custom_call_target="tpu_custom_call" | custom-call | flops 3630000128 | bytes 4259840 | tf_op jit(solution)/shard_map/pallas_call | solution.py:44
  60.5 3.4 %shard_map.176 = (bf16[2,128,512]{2,1,0:T(8,128)(2,1)S(1)}, f32[128,512]{1,0:T(8,128)S(1)}, f32[8,1024]{1,0:T(8,128)S(1)}) custom-call(s32[8,4]{1,0:T(8,128)S(1)} %copy.18.refs_0_, f32[8,2]{1,0:T(8,128)S(1)} %copy.19.refs_1_, s32[8,4,128]{2,1,0:T(4,128)S(1)} %bitcast.29, s32[8,4,128]{2,1,0:T(4,128)S(1)} %bitcast.37, f32[4,256,512]{2,1,0:T(8,128)S(1)} %copy-done.3, ...), custom_call_target="tpu_custom_call" | custom-call | flops 3630000128 | bytes 4259840 | tf_op jit(solution)/shard_map/pallas_call | solution.py:44
  63.9 3.4 %shard_map.177 = (bf16[2,128,512]{2,1,0:T(8,128)(2,1)S(1)}, f32[128,512]{1,0:T(8,128)S(1)}, f32[8,128]{1,0:T(8,128)S(1)}) custom-call(s32[8,4]{1,0:T(8,128)S(1)} %copy.18.refs_0_, f32[8,2]{1,0:T(8,128)S(1)} %copy.19.refs_1_, s32[8,4,128]{2,1,0:T(4,128)S(1)} %bitcast.30, s32[8,4,128]{2,1,0:T(4,128)S(1)} %bitcast.38, f32[4,256,512]{2,1,0:T(8,128)S(1)} %copy-done.3, ...), custom_call_target="tpu_custom_call" | custom-call | flops 3630000128 | bytes 4259840 | tf_op jit(solution)/shard_map/pallas_call | solution.py:44
  70.1 3.4 %shard_map.180 = (f32[512,512]{1,0:T(8,128)S(1)}, f32[512,512]{1,0:T(8,128)S(1)}, f32[512,512]{1,0:T(8,128)S(1)}, f32[80,256]{1,0:T(8,128)S(1)}, f32[80,256]{1,0:T(8,128)S(1)}) custom-call(s32[8,128]{1,0:T(8,128)S(1)} %broadcast_in_dim.2.refs_0_.place_ref, f32[512,512]{1,0:T(8,128)S(1)} %copy-done.36, f32[512,512]{1,0:T(8,128)S(1)} %copy-done.13, ...), custom_call_target="tpu_custom_call" | custom-call | flops 2200000000 | bytes 2252800 | tf_op jit(solution)/shard_map/pallas_call | solution.py:44
  73.6 3.1 %shard_map.181 = (bf16[512,512]{1,0:T(8,128)(2,1)S(1)}, f32[512,512]{1,0:T(8,128)}, f32[256,1024]{1,0:T(8,128)S(1)}, bf16[256,1024]{1,0:T(8,128)(2,1)}) custom-call(s32[8,128]{1,0:T(8,128)S(1)} %broadcast_in_dim.2.refs_0_.place_ref, f32[512,512]{1,0:T(8,128)S(1)} %copy-done.36, f32[512,512]{1,0:T(8,128)S(1)} %get-tuple-element.66.refs_2_, ...), custom_call_target="tpu_custom_call" | custom-call | flops 2969999872 | bytes 6967296 | tf_op jit(solution)/shard_map/pallas_call | solution.py:44
  95.0 2.4 %collective-permute-start.12 = (f32[80,256]{1,0:T(8,128)S(1)}, f32[80,256]{1,0:T(8,128)S(1)}, u32[]{:S(2)}, u32[]{:S(2)}) collective-permute-start(f32[80,256]{1,0:T(8,128)S(1)} %shard_map.187.refs_0_), channel_id=1, source_target_pairs={{0,8},{1,9},{2,10},{3,11},{4,12},{5,13},{6,14},{7,15},{8,0},{9,1},... | collective-permute-start | bytes 245768 | tf_op jit(solution)/shard_map/ppermute | solution.py:465
  97.4 3.9 %collective-permute-done.12.refs_1_ = f32[80,256]{1,0:T(8,128)S(1)} collective-permute-done((f32[80,256]{1,0:T(8,128)S(1)}, f32[80,256]{1,0:T(8,128)S(1)}, u32[]{:S(2)}, u32[]{:S(2)}) %collective-permute-start.12) | collective-permute-done | bytes 81952 | tf_op jit(solution)/shard_map/ppermute | solution.py:465
  101.4 3.0 %collective-permute-done.15.refs_2_ = bf16[64,2048]{1,0:T(8,128)(2,1)S(1)} collective-permute-done((bf16[64,2048]{1,0:T(8,128)(2,1)S(1)}, bf16[64,2048]{1,0:T(8,128)(2,1)S(1)}, u32[]{:S(2)}, u32[]{:S(2)}) %collective-permute-start.15) | collective-permute-done | bytes 262176 | tf_op jit(solution)/shard_map/ppermute | solution.py:481
  115.5 2.4 %collective-permute-start.22 = (bf16[16,2560]{1,0:T(8,128)(2,1)S(1)}, bf16[16,2560]{1,0:T(8,128)(2,1)S(1)}, u32[]{:S(2)}, u32[]{:S(2)}) collective-permute-start(bf16[16,2560]{1,0:T(8,128)(2,1)S(1)} %get-tuple-element.95), channel_id=1, source_target_pairs={{0,8},{1,9},{2,10},{3,11},{4,12},{5,13},{6,14},{7,15},{8,0},{9,1},... | collective-permute-start | bytes 245768 | tf_op jit(solution)/shard_map/ppermute | solution.py:481
  119.3 3.8 %collective-permute-done.22.refs_2_ = bf16[16,2560]{1,0:T(8,128)(2,1)S(1)} collective-permute-done((bf16[16,2560]{1,0:T(8,128)(2,1)S(1)}, bf16[16,2560]{1,0:T(8,128)(2,1)S(1)}, u32[]{:S(2)}, u32[]{:S(2)}) %collective-permute-start.22) | collective-permute-done | bytes 81952 | tf_op jit(solution)/shard_map/ppermute | solution.py:481
  124.1 2.6 %collective-permute-start.26 = (bf16[16,2560]{1,0:T(8,128)(2,1)S(1)}, bf16[16,2560]{1,0:T(8,128)(2,1)S(1)}, u32[]{:S(2)}, u32[]{:S(2)}) collective-permute-start(bf16[16,2560]{1,0:T(8,128)(2,1)S(1)} %shard_map.194.refs_1_), channel_id=1, source_target_pairs={{0,12},{1,13},{2,14},{3,15},{4,8},{5,9},{6,10},{7,11},{8,4},{9,5},... | collective-permute-start | bytes 245768 | tf_op jit(solution)/shard_map/ppermute | solution.py:481
  128.6 2.7 %collective-permute-done.26.refs_4_ = bf16[16,2560]{1,0:T(8,128)(2,1)S(1)} collective-permute-done((bf16[16,2560]{1,0:T(8,128)(2,1)S(1)}, bf16[16,2560]{1,0:T(8,128)(2,1)S(1)}, u32[]{:S(2)}, u32[]{:S(2)}) %collective-permute-start.26) | collective-permute-done | bytes 81952 | tf_op jit(solution)/shard_map/ppermute | solution.py:481
  136.9 7.9 %collective-permute-done.29.refs_4_ = bf16[64,2560]{1,0:T(8,128)(2,1)S(1)} collective-permute-done((bf16[64,2560]{1,0:T(8,128)(2,1)S(1)}, bf16[64,2560]{1,0:T(8,128)(2,1)S(1)}, u32[]{:S(2)}, u32[]{:S(2)}) %collective-permute-start.29) | collective-permute-done | bytes 327712 | tf_op jit(solution)/shard_map/ppermute | solution.py:481
  144.8 3.5 %collective-permute-done.28.refs_3_ = bf16[64,2560]{1,0:T(8,128)(2,1)S(1)} collective-permute-done((bf16[64,2560]{1,0:T(8,128)(2,1)S(1)}, bf16[64,2560]{1,0:T(8,128)(2,1)S(1)}, u32[]{:S(2)}, u32[]{:S(2)}) %collective-permute-start.28) | collective-permute-done | bytes 327712 | tf_op jit(solution)/shard_map/ppermute | solution.py:481
  155.9 2.5 %shard_map.192 = f32[512,512]{1,0:T(8,128)} custom-call(s32[8,128]{1,0:T(8,128)S(1)} %broadcast_in_dim.2.refs_0_.place_ref, bf16[512,512]{1,0:T(8,128)(2,1)S(1)} %copy-done.38, bf16[512,512]{1,0:T(8,128)(2,1)S(1)} %copy-done.34, f32[512,512]{1,0:T(8,128)S(1)} %copy-done.30, f32[80,256]{1,0:T(8,128)S(1)} %shard_map.188.refs_4_.refs_3_.sum_mine_ref, ...), custom_call_target="tpu_custom_call" | custom-call | flops 3849999872 | bytes 4886528 | tf_op jit(solution)/shard_map/pallas_call | solution.py:44
  158.5 4.0 %shard_map.197 = (f32[2,512,512]{2,1,0:T(8,128)}, f32[512,512]{1,0:T(8,128)}, f32[512,512]{1,0:T(8,128)}, f32[512,512]{1,0:T(8,128)}) custom-call(s32[8,128]{1,0:T(8,128)S(1)} %broadcast_in_dim.2.refs_0_.place_ref, f32[80,256]{1,0:T(8,128)S(1)} %shard_map.188.refs_4_.refs_3_.sum_mine_ref, ...), custom_call_target="tpu_custom_call" | custom-call | tf_op jit(solution)/shard_map/pallas_call | solution.py:707
  (166 shorter events, 74.7 us)
Async XLA Ops:
  3.8 39.3 %all-to-all-start = ((bf16[16,32,512]{2,1,0:T(8,128)(2,1)}), bf16[16,32,512]{2,1,0:T(8,128)(2,1)S(1)}, u32[]{:S(2)}, u32[]{:S(2)}) async-start(bf16[16,32,512]{2,1,0:T(8,128)(2,1)} %bitcast.12), calls=%async_computation | async-start | bytes 1048576 | tf_op jit(solution)/shard_map/all_to_all | solution.py:512
  22.4 5.5 %collective-permute-start.1 = (f32[72,256]{1,0:T(8,128)S(1)}, f32[72,256]{1,0:T(8,128)S(1)}, u32[]{:S(2)}, u32[]{:S(2)}) collective-permute-start(f32[72,256]{1,0:T(8,128)S(1)} %shard_map.164.refs_5_.refs_0_), channel_id=1, source_target_pairs={{0,1},{1,0},{2,3},{3,2},{4,5},{5,4},{6,7},{7,6},{8,9},{9,8},{10,11... | collective-permute-start | bytes 221192 | tf_op jit(solution)/shard_map/ppermute | solution.py:465
  36.8 5.3 %collective-permute-start.4 = (f32[72,256]{1,0:T(8,128)S(1)}, f32[72,256]{1,0:T(8,128)S(1)}, u32[]{:S(2)}, u32[]{:S(2)}) collective-permute-start(f32[72,256]{1,0:T(8,128)S(1)} %shard_map.170.refs_6_.refs_0_), channel_id=1, source_target_pairs={{0,8},{1,9},{2,10},{3,11},{4,12},{5,13},{6,14},{7,15},{8,0},{9,1},... | collective-permute-start | bytes 221192 | tf_op jit(solution)/shard_map/ppermute | solution.py:465
  42.2 28.0 %collective-permute-start.5 = (f32[72,256]{1,0:T(8,128)S(1)}, f32[72,256]{1,0:T(8,128)S(1)}, u32[]{:S(2)}, u32[]{:S(2)}) collective-permute-start(f32[72,256]{1,0:T(8,128)S(1)} %shard_map.172.refs_8_.refs_9_.refs_1_.refs_6_.refs_3_.refs_4_), channel_id=1, source_target_pairs={{0,16},{16,0},{1,17},{17,1},{2,18},{18,2},{3,19},{19,3},{4,20},{20... | collective-permute-start | bytes 221192 | tf_op jit(solution)/shard_map/ppermute | solution.py:460
  43.1 39.3 %all-to-all-start.1 = ((bf16[16,32,512]{2,1,0:T(8,128)(2,1)}), bf16[16,32,512]{2,1,0:T(8,128)(2,1)S(1)}, u32[]{:S(2)}, u32[]{:S(2)}) async-start(bf16[16,32,512]{2,1,0:T(8,128)(2,1)} %bitcast.14), calls=%async_computation.1 | async-start | bytes 1048576 | tf_op jit(solution)/shard_map/all_to_all | solution.py:578
  69.9 17.0 %collective-permute-start.9 = (bf16[256,1024]{1,0:T(8,128)(2,1)}, bf16[256,1024]{1,0:T(8,128)(2,1)}, u32[]{:S(2)}, u32[]{:S(2)}) collective-permute-start(bf16[256,1024]{1,0:T(8,128)(2,1)} %get-tuple-element.65.refs_11_), channel_id=1, source_target_pairs={{0,16},{16,0},{1,17},{17,1},{2,18},{18,2},{3,19},{19,3},{4,20},{20... | collective-permute-start | bytes 1572872 | tf_op jit(solution)/shard_map/ppermute | solution.py:460
  77.5 9.5 %collective-permute-start.10 = (bf16[256,1024]{1,0:T(8,128)(2,1)}, bf16[256,1024]{1,0:T(8,128)(2,1)}, u32[]{:S(2)}, u32[]{:S(2)}) collective-permute-start(bf16[256,1024]{1,0:T(8,128)(2,1)} %get-tuple-element.79.refs_2_), channel_id=1, source_target_pairs={{0,16},{16,0},{1,17},{17,1},{2,18},{18,2},{3,19},{19,3},{4,20},{20... | collective-permute-start | bytes 1572872 | tf_op jit(solution)/shard_map/ppermute | solution.py:460
  80.6 4.7 %collective-permute-start.7 = (f32[80,256]{1,0:T(8,128)S(1)}, f32[80,256]{1,0:T(8,128)S(1)}, u32[]{:S(2)}, u32[]{:S(2)}) collective-permute-start(f32[80,256]{1,0:T(8,128)S(1)} %shard_map.182.refs_3_.refs_0_), channel_id=1, source_target_pairs={{0,1},{1,0},{2,3},{3,2},{4,5},{5,4},{6,7},{7,6},{8,9},{9,8},{10,11... | collective-permute-start | bytes 245768 | tf_op jit(solution)/shard_map/ppermute | solution.py:465
  89.8 5.1 %collective-permute-start.11 = (f32[80,256]{1,0:T(8,128)S(1)}, f32[80,256]{1,0:T(8,128)S(1)}, u32[]{:S(2)}, u32[]{:S(2)}) collective-permute-start(f32[80,256]{1,0:T(8,128)S(1)} %shard_map.186.refs_0_), channel_id=1, source_target_pairs={{0,4},{1,5},{2,6},{3,7},{4,0},{5,1},{6,2},{7,3},{8,12},{9,13},{10,... | collective-permute-start | bytes 245768 | tf_op jit(solution)/shard_map/ppermute | solution.py:465
  91.5 9.9 %collective-permute-start.14 = (bf16[64,2048]{1,0:T(8,128)(2,1)S(1)}, bf16[64,2048]{1,0:T(8,128)(2,1)S(1)}, u32[]{:S(2)}, u32[]{:S(2)}) collective-permute-start(bf16[64,2048]{1,0:T(8,128)(2,1)S(1)} %get-tuple-element.83), channel_id=1, source_target_pairs={{0,1},{1,0},{2,3},{3,2},{4,5},{5,4},{6,7},{7,6},{8,9},{9,8},{10,11... | collective-permute-start | bytes 786440 | tf_op jit(solution)/shard_map/ppermute | solution.py:481
  92.9 11.4 %collective-permute-start.15 = (bf16[64,2048]{1,0:T(8,128)(2,1)S(1)}, bf16[64,2048]{1,0:T(8,128)(2,1)S(1)}, u32[]{:S(2)}, u32[]{:S(2)}) collective-permute-start(bf16[64,2048]{1,0:T(8,128)(2,1)S(1)} %get-tuple-element.84), channel_id=1, source_target_pairs={{0,2},{1,3},{2,0},{3,1},{4,6},{5,7},{6,4},{7,5},{8,10},{9,11},{10,... | collective-permute-start | bytes 786440 | tf_op jit(solution)/shard_map/ppermute | solution.py:481
  94.4 10.0 %collective-permute-start.16 = (bf16[64,2048]{1,0:T(8,128)(2,1)S(1)}, bf16[64,2048]{1,0:T(8,128)(2,1)S(1)}, u32[]{:S(2)}, u32[]{:S(2)}) collective-permute-start(bf16[64,2048]{1,0:T(8,128)(2,1)S(1)} %get-tuple-element.85), channel_id=1, source_target_pairs={{0,3},{1,2},{2,1},{3,0},{4,7},{5,6},{6,5},{7,4},{8,11},{9,10},{10,... | collective-permute-start | bytes 786440 | tf_op jit(solution)/shard_map/ppermute | solution.py:481
  95.0 6.3 %collective-permute-start.12 = (f32[80,256]{1,0:T(8,128)S(1)}, f32[80,256]{1,0:T(8,128)S(1)}, u32[]{:S(2)}, u32[]{:S(2)}) collective-permute-start(f32[80,256]{1,0:T(8,128)S(1)} %shard_map.187.refs_0_), channel_id=1, source_target_pairs={{0,8},{1,9},{2,10},{3,11},{4,12},{5,13},{6,14},{7,15},{8,0},{9,1},... | collective-permute-start | bytes 245768 | tf_op jit(solution)/shard_map/ppermute | solution.py:465
  108.6 5.0 %collective-permute-start.19 = (bf16[64,512]{1,0:T(8,128)(2,1)S(1)}, bf16[64,512]{1,0:T(8,128)(2,1)S(1)}, u32[]{:S(2)}, u32[]{:S(2)}) collective-permute-start(bf16[64,512]{1,0:T(8,128)(2,1)S(1)} %get-tuple-element.91), channel_id=1, source_target_pairs={{0,2},{1,3},{2,0},{3,1},{4,6},{5,7},{6,4},{7,5},{8,10},{9,11},{10,... | collective-permute-start | bytes 196616 | tf_op jit(solution)/shard_map/ppermute | solution.py:481
  109.5 5.2 %collective-permute-start.20 = (bf16[64,512]{1,0:T(8,128)(2,1)S(1)}, bf16[64,512]{1,0:T(8,128)(2,1)S(1)}, u32[]{:S(2)}, u32[]{:S(2)}) collective-permute-start(bf16[64,512]{1,0:T(8,128)(2,1)S(1)} %get-tuple-element.92), channel_id=1, source_target_pairs={{0,3},{1,2},{2,1},{3,0},{4,7},{5,6},{6,5},{7,4},{8,11},{9,10},{10,... | collective-permute-start | bytes 196616 | tf_op jit(solution)/shard_map/ppermute | solution.py:481
  115.5 7.6 %collective-permute-start.22 = (bf16[16,2560]{1,0:T(8,128)(2,1)S(1)}, bf16[16,2560]{1,0:T(8,128)(2,1)S(1)}, u32[]{:S(2)}, u32[]{:S(2)}) collective-permute-start(bf16[16,2560]{1,0:T(8,128)(2,1)S(1)} %get-tuple-element.95), channel_id=1, source_target_pairs={{0,8},{1,9},{2,10},{3,11},{4,12},{5,13},{6,14},{7,15},{8,0},{9,1},... | collective-permute-start | bytes 245768 | tf_op jit(solution)/shard_map/ppermute | solution.py:481
  117.8 6.3 %collective-permute-start.23 = (bf16[16,2560]{1,0:T(8,128)(2,1)S(1)}, bf16[16,2560]{1,0:T(8,128)(2,1)S(1)}, u32[]{:S(2)}, u32[]{:S(2)}) collective-permute-start(bf16[16,2560]{1,0:T(8,128)(2,1)S(1)} %get-tuple-element.96), channel_id=1, source_target_pairs={{0,12},{1,13},{2,14},{3,15},{4,8},{5,9},{6,10},{7,11},{8,4},{9,5},... | collective-permute-start | bytes 245768 | tf_op jit(solution)/shard_map/ppermute | solution.py:481
  124.1 7.2 %collective-permute-start.26 = (bf16[16,2560]{1,0:T(8,128)(2,1)S(1)}, bf16[16,2560]{1,0:T(8,128)(2,1)S(1)}, u32[]{:S(2)}, u32[]{:S(2)}) collective-permute-start(bf16[16,2560]{1,0:T(8,128)(2,1)S(1)} %shard_map.194.refs_1_), channel_id=1, source_target_pairs={{0,12},{1,13},{2,14},{3,15},{4,8},{5,9},{6,10},{7,11},{8,4},{9,5},... | collective-permute-start | bytes 245768 | tf_op jit(solution)/shard_map/ppermute | solution.py:481
  126.7 6.5 %collective-permute-start.25 = (bf16[16,2560]{1,0:T(8,128)(2,1)S(1)}, bf16[16,2560]{1,0:T(8,128)(2,1)S(1)}, u32[]{:S(2)}, u32[]{:S(2)}) collective-permute-start(bf16[16,2560]{1,0:T(8,128)(2,1)S(1)} %shard_map.194.refs_1_), channel_id=1, source_target_pairs={{0,8},{1,9},{2,10},{3,11},{4,12},{5,13},{6,14},{7,15},{8,0},{9,1},... | collective-permute-start | bytes 245768 | tf_op jit(solution)/shard_map/ppermute | solution.py:481
  127.0 6.3 %collective-permute-start.24 = (bf16[16,2560]{1,0:T(8,128)(2,1)S(1)}, bf16[16,2560]{1,0:T(8,128)(2,1)S(1)}, u32[]{:S(2)}, u32[]{:S(2)}) collective-permute-start(bf16[16,2560]{1,0:T(8,128)(2,1)S(1)} %shard_map.194.refs_1_), channel_id=1, source_target_pairs={{0,4},{1,5},{2,6},{3,7},{4,0},{5,1},{6,2},{7,3},{8,12},{9,13},{10,... | collective-permute-start | bytes 245768 | tf_op jit(solution)/shard_map/ppermute | solution.py:481
  133.4 11.5 %collective-permute-start.29 = (bf16[64,2560]{1,0:T(8,128)(2,1)S(1)}, bf16[64,2560]{1,0:T(8,128)(2,1)S(1)}, u32[]{:S(2)}, u32[]{:S(2)}) collective-permute-start(bf16[64,2560]{1,0:T(8,128)(2,1)S(1)} %shard_map.195.refs_1_), channel_id=1, source_target_pairs={{0,3},{1,2},{2,1},{3,0},{4,7},{5,6},{6,5},{7,4},{8,11},{9,10},{10,... | collective-permute-start | bytes 983048 | tf_op jit(solution)/shard_map/ppermute | solution.py:481
  134.9 13.4 %collective-permute-start.28 = (bf16[64,2560]{1,0:T(8,128)(2,1)S(1)}, bf16[64,2560]{1,0:T(8,128)(2,1)S(1)}, u32[]{:S(2)}, u32[]{:S(2)}) collective-permute-start(bf16[64,2560]{1,0:T(8,128)(2,1)S(1)} %shard_map.195.refs_1_), channel_id=1, source_target_pairs={{0,2},{1,3},{2,0},{3,1},{4,6},{5,7},{6,4},{7,5},{8,10},{9,11},{10,... | collective-permute-start | bytes 983048 | tf_op jit(solution)/shard_map/ppermute | solution.py:481
  136.1 12.2 %collective-permute-start.27 = (bf16[64,2560]{1,0:T(8,128)(2,1)S(1)}, bf16[64,2560]{1,0:T(8,128)(2,1)S(1)}, u32[]{:S(2)}, u32[]{:S(2)}) collective-permute-start(bf16[64,2560]{1,0:T(8,128)(2,1)S(1)} %shard_map.195.refs_1_), channel_id=1, source_target_pairs={{0,1},{1,0},{2,3},{3,2},{4,5},{5,4},{6,7},{7,6},{8,9},{9,8},{10,11... | collective-permute-start | bytes 983048 | tf_op jit(solution)/shard_map/ppermute | solution.py:481
  148.7 9.7 %collective-permute-start.30 = (bf16[256,2560]{1,0:T(8,128)(2,1)S(1)}, bf16[256,2560]{1,0:T(8,128)(2,1)}, u32[]{:S(2)}, u32[]{:S(2)}) collective-permute-start(bf16[256,2560]{1,0:T(8,128)(2,1)S(1)} %shard_map.196.mine_ref), channel_id=1, source_target_pairs={{0,16},{16,0},{1,17},{17,1},{2,18},{18,2},{3,19},{19,3},{4,20},{20... | collective-permute-start | bytes 3932168 | tf_op jit(solution)/shard_map/ppermute | solution.py:460
  (50 other events, 182.2 us)

commit v3 on v2

v3 whole, which is shorter than its diff:
```python
import functools
import math

import jax
import jax.numpy as jnp
from jax import lax
from jax.experimental import pallas as pl
from jax.experimental.pallas import tpu as pltpu
from jax.sharding import PartitionSpec as P

HEAD_DIM = 64
TILE = 128
LANES = 128

f32 = jnp.float32
bf16 = jnp.bfloat16
NN = (((1,), (0,)), ((), ()))
NT = (((1,), (1,)), ((), ()))
TN = (((0,), (0,)), ((), ()))

VMEM = pl.BlockSpec(memory_space=pltpu.VMEM)
HBM = pl.BlockSpec(memory_space=pltpu.HBM)


def shape(*dims, dtype=f32):
    return jax.ShapeDtypeStruct(dims, dtype)


def call(body, outs, arrays, after=(), megabytes=8, far=(), us=0.3, lazy=False, scratch=(), far_outs=()):
    n_in, n_after, n_far = len(arrays), len(after), len(far)
    n_outs, n_leave = len(outs), len(far_outs)

    def kernel(*refs):
        refs = list(refs)

        def take(n):
            taken = refs[:n]
            del refs[:n]
            return taken

        given, _, sources, results, leaving = take(n_in), take(n_after), take(n_far), take(n_outs), take(n_leave)
        targets, held, more = take(n_far), take(n_leave), take(len(scratch))
        moves = [pltpu.make_async_copy(sources[i], targets[i], refs[0].at[i]) for i in range(n_far)]
        leaves = [pltpu.make_async_copy(held[i], leaving[i], refs[0].at[n_far + i]) for i in range(n_leave)]
        for move in moves:
            move.start()
        options = {}
        if lazy:
            options["arrive"] = lambda i: moves[i].wait()
        else:
            for move in moves:
                move.wait()
        if far_outs:
            options["leave"] = lambda i: leaves[i].start()
        body(*given, *targets, *results, *held, *more, **options)
        for leave in leaves:
            leave.wait()

    scratches = [pltpu.VMEM(x.shape, x.dtype) for x in (*far, *far_outs, *scratch)]
    sems = n_far + n_leave
    return pl.pallas_call(
        kernel,
        out_shape=list(outs) + [pltpu.HBM(x.shape, x.dtype) for x in far_outs],
        in_specs=[VMEM] * (n_in + n_after) + [HBM] * n_far,
        out_specs=[VMEM] * n_outs + [HBM] * n_leave,
        scratch_shapes=scratches + ([pltpu.SemaphoreType.DMA((sems,))] if sems else []),
        compiler_params=pltpu.CompilerParams(vmem_limit_bytes=megabytes * 1024 * 1024),
        cost_estimate=pl.CostEstimate(
            flops=int(us * 1.1e9),
            bytes_accessed=sum(x.size * x.dtype.itemsize for x in arrays),
            transcendentals=0,
        ),
    )(*arrays, *after, *[pltpu.with_memory_space_constraint(x, pltpu.HBM) for x in far])


def on_core_zero(place_ref):
    return place_ref[0:1, 0:1] == 0


def bit_is_zero(place_ref, bit):
    return place_ref[1 + bit : 2 + bit, 0:1] == 0


def mm(a, b, dims=NN):
    return lax.dot_general(a, b, dims, preferred_element_type=f32)


def split(x):
    high = x.astype(bf16)
    return high, (x - high.astype(f32)).astype(bf16)


def mm_exact_right(a, b, dims=NN):
    high, low = split(a)
    return mm(high, b, dims) + mm(low, b, dims)


def mm_exact_left(a, b, dims=NN):
    high, low = split(b)
    return mm(a, high, dims) + mm(a, low, dims)


def mm_wide(a, b, dims=NN):
    ah, al = split(a)
    bh, bl = split(b)
    return mm(ah, bh, dims) + (mm(ah, bl, dims) + mm(al, bh, dims))


def iota(dims, axis):
    return lax.broadcasted_iota(jnp.int32, dims, axis)


def one_hot_rows(index_row, count):
    return jnp.where(iota((count, index_row.shape[1]), 0) == index_row, 1.0, 0.0).astype(bf16)


def head_mask():
    return (iota((LANES, LANES), 0) < HEAD_DIM) == (iota((LANES, LANES), 1) < HEAD_DIM)


def block_diagonal(packed):
    return jnp.where(head_mask(), jnp.concatenate([packed, packed], axis=0), 0.0)


def pack_diagonal(full):
    left = iota((HEAD_DIM, LANES), 1) < HEAD_DIM
    return jnp.where(left, full[:HEAD_DIM], full[HEAD_DIM:])


def store_summary(place_ref, packed, rows, mine_ref, theirs_ref, extra=None):
    zero = on_core_zero(place_ref)
    half = len(packed) // 2
    first = iota((8, LANES), 0) == 0
    if extra is not None:
        at = slice(HEAD_DIM + 8, HEAD_DIM + 16)
        mine_ref[at, :] = jnp.zeros((8, mine_ref.shape[1]), f32)
        theirs_ref[at, :] = jnp.zeros((8, mine_ref.shape[1]), f32)
        mine_ref[at, :LANES] = jnp.where(zero, extra, 0.0)
        theirs_ref[at, :LANES] = jnp.where(zero, 0.0, extra)
    for p in range(half):
        at = slice(p * LANES, (p + 1) * LANES)
        low = jnp.concatenate([packed[p], jnp.where(first, rows[p], 0.0)], axis=0)
        high = jnp.concatenate([packed[p + half], jnp.where(first, rows[p + half], 0.0)], axis=0)
        mine_ref[: HEAD_DIM + 8, at] = jnp.where(zero, low, high)
        theirs_ref[: HEAD_DIM + 8, at] = jnp.where(zero, high, low)


def load_summary(place_ref, pair, pairs, mine_ref, theirs_ref):
    half = pairs // 2
    at = slice(pair % half * LANES, (pair % half + 1) * LANES)
    low, high = (mine_ref, theirs_ref) if pair < half else (theirs_ref, mine_ref)
    both = jnp.where(on_core_zero(place_ref), low[:, at], high[:, at])
    return both[:HEAD_DIM], both[HEAD_DIM : HEAD_DIM + 1]


def store_halves(place_ref, whole, mine_ref, theirs_ref, at):
    zero = on_core_zero(place_ref)
    rows = whole.shape[0] // 2
    low, high = whole[:rows], whole[rows:]
    mine_ref[:, at] = jnp.where(zero, low, high)
    theirs_ref[:, at] = jnp.where(zero, high, low).astype(bf16)


def send_row(send_ref):
    return jnp.concatenate([send_ref[p : p + 1, :] for p in range(send_ref.shape[0])], axis=1)


def start_kernel(
    place_ref,
    features_ref,
    wq_ref,
    wk_ref,
    wv_ref,
    send_ref,
    bases_ref,
    cot_ref,
    mine_ref,
    theirs_ref,
    out_ref,
    high_ref,
    low_ref,
    eq_ref,
    ek_ref,
    v_ref,
    *,
    arrive,
    leave,
):
    pairs = features_ref.shape[1] // LANES
    arrive(0)
    features = features_ref[...]
    arrive(1)
    eq_ref[...] = jnp.exp(mm(features, wq_ref[...]))
    leave(0)
    arrive(2)
    ek_ref[...] = jnp.exp(mm(features, wk_ref[...]))
    leave(1)
    arrive(3)
    v_ref[...] = mm(features, wv_ref[...])
    leave(2)
    packed, sums = [], []
    for p in range(pairs):
        at = slice(p * LANES, (p + 1) * LANES)
        key = ek_ref[:, at]
        packed.append(pack_diagonal(mm_wide(key, v_ref[:, at], TN)))
        sums.append(jnp.sum(key, axis=0, keepdims=True))
    store_summary(place_ref, packed, sums, mine_ref, theirs_ref)
    arrive(4)
    pick = one_hot_rows(send_row(send_ref), features.shape[0])
    out_ref[...] = mm(pick, features, TN).astype(bf16)
    arrive(5)
    arrive(6)
    cot = cot_ref[...].astype(bf16)
    for b in range(bases_ref.shape[0]):
        high, low = split(mm(cot, bases_ref[b], NT))
        for t in range(high_ref.shape[0]):
            high_ref[t, b * TILE : (b + 1) * TILE, :] = high[t * TILE : (t + 1) * TILE]
            low_ref[t, b * TILE : (b + 1) * TILE, :] = low[t * TILE : (t + 1) * TILE]


def attend_kernel(
    place_ref,
    eq_ref,
    cot_ref,
    sum_mine_ref,
    sum_theirs_ref,
    coef_ref,
    conv_ref,
    mine_ref,
    theirs_ref,
    qblock_ref,
    layer_ref,
    *,
    leave,
):
    pairs = eq_ref.shape[1] // LANES
    same_head = jnp.where(head_mask(), 1.0, 0.0).astype(bf16)
    packed, sums = [], []
    for p in range(pairs):
        at = slice(p * LANES, (p + 1) * LANES)
        kv, ks = load_summary(place_ref, p, pairs, sum_mine_ref, sum_theirs_ref)
        kv = block_diagonal(kv)
        query = eq_ref[:, at]
        cot = cot_ref[:, at]
        inverse = 1.0 / mm_exact_right(query * ks, same_head)
        attended = mm_wide(query, kv) * inverse
        layer_ref[:, at] = attended + conv_ref[:, at]
        num_grad = cot * inverse
        den_grad = -mm_exact_right(cot * attended, same_head) * inverse
        packed.append(pack_diagonal(mm_wide(query, num_grad, TN)))
        sums.append(jnp.sum(query * den_grad, axis=0, keepdims=True))
        query_side = mm_wide(num_grad, kv, NT) + den_grad * ks
        qblock_ref[:, at] = (query_side * query).astype(bf16)
    leave(0)
    store_summary(place_ref, packed, sums, mine_ref, theirs_ref, coef_ref[...])


def query_kernel(place_ref, qblock_ref, ek_ref, bases_theirs_ref, features_ref, mine_ref, theirs_ref):
    width = features_ref.shape[1]
    bases_width = bases_theirs_ref.shape[1]
    theirs_ref[:, :bases_width] = bases_theirs_ref[...]
    theirs_ref = theirs_ref.at[:, bases_width:]
    features = features_ref[...]
    store_halves(place_ref, mm(features, qblock_ref[...], TN), mine_ref, theirs_ref, slice(0, width))
    whole = mm_exact_left(features, ek_ref[...], TN)
    store_halves(place_ref, whole, mine_ref, theirs_ref, slice(width, 2 * width))


def key_kernel(
    place_ref, ek_ref, v_ref, sum_mine_ref, sum_theirs_ref, features_ref, kblock_ref, mine_ref, theirs_ref
):
    pairs = ek_ref.shape[1] // LANES
    for p in range(pairs):
        at = slice(p * LANES, (p + 1) * LANES)
        dkv, dks = load_summary(place_ref, p, pairs, sum_mine_ref, sum_theirs_ref)
        key_side = mm_wide(v_ref[:, at], block_diagonal(dkv), NT) + dks
        kblock_ref[:, at] = (key_side * ek_ref[:, at]).astype(bf16)
    store_halves(place_ref, mm(features_ref[...], kblock_ref[...], TN), mine_ref, theirs_ref, slice(None))


def returned_kernel(send_ref, table_ref, returned_ref, out_ref):
    rows = out_ref.shape[0]
    out_ref[...] = table_ref[:rows, :] + mm(one_hot_rows(send_row(send_ref), rows), returned_ref[...])


def input_grad_kernel(
    place_ref,
    qblock_ref,
    kblock_ref,
    ek_ref,
    sum_mine_ref,
    sum_theirs_ref,
    graph_ref,
    wq_ref,
    wk_ref,
    wv_ref,
    out_ref,
    token_ref,
):
    token_ref[...] = jnp.zeros((8, LANES), f32)
    pairs = ek_ref.shape[1] // LANES
    blocks = []
    for p in range(pairs):
        at = slice(p * LANES, (p + 1) * LANES)
        dkv, _ = load_summary(place_ref, p, pairs, sum_mine_ref, sum_theirs_ref)
        blocks.append(mm_wide(ek_ref[:, at], block_diagonal(dkv)).astype(bf16))
    total = mm(qblock_ref[...], wq_ref[...], NT) + mm(kblock_ref[...], wk_ref[...], NT)
    out_ref[...] = total + mm(jnp.concatenate(blocks, axis=1), wv_ref[...], NT) + graph_ref[...]


def tile_hits(count_ref, dst_ref, r, tile):
    slots = dst_ref.shape[2]
    live = iota((TILE, slots), 1) < count_ref[r : r + 1, tile : tile + 1]
    target = iota((TILE, slots), 0) == dst_ref[r, tile : tile + 1, :]
    hit = jnp.where(target & live, 1.0, 0.0)
    return hit / jnp.maximum(jnp.sum(hit, axis=1, keepdims=True), 1.0)


def tile_incidence(count_ref, coef_ref, dst_ref, tile):
    basis_count = coef_ref.shape[1]
    hits, scaled = [], [[] for _ in range(basis_count)]
    for r in range(dst_ref.shape[0]):
        hit = tile_hits(count_ref, dst_ref, r, tile)
        hits.append(hit)
        for b in range(basis_count):
            scaled[b].append(hit * coef_ref[r : r + 1, b : b + 1])
    high, low = split(jnp.concatenate([jnp.concatenate(part, axis=1) for part in scaled], axis=0))
    return jnp.concatenate(hits, axis=1), jnp.concatenate([high, low], axis=0)


def tile_pick(src_ref, tile, table_rows):
    picks = [one_hot_rows(src_ref[r, tile : tile + 1, :], table_rows) for r in range(src_ref.shape[0])]
    return jnp.concatenate(picks, axis=1)


def backward_kernel(count_ref, coef_ref, src_ref, dst_ref, grad_ref, *refs, tile, last, leave):
    mixed_ref = refs[-1]
    table_ref = refs[0 if tile == 0 else 1]
    _, scaled = tile_incidence(count_ref, coef_ref, dst_ref, tile)
    both = mm(scaled, tile_pick(src_ref, tile, table_ref.shape[0]), NT)
    wide = both.shape[0] // 2
    high, low = split(both[:wide] + both[wide:])
    mixed_ref[:wide, :] = high
    mixed_ref[wide:, :] = low
    leave(0)
    table = mm(high, grad_ref[tile], TN)
    table = table if tile == 0 else table + refs[0][...]
    table_ref[...] = table
    if last:
        sent_ref = refs[-2]
        sent_ref[...] = table[table.shape[0] - sent_ref.shape[0] :, :].astype(bf16)


def forward_kernel(count_ref, coef_ref, place_ref, src_ref, dst_ref, *refs, arrive):
    relations, tiles, slots = src_ref.shape
    own_ref, halo_ref, high_ref, low_ref, bases_ref = refs[:5]
    mixed_refs, (cot_ref, conv_ref, coef_grad_ref, mine_ref, theirs_ref, basis_ref) = refs[5 : 5 + tiles], refs[5 + tiles :]
    basis_count = bases_ref.shape[0]
    wide = basis_count * TILE
    rows, width = own_ref.shape
    sums = [jnp.zeros((1, relations * slots), f32) for _ in range(basis_count)]
    for t in range(tiles):
        hit, _ = tile_incidence(count_ref, coef_ref, dst_ref, t)
        pick = tile_pick(src_ref, t, rows + halo_ref.shape[0])
        if t == 0:
            for i in range(4):
                arrive(i)
        grads = jnp.concatenate([high_ref[t], low_ref[t]], axis=0)
        dots = [mm(grads, table_ref[...], NT) for table_ref in (own_ref, halo_ref)]
        dots = [(x[:wide] + x[wide:]).astype(bf16) for x in dots]
        edge = mm(dots[0], pick[:rows]) + mm(dots[1], pick[rows:])
        for b in range(basis_count):
            sums[b] += jnp.sum(edge[b * TILE : (b + 1) * TILE] * hit, axis=0, keepdims=True)
        if t == 0:
            arrive(4)
        arrive(5 + t)
        mixed_ref = mixed_refs[t]
        both = mm(mixed_ref[:, :rows], own_ref[...]) + mm(mixed_ref[:, rows:], halo_ref[...])
        both = (both[:wide] + both[wide:]).astype(bf16)
        at = slice(t * TILE, (t + 1) * TILE)
        conv = None
        for b in range(basis_count):
            basis_in = both[b * TILE : (b + 1) * TILE]
            basis_ref[b, at, :] = basis_in
            part = mm(basis_in, bases_ref[b])
            conv = part if conv is None else conv + part
        conv_ref[at, :] = conv
    row, lane = iota((8, LANES), 0), iota((8, LANES), 1)
    total = jnp.zeros((8, LANES), f32)
    for b in range(basis_count):
        for r in range(relations):
            part = jnp.sum(sums[b][:, r * slots : (r + 1) * slots], axis=1, keepdims=True)
            total = jnp.where((row == r) & (lane == b), part, total)
    coef_grad_ref[...] = total
    arrive(5 + tiles)
    cot = cot_ref[...].astype(bf16)
    for b in range(basis_count):
        whole = mm(basis_ref[b], cot, TN)
        store_halves(place_ref, whole, mine_ref, theirs_ref, slice(b * width, (b + 1) * width))


def add_kernel(a_ref, b_ref, out_ref):
    out_ref[...] = a_ref[...] + b_ref[...]


def choose(place_ref, first_bit, blocks, index):
    bit = first_bit
    while len(blocks) > 1:
        zero = bit_is_zero(place_ref, bit)
        pairs = [(blocks[i], blocks[i + 1]) for i in range(0, len(blocks), 2)]
        if index % 2:
            blocks = [jnp.where(zero, high, low) for low, high in pairs]
        else:
            blocks = [jnp.where(zero, low, high) for low, high in pairs]
        index //= 2
        bit += 1
    return blocks[0]


def scatter_kernel(place_ref, *refs, first_bit, beside, others):
    pieces, others = refs[:beside], refs[beside : beside + others]
    keep_ref, *send_refs = refs[beside + len(others) :]
    rows = keep_ref.shape[0]
    count = len(send_refs) + 1
    at = 0
    for piece in pieces:
        lanes = slice(at, at + piece.shape[1])
        blocks = []
        for i in range(count):
            rows_at = slice(i * rows, (i + 1) * rows)
            block = piece[rows_at, :].astype(f32)
            for other in others:
                block += other[rows_at, lanes].astype(f32)
            blocks.append(block)
        keep_ref[:, lanes] = choose(place_ref, first_bit, blocks, 0)
        for k in range(1, count):
            send_refs[k - 1][:, lanes] = choose(place_ref, first_bit, blocks, k).astype(send_refs[k - 1].dtype)
        at += piece.shape[1]


def total_kernel(*refs):
    out_ref = refs[-1]
    total = refs[0][...].astype(f32)
    for ref in refs[1:-1]:
        total += ref[...].astype(f32)
    out_ref[...] = total.astype(out_ref.dtype)


def join_kernel(place_ref, *refs, first_bit):
    out_ref = refs[-1]
    blocks = [ref[...] for ref in refs[:-1]]
    rows = blocks[0].shape[0]
    for i in range(len(blocks)):
        out_ref[i * rows : (i + 1) * rows, :] = choose(place_ref, first_bit, blocks, i)


def finish_kernel(
    place_ref, sum_mine_ref, sum_theirs_ref, mine_ref, theirs_ref, *refs, scale, value_at, outs
):
    holds, sems = refs[outs:-1], refs[-1]
    targets = []
    for out_ref in refs[:outs]:
        targets += [out_ref] if len(out_ref.shape) == 2 else [out_ref.at[b] for b in range(out_ref.shape[0])]
    zero = on_core_zero(place_ref)
    rows = mine_ref.shape[0]
    width = holds[0].shape[1]
    moves = []
    for i, hold in enumerate(holds):
        for p in range(width // LANES):
            at = slice(p * LANES, (p + 1) * LANES)
            source = slice(i * width + p * LANES, i * width + (p + 1) * LANES)
            if i == value_at:
                dkv, _ = load_summary(place_ref, p, width // LANES, sum_mine_ref, sum_theirs_ref)
                dkv = block_diagonal(dkv)
                a = mm_exact_left(mine_ref[:, source], dkv) * scale
                b = mm_exact_left(theirs_ref[:, source], dkv) * scale
            else:
                a = mine_ref[:, source].astype(f32) * scale
                b = theirs_ref[:, source].astype(f32) * scale
            hold[:rows, at] = jnp.where(zero, a, b)
            hold[rows:, at] = jnp.where(zero, b, a)
        moves.append(pltpu.make_async_copy(hold, targets[i], sems.at[i]))
        moves[-1].start()
    for move in moves:
        move.wait()


def swap_cores(x):
    return lax.ppermute(x, "outer", [(0, 1), (1, 0)])


def swap_nodes(x, bit):
    nodes = lax.axis_size("nodes")
    return lax.ppermute(x, "nodes", [(i, i ^ (1 << bit)) for i in range(nodes)])


def run_all(plan, step, x):
    return [y for y in [run(x) for run in plan.get(step, [])] if y is not None]


def sum_summary(mine, theirs, bits, beside):
    out = [shape(*mine.shape)]
    received = swap_cores(theirs)
    (mine,) = call(add_kernel, out, [mine, received], beside("core", mine))
    for bit in bits:
        received = swap_nodes(mine, bit)
        (mine,) = call(add_kernel, out, [mine, received], beside(bit, mine))
    return mine, swap_cores(mine), beside("back", mine)


def exchange(sends, first_bit):
    nodes = lax.axis_size("nodes")
    return [
        lax.ppermute(x, "nodes", [(i, i ^ (k << first_bit)) for i in range(nodes)])
        for k, x in enumerate(sends, start=1)
    ]


def per_device(
    features, w_query, w_key, w_value, bases, rel_coef, send_rows, tile_src, tile_dst, tile_count, cotangent
):
    rows, width = features.shape
    nodes = lax.axis_size("nodes")
    scale = 1.0 / math.sqrt(rows * nodes * lax.axis_size("outer"))
    basis_count = bases.shape[0]
    slots = send_rows.shape[2]
    halo_rows = nodes * slots
    table_rows = rows + halo_rows
    core, node = lax.axis_index("outer"), lax.axis_index("nodes")
    place = jnp.stack([core] + [(node >> bit) & 1 for bit in range(7)]).astype(jnp.int32)
    place = jnp.broadcast_to(place[:, None], (8, LANES))
    send, src, dst, count = send_rows[0], tile_src[0], tile_dst[0], tile_count[0]
    relations, tiles, cap = src.shape
    bits = list(range(nodes.bit_length() - 1))
    y, z1, z2 = bits[-3:]

    square, square_half = shape(rows, width), shape(rows, width, dtype=bf16)
    summary = shape(HEAD_DIM + 8, width // 2)
    wide_summary = shape(HEAD_DIM + 16, width // 2)

    def halves(n):
        return shape(width // 2, n * width), shape(width // 2, n * width, dtype=bf16)

    grads = shape(tiles, basis_count * TILE, width, dtype=bf16)
    kv_mine, kv_theirs, outgoing, grad_high, grad_low, exp_query, exp_key, values = call(
        start_kernel,
        [summary, summary, shape(halo_rows, width, dtype=bf16), grads, grads],
        [place],
        (),
        16,
        far=[features, w_query, w_key, w_value, send, bases, cotangent],
        us=5.5,
        lazy=True,
        far_outs=[square, square, square],
    )
    halo = lax.all_to_all(
        outgoing.reshape(nodes, slots, width), "nodes", split_axis=0, concat_axis=0, tiled=True
    ).reshape(halo_rows, width)

    kept = {}

    def run_backward(t, x):
        last = t == tiles - 1
        sent = [shape(halo_rows, width, dtype=bf16)] if last else []
        kept["table"], *sent, kept["mixed", t] = call(
            functools.partial(backward_kernel, tile=t, last=last),
            [shape(table_rows, width), *sent],
            [count, rel_coef, src, dst, grad_high] + ([kept["table"]] if t > 0 else []),
            [x],
            table_rows // 64,
            us=2.1,
            far_outs=[shape(2 * basis_count * TILE, table_rows, dtype=bf16)],
        )
        if last:
            kept["returned"] = lax.all_to_all(
                sent[0].reshape(nodes, slots, width), "nodes", split_axis=0, concat_axis=0, tiled=True
            ).reshape(halo_rows, width)
        return kept["table"]

    def run_forward(x):
        kept["conv"], kept["coef"], *kept["bases"] = call(
            forward_kernel,
            [square, shape(8, LANES), *halves(basis_count)],
            [count, rel_coef, place, src, dst],
            [x],
            8 + table_rows // 64,
            far=[features, halo, grad_high, grad_low, bases, *[kept["mixed", t] for t in range(tiles)], cotangent],
            us=9,
            lazy=True,
            scratch=[shape(basis_count, rows, width, dtype=bf16)],
        )
        return None

    backward = [functools.partial(run_backward, t) for t in range(tiles)]
    first = {bits[0]: backward[:1], y: backward[1:2], z1: backward[2:3], z2: backward[3:], "back": [run_forward]}
    kv_mine, kv_theirs, after = sum_summary(
        kv_mine, kv_theirs, bits, functools.partial(run_all, first)
    )
    dkv_mine, dkv_theirs, qblock, layer_out = call(
        attend_kernel,
        [wide_summary, wide_summary, square_half],
        [place, exp_query, cotangent, kv_mine, kv_theirs, kept["coef"], kept["conv"]],
        after,
        us=2.7,
        far_outs=[square],
    )

    plane, planes = nodes // 4, 4
    plane_rows = width // 2 // plane
    place_rows = plane_rows // planes
    early_count = basis_count + 2
    early_width = early_count * width

    def scatter(operands, first_bit, count, n_rows, beside=1, after=()):
        columns = sum(x.shape[1] for x in operands[:beside])
        own, *out = call(
            functools.partial(
                scatter_kernel, first_bit=first_bit, beside=beside, others=len(operands) - beside
            ),
            [shape(n_rows, columns)] + [shape(n_rows, columns, dtype=bf16 if n_rows >= 16 else f32)] * (count - 1),
            [place, *operands],
            after,
            12,
        )
        return [own, *exchange(out, first_bit)]

    def gather(own, first_bit, count, after=()):
        outs = [shape(own.shape[0] * count, own.shape[1], dtype=own.dtype)]
        blocks = [own, *exchange([own] * (count - 1), first_bit)]
        return call(functools.partial(join_kernel, first_bit=first_bit), outs, [place, *blocks], after)[0]

    def total(blocks, after=()):
        out = shape(*blocks[0].shape, dtype=bf16 if blocks[0].shape[0] >= 16 else f32)
        return call(total_kernel, [out], blocks, after)[0]

    def finish(own, bodies, value_at):
        count = sum(max(n, 1) for n in bodies)
        return pl.pallas_call(
            functools.partial(finish_kernel, scale=scale, value_at=value_at, outs=len(bodies)),
            out_shape=[shape(n, width, width) if n else shape(width, width) for n in bodies],
            in_specs=[VMEM] * 5,
            out_specs=[HBM] * len(bodies),
            scratch_shapes=[pltpu.VMEM((width, width), f32)] * count + [pltpu.SemaphoreType.DMA((count,))],
            compiler_params=pltpu.CompilerParams(vmem_limit_bytes=12 * 1024 * 1024),
            cost_estimate=pl.CostEstimate(flops=int(count * 0.8e9), bytes_accessed=0, transcendentals=0),
        )(place, dkv_mine, dkv_theirs, own, swap_cores(own))

    def run_returned(x):
        (kept["graph"],) = call(
            returned_kernel, [square], [send, kept["table"], kept["returned"]], [x], us=0.5
        )
        return kept["graph"]

    def run_query(x):
        kept["early"] = call(
            query_kernel,
            [halves(2)[0], halves(early_count)[1]],
            [place, qblock, exp_key, kept["bases"][1]],
            [x],
            12,
            far=[features],
            us=1.8,
        )
        return kept["early"][1]

    def run_early_plane(x):
        operands = [kept["bases"][0], kept["early"][0], swap_cores(kept["early"][1])]
        kept["blocks"] = scatter(operands, 0, plane, plane_rows, 2, [x])
        return kept["blocks"][0]

    def run_early_sum(x):
        (kept["early sum"],) = call(total_kernel, [shape(plane_rows, early_width)], kept["blocks"], [x])
        return kept["early sum"]

    second = {"core": [run_returned], bits[0]: [run_query], z1: [run_early_plane], "back": [run_early_sum]}
    dkv_mine, dkv_theirs, after = sum_summary(dkv_mine, dkv_theirs, bits, functools.partial(run_all, second))
    kblock, key_mine, key_theirs = call(
        key_kernel,
        [square_half, *halves(1)],
        [place, exp_key, values, dkv_mine, dkv_theirs],
        after,
        far=[features],
        us=1.8,
    )
    key = scatter([key_mine, swap_cores(key_theirs)], 0, plane, plane_rows)
    (key,) = call(total_kernel, [shape(plane_rows, width)], key)
    own = scatter([kept["early sum"], key], z1, planes, place_rows, 2)
    own = total(own)
    cut = (basis_count + 1) * width
    own, last = own[:, :cut], own[:, cut:]
    own = gather(own, z1, planes).astype(bf16)
    grad_x, token = call(
        input_grad_kernel,
        [square, shape(8, LANES)],
        [place, qblock, kblock, exp_key, dkv_mine, dkv_theirs, kept["graph"]],
        [own],
        16,
        far=[w_query, w_key, w_value],
        us=3.5,
    )
    last = gather(last, z1, planes, [token]).astype(bf16)
    own = gather(own, 0, plane)
    last = gather(last, 0, plane)
    bases_grad, query_grad = finish(own, [basis_count, 0], -1)
    value_grad, key_grad = finish(last, [0, 0], 0)
    coef_sum = jnp.where(core == 0, dkv_mine, dkv_theirs)[HEAD_DIM + 8 :, :]
    coef_grad = coef_sum[:relations, :basis_count] * scale
    return layer_out, grad_x, query_grad, key_grad, value_grad, bases_grad, coef_grad


def solution(mesh):
    both = ("outer", "nodes")
    in_specs = (
        P(both, None),
        P(),
        P(),
        P(),
        P(),
        P(),
        P(both, None, None),
        P(both, None, None, None),
        P(both, None, None, None),
        P(both, None, None),
        P(both, None),
    )
    out_specs = (P(both, None), P(both, None), P(), P(), P(), P(), P())
    return jax.shard_map(per_device, mesh=mesh, in_specs=in_specs, out_specs=out_specs, check_vma=False)
```

time: 164 us -> 139 us (0.85)
  local copies, waits for them, and re-layouts: 23.7 us -> 1.29 us
  starting transfers between devices: 50.5 us -> 59.7 us
  waiting for transfers between devices: 37.6 us -> 29.6 us
  Pallas kernels: 49.6 us -> 46.4 us
    unnamed x84 -> x36, local copies, waits for them, and re-layouts: 23.5 us -> 1.04 us
    ppermute x15 -> x21, waiting for transfers between devices: 27.5 us -> 15.3 us  [exchange(): lax.ppermute(x, 'nodes', [(i, i ^ k << first_bit) for i in range(nodes)])]
    ppermute x15 -> x21, starting transfers between devices: 19.5 us -> 27.5 us  [exchange(): lax.ppermute(x, 'nodes', [(i, i ^ k << first_bit) for i in range(nodes)])]
    ppermute x8, waiting for transfers between devices: 6.89 us -> 10.9 us  [swap_nodes(): return lax.ppermute(x, 'nodes', [(i, i ^ 1 << bit) for i in range(nodes)])]
    pallas_call x36 -> x33, Pallas kernels: 49.6 us -> 46.4 us  [the longest x31 42.6 us: call(): pl.pallas_call(kernel, out_shape=list(outs) + [pltpu.HBM(x.shape, x.dtype...]
  transfers between devices with their start and end apart: 33 -> 39, of which waited for: 19 -> 19; matrix products, arithmetic and copies ran while one was open for 1% -> 1% of each run, Pallas kernels for 26% -> 25%
where the time goes in v3:
time: 139 us; the launch traced here: 138 us
  starting transfers between devices  59.7 us (43%)
  Pallas kernels  46.4 us (33%)
  waiting for transfers between devices  29.6 us (21%)
    pallas_call x31, Pallas kernels, call(): pl.pallas_call(kernel, out_shape=list(outs) + [pltpu.HBM(x.shape, x.dtype...  42.6 us
    ppermute x21, starting transfers between devices, exchange(): lax.ppermute(x, 'nodes', [(i, i ^ k << first_bit) for i in range(nodes)])  27.5 us
    ppermute x8, starting transfers between devices, swap_nodes(): return lax.ppermute(x, 'nodes', [(i, i ^ 1 << bit) for i in range(nodes)])  16.3 us
    ppermute x21, waiting for transfers between devices, exchange(): lax.ppermute(x, 'nodes', [(i, i ^ k << first_bit) for i in range(nodes)])  15.3 us
    ppermute x8, waiting for transfers between devices, swap_nodes(): return lax.ppermute(x, 'nodes', [(i, i ^ 1 << bit) for i in range(nodes)])  10.9 us
    all_to_all x1, starting transfers between devices, per_device(): lax.all_to_all(outgoing.reshape(nodes, slots, width), 'nodes', split_axis...  8.01 us
    all_to_all x1, starting transfers between devices, run_backward(): lax.all_to_all(sent[0].reshape(nodes, slots, width), 'nodes', split_axis=...  6.08 us
    pallas_call x2, Pallas kernels, finish(): pl.pallas_call(functools.partial(finish_kernel, scale=scale, value_at=val...  3.85 us
  transfers between devices with their start and end apart: 39, of which 19 were waited for; matrix products, arithmetic and copies ran while one was open for 1% of the time, Pallas kernels for 25%

profile of v3, /device:TPU:0, one launch (start us, length us, event | category | flops | bytes accessed | tf_op | source)
XLA Modules:
  0.0 138.3 jit_solution(3190032799774124053)
XLA Ops:
  0.8 5.4 %shard_map.162 = (f32[72,256]{1,0:T(8,128)S(1)}, f32[72,256]{1,0:T(8,128)S(1)}, bf16[512,512]{1,0:T(8,128)(2,1)}, bf16[4,256,512]{2,1,0:T(8,128)(2,1)S(1)}, bf16...) custom-call(s32[8,128]{1,0:T(8,128)S(1)} %broadcast_in_dim.2.refs_0_.refs_2_.place_r, ...), custom_call_target="tpu_custom_call" | custom-call | flops 6049999872 | bytes 4096 | tf_op jit(solution)/shard_map/pallas_call | solution.py:61
  6.8 8.0 %all-to-all-start = ((bf16[16,32,512]{2,1,0:T(8,128)(2,1)}), bf16[16,32,512]{2,1,0:T(8,128)(2,1)S(1)}, u32[]{:S(2)}, u32[]{:S(2)}) async-start(bf16[16,32,512]{2,1,0:T(8,128)(2,1)} %bitcast.12), calls=%async_computation | async-start | bytes 1048576 | tf_op jit(solution)/shard_map/all_to_all | solution.py:556
  15.0 2.0 %collective-permute-start.1 = (f32[72,256]{1,0:T(8,128)S(1)}, f32[72,256]{1,0:T(8,128)S(1)}, u32[]{:S(2)}, u32[]{:S(2)}) collective-permute-start(f32[72,256]{1,0:T(8,128)S(1)} %shard_map.163.refs_5_.refs_0_), channel_id=1, source_target_pairs={{0,1},{1,0},{2,3},{3,2},{4,5},{5,4},{6,7},{7,6},{8,9},{9,8},{10,11... | collective-permute-start | bytes 221192 | tf_op jit(solution)/shard_map/ppermute | solution.py:494
  17.0 2.5 %shard_map.164 = (f32[1024,512]{1,0:T(8,128)S(1)}, bf16[512,1024]{1,0:T(8,128)(2,1)}) custom-call(s32[8,4]{1,0:T(8,128)S(1)} %copy.18.refs_0_, f32[8,2]{1,0:T(8,128)S(1)} %copy.19.refs_1_, s32[8,4,128]{2,1,0:T(4,128)S(1)} %bitcast.19, s32[8,4,128]{2,1,0:T(4,128)S(1)} %bitcast.24, bf16[4,256,512]{2,1,0:T(8,128)(2,1)S(1)} %get-tuple-element.58.refs_4_.refs_8_, ...), custom_call_target="tpu_custom_call" | custom-call | flops 2310000128 | bytes 1081536 | tf_op jit(solution)/shard_map/pallas_call | solution.py:61
  22.6 2.6 %shard_map.166 = (f32[1024,512]{1,0:T(8,128)S(1)}, bf16[512,1024]{1,0:T(8,128)(2,1)}) custom-call(s32[8,4]{1,0:T(8,128)S(1)} %copy.18.refs_0_, f32[8,2]{1,0:T(8,128)S(1)} %copy.19.refs_1_, s32[8,4,128]{2,1,0:T(4,128)S(1)} %bitcast.20, s32[8,4,128]{2,1,0:T(4,128)S(1)} %bitcast.25, bf16[4,256,512]{2,1,0:T(8,128)(2,1)S(1)} %get-tuple-element.58.refs_4_.refs_8_, ...), custom_call_target="tpu_custom_call" | custom-call | flops 2310000128 | bytes 3178688 | tf_op jit(solution)/shard_map/pallas_call | solution.py:61
  25.6 2.6 %collective-permute-start.3 = (f32[72,256]{1,0:T(8,128)S(1)}, f32[72,256]{1,0:T(8,128)S(1)}, u32[]{:S(2)}, u32[]{:S(2)}) collective-permute-start(f32[72,256]{1,0:T(8,128)S(1)} %shard_map.167.refs_6_.refs_0_), channel_id=1, source_target_pairs={{0,4},{1,5},{2,6},{3,7},{4,0},{5,1},{6,2},{7,3},{8,12},{9,13},{10,... | collective-permute-start | bytes 221192 | tf_op jit(solution)/shard_map/ppermute | solution.py:494
  28.2 2.6 %shard_map.168 = (f32[1024,512]{1,0:T(8,128)S(1)}, bf16[512,1024]{1,0:T(8,128)(2,1)}) custom-call(s32[8,4]{1,0:T(8,128)S(1)} %copy.18.refs_0_, f32[8,2]{1,0:T(8,128)S(1)} %copy.19.refs_1_, s32[8,4,128]{2,1,0:T(4,128)S(1)} %bitcast.21, s32[8,4,128]{2,1,0:T(4,128)S(1)} %bitcast.26, bf16[4,256,512]{2,1,0:T(8,128)(2,1)S(1)} %get-tuple-element.58.refs_4_.refs_8_, ...), custom_call_target="tpu_custom_call" | custom-call | flops 2310000128 | bytes 3178688 | tf_op jit(solution)/shard_map/pallas_call | solution.py:61
  30.9 2.4 %collective-permute-start.4 = (f32[72,256]{1,0:T(8,128)S(1)}, f32[72,256]{1,0:T(8,128)S(1)}, u32[]{:S(2)}, u32[]{:S(2)}) collective-permute-start(f32[72,256]{1,0:T(8,128)S(1)} %shard_map.169.refs_6_.refs_0_), channel_id=1, source_target_pairs={{0,8},{1,9},{2,10},{3,11},{4,12},{5,13},{6,14},{7,15},{8,0},{9,1},... | collective-permute-start | bytes 221192 | tf_op jit(solution)/shard_map/ppermute | solution.py:494
  33.3 3.4 %shard_map.170 = (f32[1024,512]{1,0:T(8,128)S(1)}, bf16[512,512]{1,0:T(8,128)(2,1)}, bf16[512,1024]{1,0:T(8,128)(2,1)}) custom-call(s32[8,4]{1,0:T(8,128)S(1)} %copy.18.refs_0_, f32[8,2]{1,0:T(8,128)S(1)} %copy.19.refs_1_, s32[8,4,128]{2,1,0:T(4,128)S(1)} %bitcast.22, s32[8,4,128]{2,1,0:T(4,128)S(1)} %bitcast.27, bf16[4,256,512]{2,1,0:T(8,128)(2,1)S(1)} %copy-done.9, ...), custom_call_target="tpu_custom_call" | custom-call | flops 2310000128 | bytes 3178688 | tf_op jit(solution)/shard_map/pallas_call | solution.py:61
  36.8 6.1 %all-to-all-start.1 = ((bf16[16,32,512]{2,1,0:T(8,128)(2,1)}), bf16[16,32,512]{2,1,0:T(8,128)(2,1)S(1)}, u32[]{:S(2)}, u32[]{:S(2)}) async-start(bf16[16,32,512]{2,1,0:T(8,128)(2,1)} %bitcast.14), calls=%async_computation.1 | async-start | bytes 1048576 | tf_op jit(solution)/shard_map/all_to_all | solution.py:575
  43.0 12.8 %shard_map.172 = (f32[512,512]{1,0:T(8,128)S(1)}, f32[8,128]{1,0:T(8,128)S(1)}, f32[256,1024]{1,0:T(8,128)S(1)}, bf16[256,1024]{1,0:T(8,128)(2,1)S(1)}) custom-call(s32[8,4]{1,0:T(8,128)S(1)} %copy.18.refs_0_, f32[8,2]{1,0:T(8,128)S(1)} %copy.19.refs_1_, s32[8,128]{1,0:T(8,128)S(1)} %broadcast_in_dim.2.refs_0_.refs_2_.place_ref, s32[8,4,128]{2,1,0:T(4,128)S(1)} %bitcast.23, ...), custom_call_target="tpu_custom_call" | custom-call | flops 9900000256 | bytes 37056 | tf_op jit(solution)/shard_map/pallas_call | solution.py:61
  55.8 3.0 %shard_map.173 = (f32[80,256]{1,0:T(8,128)S(1)}, f32[80,256]{1,0:T(8,128)S(1)}, bf16[512,512]{1,0:T(8,128)(2,1)S(1)}, f32[512,512]{1,0:T(8,128)}) custom-call(s32[8,128]{1,0:T(8,128)S(1)} %broadcast_in_dim.2.refs_0_.refs_2_.place_ref, f32[512,512]{1,0:T(8,128)S(1)} %copy-done.12, f32[512,512]{1,0:T(8,128)S(1)} %copy-done.3, ...), custom_call_target="tpu_custom_call" | custom-call | flops 2969999872 | bytes 3301376 | tf_op jit(solution)/shard_map/pallas_call | solution.py:61
  60.4 2.1 %shard_map.176 = (f32[256,1024]{1,0:T(8,128)S(1)}, bf16[256,2048]{1,0:T(8,128)(2,1)S(1)}) custom-call(s32[8,128]{1,0:T(8,128)S(1)} %broadcast_in_dim.2.refs_0_.refs_2_.place_ref, bf16[512,512]{1,0:T(8,128)(2,1)S(1)} %get-tuple-element.72.refs_1_, f32[512,512]{1,0:T(8,128)S(1)} %copy-done.6, bf16[256,1024]{1,0:T(8,128)(2,1)S(1)} %copy-done.11, ...), custom_call_target="tpu_custom_call" | custom-call | flops 1980000000 | bytes 2101248 | tf_op jit(solution)/shard_map/pallas_call | solution.py:61
  64.7 2.8 %collective-permute-done.7.refs_1_ = f32[80,256]{1,0:T(8,128)S(1)} collective-permute-done((f32[80,256]{1,0:T(8,128)S(1)}, f32[80,256]{1,0:T(8,128)S(1)}, u32[]{:S(2)}, u32[]{:S(2)}) %collective-permute-start.7) | collective-permute-done | bytes 81952 | tf_op jit(solution)/shard_map/ppermute | solution.py:494
  69.3 2.8 %collective-permute-done.8.refs_1_ = f32[80,256]{1,0:T(8,128)S(1)} collective-permute-done((f32[80,256]{1,0:T(8,128)S(1)}, f32[80,256]{1,0:T(8,128)S(1)}, u32[]{:S(2)}, u32[]{:S(2)}) %collective-permute-start.8) | collective-permute-done | bytes 81952 | tf_op jit(solution)/shard_map/ppermute | solution.py:494
  78.0 2.4 %collective-permute-start.11 = (f32[80,256]{1,0:T(8,128)S(1)}, f32[80,256]{1,0:T(8,128)S(1)}, u32[]{:S(2)}, u32[]{:S(2)}) collective-permute-start(f32[80,256]{1,0:T(8,128)S(1)} %shard_map.180.refs_0_), channel_id=1, source_target_pairs={{0,8},{1,9},{2,10},{3,11},{4,12},{5,13},{6,14},{7,15},{8,0},{9,1},... | collective-permute-start | bytes 245768 | tf_op jit(solution)/shard_map/ppermute | solution.py:494
  80.4 3.6 %collective-permute-done.11.refs_1_ = f32[80,256]{1,0:T(8,128)S(1)} collective-permute-done((f32[80,256]{1,0:T(8,128)S(1)}, f32[80,256]{1,0:T(8,128)S(1)}, u32[]{:S(2)}, u32[]{:S(2)}) %collective-permute-start.11) | collective-permute-done | bytes 81952 | tf_op jit(solution)/shard_map/ppermute | solution.py:494
  84.4 2.6 %collective-permute-done.14.refs_2_ = bf16[64,2048]{1,0:T(8,128)(2,1)S(1)} collective-permute-done((bf16[64,2048]{1,0:T(8,128)(2,1)S(1)}, bf16[64,2048]{1,0:T(8,128)(2,1)S(1)}, u32[]{:S(2)}, u32[]{:S(2)}) %collective-permute-start.14) | collective-permute-done | bytes 262176 | tf_op jit(solution)/shard_map/ppermute | solution.py:514
  87.1 2.1 %shard_map.183 = (bf16[512,512]{1,0:T(8,128)(2,1)S(1)}, f32[256,512]{1,0:T(8,128)S(1)}, bf16[256,512]{1,0:T(8,128)(2,1)S(1)}) custom-call(s32[8,128]{1,0:T(8,128)S(1)} %broadcast_in_dim.2.refs_0_.refs_2_.place_ref, f32[512,512]{1,0:T(8,128)S(1)} %copy-done.6, f32[512,512]{1,0:T(8,128)S(1)} %copy-done.7, ...), custom_call_target="tpu_custom_call" | custom-call | flops 1980000000 | bytes 2265088 | tf_op jit(solution)/shard_map/pallas_call | solution.py:61
  99.1 2.4 %collective-permute-start.21 = (bf16[16,2560]{1,0:T(8,128)(2,1)S(1)}, bf16[16,2560]{1,0:T(8,128)(2,1)S(1)}, u32[]{:S(2)}, u32[]{:S(2)}) collective-permute-start(bf16[16,2560]{1,0:T(8,128)(2,1)S(1)} %get-tuple-element.95), channel_id=1, source_target_pairs={{0,8},{1,9},{2,10},{3,11},{4,12},{5,13},{6,14},{7,15},{8,0},{9,1},... | collective-permute-start | bytes 245768 | tf_op jit(solution)/shard_map/ppermute | solution.py:514
  103.0 3.7 %collective-permute-done.21.refs_2_ = bf16[16,2560]{1,0:T(8,128)(2,1)S(1)} collective-permute-done((bf16[16,2560]{1,0:T(8,128)(2,1)S(1)}, bf16[16,2560]{1,0:T(8,128)(2,1)S(1)}, u32[]{:S(2)}, u32[]{:S(2)}) %collective-permute-start.21) | collective-permute-done | bytes 81952 | tf_op jit(solution)/shard_map/ppermute | solution.py:514
  107.8 2.6 %collective-permute-start.25 = (bf16[16,1536]{1,0:T(8,128)(2,1)S(1)}, bf16[16,1536]{1,0:T(8,128)(2,1)S(1)}, u32[]{:S(2)}, u32[]{:S(2)}) collective-permute-start(bf16[16,1536]{1,0:T(8,128)(2,1)S(1)} %slice.14.refs_1_), channel_id=1, source_target_pairs={{0,12},{1,13},{2,14},{3,15},{4,8},{5,9},{6,10},{7,11},{8,4},{9,5},... | collective-permute-start | bytes 147464 | tf_op jit(solution)/shard_map/ppermute | solution.py:514
  112.2 2.5 %collective-permute-start.32 = (bf16[16,1024]{1,0:T(8,128)(2,1)S(1)}, bf16[16,1024]{1,0:T(8,128)(2,1)S(1)}, u32[]{:S(2)}, u32[]{:S(2)}) collective-permute-start(bf16[16,1024]{1,0:T(8,128)(2,1)S(1)} %slice.15.refs_1_), channel_id=1, source_target_pairs={{0,12},{1,13},{2,14},{3,15},{4,8},{5,9},{6,10},{7,11},{8,4},{9,5},... | collective-permute-start | bytes 98312 | tf_op jit(solution)/shard_map/ppermute | solution.py:514
  120.3 3.8 %shard_map.189 = (f32[512,512]{1,0:T(8,128)}, f32[8,128]{1,0:T(8,128)S(1)}) custom-call(s32[8,128]{1,0:T(8,128)S(1)} %broadcast_in_dim.2.refs_0_.refs_2_.place_ref, bf16[512,512]{1,0:T(8,128)(2,1)S(1)} %get-tuple-element.72.refs_1_, bf16[512,512]{1,0:T(8,128)(2,1)S(1)} %get-tuple-element.86.refs_2_, f32[512,512]{1,0:T(8,128)S(1)} %copy-done.6, ...), custom_call_target="tpu_custom_call" | custom-call | flops 3849999872 | bytes 3313664 | tf_op jit(solution)/shard_map/pallas_call | solution.py:61
  (129 shorter events, 50.0 us)
Async XLA Ops:
  6.3 8.7 %collective-permute-start = (f32[72,256]{1,0:T(8,128)S(1)}, f32[72,256]{1,0:T(8,128)S(1)}, u32[]{:S(2)}, u32[]{:S(2)}) collective-permute-start(f32[72,256]{1,0:T(8,128)S(1)} %get-tuple-element.57), channel_id=1, source_target_pairs={{0,16},{16,0},{1,17},{17,1},{2,18},{18,2},{3,19},{19,3},{4,20},{20... | collective-permute-start | bytes 221192 | tf_op jit(solution)/shard_map/ppermute | solution.py:489
  6.8 30.0 %all-to-all-start = ((bf16[16,32,512]{2,1,0:T(8,128)(2,1)}), bf16[16,32,512]{2,1,0:T(8,128)(2,1)S(1)}, u32[]{:S(2)}, u32[]{:S(2)}) async-start(bf16[16,32,512]{2,1,0:T(8,128)(2,1)} %bitcast.12), calls=%async_computation | async-start | bytes 1048576 | tf_op jit(solution)/shard_map/all_to_all | solution.py:556
  15.0 5.9 %collective-permute-start.1 = (f32[72,256]{1,0:T(8,128)S(1)}, f32[72,256]{1,0:T(8,128)S(1)}, u32[]{:S(2)}, u32[]{:S(2)}) collective-permute-start(f32[72,256]{1,0:T(8,128)S(1)} %shard_map.163.refs_5_.refs_0_), channel_id=1, source_target_pairs={{0,1},{1,0},{2,3},{3,2},{4,5},{5,4},{6,7},{7,6},{8,9},{9,8},{10,11... | collective-permute-start | bytes 221192 | tf_op jit(solution)/shard_map/ppermute | solution.py:494
  36.7 19.0 %collective-permute-start.5 = (f32[72,256]{1,0:T(8,128)S(1)}, f32[72,256]{1,0:T(8,128)S(1)}, u32[]{:S(2)}, u32[]{:S(2)}) collective-permute-start(f32[72,256]{1,0:T(8,128)S(1)} %shard_map.171.refs_5_.refs_3_), channel_id=1, source_target_pairs={{0,16},{16,0},{1,17},{17,1},{2,18},{18,2},{3,19},{19,3},{4,20},{20... | collective-permute-start | bytes 221192 | tf_op jit(solution)/shard_map/ppermute | solution.py:489
  36.8 22.2 %all-to-all-start.1 = ((bf16[16,32,512]{2,1,0:T(8,128)(2,1)}), bf16[16,32,512]{2,1,0:T(8,128)(2,1)S(1)}, u32[]{:S(2)}, u32[]{:S(2)}) async-start(bf16[16,32,512]{2,1,0:T(8,128)(2,1)} %bitcast.14), calls=%async_computation.1 | async-start | bytes 1048576 | tf_op jit(solution)/shard_map/all_to_all | solution.py:575
  62.6 11.2 %collective-permute-start.10 = (bf16[256,2048]{1,0:T(8,128)(2,1)S(1)}, bf16[256,2048]{1,0:T(8,128)(2,1)S(1)}, u32[]{:S(2)}, u32[]{:S(2)}) collective-permute-start(bf16[256,2048]{1,0:T(8,128)(2,1)S(1)} %get-tuple-element.79.refs_2_), channel_id=1, source_target_pairs={{0,16},{16,0},{1,17},{17,1},{2,18},{18,2},{3,19},{19,3},{4,20},{20... | collective-permute-start | bytes 3145736 | tf_op jit(solution)/shard_map/ppermute | solution.py:489
  72.1 5.9 %collective-permute-start.9 = (f32[80,256]{1,0:T(8,128)S(1)}, f32[80,256]{1,0:T(8,128)S(1)}, u32[]{:S(2)}, u32[]{:S(2)}) collective-permute-start(f32[80,256]{1,0:T(8,128)S(1)} %shard_map.178.refs_4_.refs_0_), channel_id=1, source_target_pairs={{0,4},{1,5},{2,6},{3,7},{4,0},{5,1},{6,2},{7,3},{8,12},{9,13},{10,... | collective-permute-start | bytes 245768 | tf_op jit(solution)/shard_map/ppermute | solution.py:494
  74.4 10.0 %collective-permute-start.13 = (bf16[64,2048]{1,0:T(8,128)(2,1)S(1)}, bf16[64,2048]{1,0:T(8,128)(2,1)S(1)}, u32[]{:S(2)}, u32[]{:S(2)}) collective-permute-start(bf16[64,2048]{1,0:T(8,128)(2,1)S(1)} %get-tuple-element.83), channel_id=1, source_target_pairs={{0,1},{1,0},{2,3},{3,2},{4,5},{5,4},{6,7},{7,6},{8,9},{9,8},{10,11... | collective-permute-start | bytes 786440 | tf_op jit(solution)/shard_map/ppermute | solution.py:514
  75.9 11.0 %collective-permute-start.14 = (bf16[64,2048]{1,0:T(8,128)(2,1)S(1)}, bf16[64,2048]{1,0:T(8,128)(2,1)S(1)}, u32[]{:S(2)}, u32[]{:S(2)}) collective-permute-start(bf16[64,2048]{1,0:T(8,128)(2,1)S(1)} %get-tuple-element.84), channel_id=1, source_target_pairs={{0,2},{1,3},{2,0},{3,1},{4,6},{5,7},{6,4},{7,5},{8,10},{9,11},{10,... | collective-permute-start | bytes 786440 | tf_op jit(solution)/shard_map/ppermute | solution.py:514
  77.4 9.6 %collective-permute-start.15 = (bf16[64,2048]{1,0:T(8,128)(2,1)S(1)}, bf16[64,2048]{1,0:T(8,128)(2,1)S(1)}, u32[]{:S(2)}, u32[]{:S(2)}) collective-permute-start(bf16[64,2048]{1,0:T(8,128)(2,1)S(1)} %get-tuple-element.85), channel_id=1, source_target_pairs={{0,3},{1,2},{2,1},{3,0},{4,7},{5,6},{6,5},{7,4},{8,11},{9,10},{10,... | collective-permute-start | bytes 786440 | tf_op jit(solution)/shard_map/ppermute | solution.py:514
  78.0 6.1 %collective-permute-start.11 = (f32[80,256]{1,0:T(8,128)S(1)}, f32[80,256]{1,0:T(8,128)S(1)}, u32[]{:S(2)}, u32[]{:S(2)}) collective-permute-start(f32[80,256]{1,0:T(8,128)S(1)} %shard_map.180.refs_0_), channel_id=1, source_target_pairs={{0,8},{1,9},{2,10},{3,11},{4,12},{5,13},{6,14},{7,15},{8,0},{9,1},... | collective-permute-start | bytes 245768 | tf_op jit(solution)/shard_map/ppermute | solution.py:494
  99.1 7.6 %collective-permute-start.21 = (bf16[16,2560]{1,0:T(8,128)(2,1)S(1)}, bf16[16,2560]{1,0:T(8,128)(2,1)S(1)}, u32[]{:S(2)}, u32[]{:S(2)}) collective-permute-start(bf16[16,2560]{1,0:T(8,128)(2,1)S(1)} %get-tuple-element.95), channel_id=1, source_target_pairs={{0,8},{1,9},{2,10},{3,11},{4,12},{5,13},{6,14},{7,15},{8,0},{9,1},... | collective-permute-start | bytes 245768 | tf_op jit(solution)/shard_map/ppermute | solution.py:514
  101.4 6.3 %collective-permute-start.22 = (bf16[16,2560]{1,0:T(8,128)(2,1)S(1)}, bf16[16,2560]{1,0:T(8,128)(2,1)S(1)}, u32[]{:S(2)}, u32[]{:S(2)}) collective-permute-start(bf16[16,2560]{1,0:T(8,128)(2,1)S(1)} %get-tuple-element.96), channel_id=1, source_target_pairs={{0,12},{1,13},{2,14},{3,15},{4,8},{5,9},{6,10},{7,11},{8,4},{9,5},... | collective-permute-start | bytes 245768 | tf_op jit(solution)/shard_map/ppermute | solution.py:514
  107.8 7.0 %collective-permute-start.25 = (bf16[16,1536]{1,0:T(8,128)(2,1)S(1)}, bf16[16,1536]{1,0:T(8,128)(2,1)S(1)}, u32[]{:S(2)}, u32[]{:S(2)}) collective-permute-start(bf16[16,1536]{1,0:T(8,128)(2,1)S(1)} %slice.14.refs_1_), channel_id=1, source_target_pairs={{0,12},{1,13},{2,14},{3,15},{4,8},{5,9},{6,10},{7,11},{8,4},{9,5},... | collective-permute-start | bytes 147464 | tf_op jit(solution)/shard_map/ppermute | solution.py:514
  110.4 6.3 %collective-permute-start.24 = (bf16[16,1536]{1,0:T(8,128)(2,1)S(1)}, bf16[16,1536]{1,0:T(8,128)(2,1)S(1)}, u32[]{:S(2)}, u32[]{:S(2)}) collective-permute-start(bf16[16,1536]{1,0:T(8,128)(2,1)S(1)} %slice.14.refs_1_), channel_id=1, source_target_pairs={{0,8},{1,9},{2,10},{3,11},{4,12},{5,13},{6,14},{7,15},{8,0},{9,1},... | collective-permute-start | bytes 147464 | tf_op jit(solution)/shard_map/ppermute | solution.py:514
  110.6 6.0 %collective-permute-start.23 = (bf16[16,1536]{1,0:T(8,128)(2,1)S(1)}, bf16[16,1536]{1,0:T(8,128)(2,1)S(1)}, u32[]{:S(2)}, u32[]{:S(2)}) collective-permute-start(bf16[16,1536]{1,0:T(8,128)(2,1)S(1)} %slice.14.refs_1_), channel_id=1, source_target_pairs={{0,4},{1,5},{2,6},{3,7},{4,0},{5,1},{6,2},{7,3},{8,12},{9,13},{10,... | collective-permute-start | bytes 147464 | tf_op jit(solution)/shard_map/ppermute | solution.py:514
  112.2 7.5 %collective-permute-start.32 = (bf16[16,1024]{1,0:T(8,128)(2,1)S(1)}, bf16[16,1024]{1,0:T(8,128)(2,1)S(1)}, u32[]{:S(2)}, u32[]{:S(2)}) collective-permute-start(bf16[16,1024]{1,0:T(8,128)(2,1)S(1)} %slice.15.refs_1_), channel_id=1, source_target_pairs={{0,12},{1,13},{2,14},{3,15},{4,8},{5,9},{6,10},{7,11},{8,4},{9,5},... | collective-permute-start | bytes 98312 | tf_op jit(solution)/shard_map/ppermute | solution.py:514
  114.8 9.3 %collective-permute-start.31 = (bf16[16,1024]{1,0:T(8,128)(2,1)S(1)}, bf16[16,1024]{1,0:T(8,128)(2,1)S(1)}, u32[]{:S(2)}, u32[]{:S(2)}) collective-permute-start(bf16[16,1024]{1,0:T(8,128)(2,1)S(1)} %slice.15.refs_1_), channel_id=1, source_target_pairs={{0,8},{1,9},{2,10},{3,11},{4,12},{5,13},{6,14},{7,15},{8,0},{9,1},... | collective-permute-start | bytes 98312 | tf_op jit(solution)/shard_map/ppermute | solution.py:514
  114.8 9.3 %collective-permute-start.30 = (bf16[16,1024]{1,0:T(8,128)(2,1)S(1)}, bf16[16,1024]{1,0:T(8,128)(2,1)S(1)}, u32[]{:S(2)}, u32[]{:S(2)}) collective-permute-start(bf16[16,1024]{1,0:T(8,128)(2,1)S(1)} %slice.15.refs_1_), channel_id=1, source_target_pairs={{0,4},{1,5},{2,6},{3,7},{4,0},{5,1},{6,2},{7,3},{8,12},{9,13},{10,... | collective-permute-start | bytes 98312 | tf_op jit(solution)/shard_map/ppermute | solution.py:514
  116.7 10.5 %collective-permute-start.28 = (bf16[64,1536]{1,0:T(8,128)(2,1)S(1)}, bf16[64,1536]{1,0:T(8,128)(2,1)S(1)}, u32[]{:S(2)}, u32[]{:S(2)}) collective-permute-start(bf16[64,1536]{1,0:T(8,128)(2,1)S(1)} %shard_map.188.refs_7_.refs_1_), channel_id=1, source_target_pairs={{0,3},{1,2},{2,1},{3,0},{4,7},{5,6},{6,5},{7,4},{8,11},{9,10},{10,... | collective-permute-start | bytes 589832 | tf_op jit(solution)/shard_map/ppermute | solution.py:514
  118.3 10.0 %collective-permute-start.27 = (bf16[64,1536]{1,0:T(8,128)(2,1)S(1)}, bf16[64,1536]{1,0:T(8,128)(2,1)S(1)}, u32[]{:S(2)}, u32[]{:S(2)}) collective-permute-start(bf16[64,1536]{1,0:T(8,128)(2,1)S(1)} %shard_map.188.refs_7_.refs_1_), channel_id=1, source_target_pairs={{0,2},{1,3},{2,0},{3,1},{4,6},{5,7},{6,4},{7,5},{8,10},{9,11},{10,... | collective-permute-start | bytes 589832 | tf_op jit(solution)/shard_map/ppermute | solution.py:514
  119.8 8.5 %collective-permute-start.26 = (bf16[64,1536]{1,0:T(8,128)(2,1)S(1)}, bf16[64,1536]{1,0:T(8,128)(2,1)S(1)}, u32[]{:S(2)}, u32[]{:S(2)}) collective-permute-start(bf16[64,1536]{1,0:T(8,128)(2,1)S(1)} %shard_map.188.refs_7_.refs_1_), channel_id=1, source_target_pairs={{0,1},{1,0},{2,3},{3,2},{4,5},{5,4},{6,7},{7,6},{8,9},{9,8},{10,11... | collective-permute-start | bytes 589832 | tf_op jit(solution)/shard_map/ppermute | solution.py:514
  124.1 6.0 %collective-permute-start.35 = (bf16[64,1024]{1,0:T(8,128)(2,1)S(1)}, bf16[64,1024]{1,0:T(8,128)(2,1)S(1)}, u32[]{:S(2)}, u32[]{:S(2)}) collective-permute-start(bf16[64,1024]{1,0:T(8,128)(2,1)S(1)} %shard_map.192.refs_1_), channel_id=1, source_target_pairs={{0,3},{1,2},{2,1},{3,0},{4,7},{5,6},{6,5},{7,4},{8,11},{9,10},{10,... | collective-permute-start | bytes 393224 | tf_op jit(solution)/shard_map/ppermute | solution.py:514
  128.5 7.7 %collective-permute-start.29 = (bf16[256,1536]{1,0:T(8,128)(2,1)S(1)}, bf16[256,1536]{1,0:T(8,128)(2,1)S(1)}, u32[]{:S(2)}, u32[]{:S(2)}) collective-permute-start(bf16[256,1536]{1,0:T(8,128)(2,1)S(1)} %shard_map.190.mine_ref), channel_id=1, source_target_pairs={{0,16},{16,0},{1,17},{17,1},{2,18},{18,2},{3,19},{19,3},{4,20},{20... | collective-permute-start | bytes 2359304 | tf_op jit(solution)/shard_map/ppermute | solution.py:489
  (32 other events, 214.0 us)

commit v4 on v3

--- a/solution.py
+++ b/solution.py
@@ -267,7 +267,7 @@
 
 
 def key_kernel(
-    place_ref, ek_ref, v_ref, sum_mine_ref, sum_theirs_ref, features_ref, kblock_ref, mine_ref, theirs_ref
+    place_ref, ek_ref, v_ref, sum_mine_ref, sum_theirs_ref, features_ref, kblock_ref, mine_ref, theirs_ref, *, arrive
 ):
     pairs = ek_ref.shape[1] // LANES
     for p in range(pairs):
@@ -275,6 +275,7 @@
         dkv, dks = load_summary(place_ref, p, pairs, sum_mine_ref, sum_theirs_ref)
         key_side = mm_wide(v_ref[:, at], block_diagonal(dkv), NT) + dks
         kblock_ref[:, at] = (key_side * ek_ref[:, at]).astype(bf16)
+    arrive(0)
     store_halves(place_ref, mm(features_ref[...], kblock_ref[...], TN), mine_ref, theirs_ref, slice(None))
 
 
@@ -308,24 +309,17 @@
     out_ref[...] = total + mm(jnp.concatenate(blocks, axis=1), wv_ref[...], NT) + graph_ref[...]
 
 
-def tile_hits(count_ref, dst_ref, r, tile):
-    slots = dst_ref.shape[2]
-    live = iota((TILE, slots), 1) < count_ref[r : r + 1, tile : tile + 1]
-    target = iota((TILE, slots), 0) == dst_ref[r, tile : tile + 1, :]
-    hit = jnp.where(target & live, 1.0, 0.0)
-    return hit / jnp.maximum(jnp.sum(hit, axis=1, keepdims=True), 1.0)
-
-
-def tile_incidence(count_ref, coef_ref, dst_ref, tile):
-    basis_count = coef_ref.shape[1]
-    hits, scaled = [], [[] for _ in range(basis_count)]
-    for r in range(dst_ref.shape[0]):
-        hit = tile_hits(count_ref, dst_ref, r, tile)
-        hits.append(hit)
-        for b in range(basis_count):
-            scaled[b].append(hit * coef_ref[r : r + 1, b : b + 1])
-    high, low = split(jnp.concatenate([jnp.concatenate(part, axis=1) for part in scaled], axis=0))
-    return jnp.concatenate(hits, axis=1), jnp.concatenate([high, low], axis=0)
+def tile_incidence(count_ref, dst_ref, tile):
+    relations, _, slots = dst_ref.shape
+    hits = []
+    for r in range(relations):
+        live = iota((TILE, slots), 1) < count_ref[r : r + 1, tile : tile + 1]
+        target = iota((TILE, slots), 0) == dst_ref[r, tile : tile + 1, :]
+        hits.append(jnp.where(target & live, 1.0, 0.0))
+    ours = jnp.where(iota((relations * slots, LANES), 0) // slots == iota((relations * slots, LANES), 1), 1.0, 0.0)
+    degree = mm(jnp.concatenate(hits, axis=1).astype(bf16), ours.astype(bf16))
+    inverse = 1.0 / jnp.maximum(degree, 1.0)
+    return [hit * inverse[:, r : r + 1] for r, hit in enumerate(hits)]
 
 
 def tile_pick(src_ref, tile, table_rows):
@@ -336,8 +330,13 @@
 def backward_kernel(count_ref, coef_ref, src_ref, dst_ref, grad_ref, *refs, tile, last, leave):
     mixed_ref = refs[-1]
     table_ref = refs[0 if tile == 0 else 1]
-    _, scaled = tile_incidence(count_ref, coef_ref, dst_ref, tile)
-    both = mm(scaled, tile_pick(src_ref, tile, table_ref.shape[0]), NT)
+    hits = tile_incidence(count_ref, dst_ref, tile)
+    scaled = [
+        jnp.concatenate([hit * coef_ref[r : r + 1, b : b + 1] for r, hit in enumerate(hits)], axis=1)
+        for b in range(coef_ref.shape[1])
+    ]
+    high, low = split(jnp.concatenate(scaled, axis=0))
+    both = mm(jnp.concatenate([high, low], axis=0), tile_pick(src_ref, tile, table_ref.shape[0]), NT)
     wide = both.shape[0] // 2
     high, low = split(both[:wide] + both[wide:])
     mixed_ref[:wide, :] = high
@@ -351,31 +350,31 @@
         sent_ref[...] = table[table.shape[0] - sent_ref.shape[0] :, :].astype(bf16)
 
 
-def forward_kernel(count_ref, coef_ref, place_ref, src_ref, dst_ref, *refs, arrive):
+def forward_kernel(count_ref, place_ref, src_ref, dst_ref, *refs, arrive):
     relations, tiles, slots = src_ref.shape
     own_ref, halo_ref, high_ref, low_ref, bases_ref = refs[:5]
-    mixed_refs, (cot_ref, conv_ref, coef_grad_ref, mine_ref, theirs_ref, basis_ref) = refs[5 : 5 + tiles], refs[5 + tiles :]
+    mixed_refs, refs = refs[5 : 5 + tiles], refs[5 + tiles :]
+    cot_ref, conv_ref, coef_grad_ref, mine_ref, theirs_ref, basis_ref, table_ref = refs
     basis_count = bases_ref.shape[0]
     wide = basis_count * TILE
     rows, width = own_ref.shape
     sums = [jnp.zeros((1, relations * slots), f32) for _ in range(basis_count)]
     for t in range(tiles):
-        hit, _ = tile_incidence(count_ref, coef_ref, dst_ref, t)
-        pick = tile_pick(src_ref, t, rows + halo_ref.shape[0])
+        hit = jnp.concatenate(tile_incidence(count_ref, dst_ref, t), axis=1)
+        pick = tile_pick(src_ref, t, table_ref.shape[0])
         if t == 0:
             for i in range(4):
                 arrive(i)
-        grads = jnp.concatenate([high_ref[t], low_ref[t]], axis=0)
-        dots = [mm(grads, table_ref[...], NT) for table_ref in (own_ref, halo_ref)]
-        dots = [(x[:wide] + x[wide:]).astype(bf16) for x in dots]
-        edge = mm(dots[0], pick[:rows]) + mm(dots[1], pick[rows:])
+            table_ref[:rows, :] = own_ref[...]
+            table_ref[rows:, :] = halo_ref[...]
+        dots = mm(jnp.concatenate([high_ref[t], low_ref[t]], axis=0), table_ref[...], NT)
+        edge = mm((dots[:wide] + dots[wide:]).astype(bf16), pick)
         for b in range(basis_count):
             sums[b] += jnp.sum(edge[b * TILE : (b + 1) * TILE] * hit, axis=0, keepdims=True)
         if t == 0:
             arrive(4)
         arrive(5 + t)
-        mixed_ref = mixed_refs[t]
-        both = mm(mixed_ref[:, :rows], own_ref[...]) + mm(mixed_ref[:, rows:], halo_ref[...])
+        both = mm(mixed_refs[t][...], table_ref[...])
         both = (both[:wide] + both[wide:]).astype(bf16)
         at = slice(t * TILE, (t + 1) * TILE)
         conv = None
@@ -399,6 +398,10 @@
         store_halves(place_ref, whole, mine_ref, theirs_ref, slice(b * width, (b + 1) * width))
 
 
+def copy_kernel(a_ref, out_ref):
+    out_ref[...] = a_ref[...]
+
+
 def add_kernel(a_ref, b_ref, out_ref):
     out_ref[...] = a_ref[...] + b_ref[...]
 
@@ -451,13 +454,15 @@
     blocks = [ref[...] for ref in refs[:-1]]
     rows = blocks[0].shape[0]
     for i in range(len(blocks)):
-        out_ref[i * rows : (i + 1) * rows, :] = choose(place_ref, first_bit, blocks, i)
+        out_ref[i * rows : (i + 1) * rows, :] = choose(place_ref, first_bit, blocks, i).astype(out_ref.dtype)
 
 
 def finish_kernel(
-    place_ref, sum_mine_ref, sum_theirs_ref, mine_ref, theirs_ref, *refs, scale, value_at, outs
+    place_ref, sum_mine_ref, sum_theirs_ref, mine_ref, theirs_ref, *refs, scale, value_at, outs, after
 ):
-    holds, sems = refs[outs:-1], refs[-1]
+    refs = refs[after:]
+    refs[outs][...] = jnp.zeros((8, LANES), f32)
+    holds, sems = refs[outs + 1 : -1], refs[-1]
     targets = []
     for out_ref in refs[:outs]:
         targets += [out_ref] if len(out_ref.shape) == 2 else [out_ref.at[b] for b in range(out_ref.shape[0])]
@@ -581,13 +586,13 @@
         kept["conv"], kept["coef"], *kept["bases"] = call(
             forward_kernel,
             [square, shape(8, LANES), *halves(basis_count)],
-            [count, rel_coef, place, src, dst],
+            [count, place, src, dst],
             [x],
             8 + table_rows // 64,
             far=[features, halo, grad_high, grad_low, bases, *[kept["mixed", t] for t in range(tiles)], cotangent],
             us=9,
             lazy=True,
-            scratch=[shape(basis_count, rows, width, dtype=bf16)],
+            scratch=[shape(basis_count, rows, width, dtype=bf16), shape(table_rows, width, dtype=bf16)],
         )
         return None
 
@@ -624,26 +629,27 @@
         )
         return [own, *exchange(out, first_bit)]
 
-    def gather(own, first_bit, count, after=()):
-        outs = [shape(own.shape[0] * count, own.shape[1], dtype=own.dtype)]
-        blocks = [own, *exchange([own] * (count - 1), first_bit)]
+    def join(blocks, first_bit, after=()):
+        own = blocks[0]
+        rows = len(blocks) * own.shape[0]
+        outs = [shape(rows, own.shape[1], dtype=bf16 if rows >= 16 else f32)]
         return call(functools.partial(join_kernel, first_bit=first_bit), outs, [place, *blocks], after)[0]
 
     def total(blocks, after=()):
         out = shape(*blocks[0].shape, dtype=bf16 if blocks[0].shape[0] >= 16 else f32)
         return call(total_kernel, [out], blocks, after)[0]
 
-    def finish(own, bodies, value_at):
+    def finish(own, bodies, value_at, after=()):
         count = sum(max(n, 1) for n in bodies)
         return pl.pallas_call(
-            functools.partial(finish_kernel, scale=scale, value_at=value_at, outs=len(bodies)),
-            out_shape=[shape(n, width, width) if n else shape(width, width) for n in bodies],
-            in_specs=[VMEM] * 5,
-            out_specs=[HBM] * len(bodies),
+            functools.partial(finish_kernel, scale=scale, value_at=value_at, outs=len(bodies), after=len(after)),
+            out_shape=[shape(n, width, width) if n else shape(width, width) for n in bodies] + [shape(8, LANES)],
+            in_specs=[VMEM] * (5 + len(after)),
+            out_specs=[HBM] * len(bodies) + [VMEM],
             scratch_shapes=[pltpu.VMEM((width, width), f32)] * count + [pltpu.SemaphoreType.DMA((count,))],
             compiler_params=pltpu.CompilerParams(vmem_limit_bytes=12 * 1024 * 1024),
             cost_estimate=pl.CostEstimate(flops=int(count * 0.8e9), bytes_accessed=0, transcendentals=0),
-        )(place, dkv_mine, dkv_theirs, own, swap_cores(own))
+        )(place, dkv_mine, dkv_theirs, own, swap_cores(own), *after)
 
     def run_returned(x):
         (kept["graph"],) = call(
@@ -664,15 +670,20 @@
         return kept["early"][1]
 
     def run_early_plane(x):
-        operands = [kept["bases"][0], kept["early"][0], swap_cores(kept["early"][1])]
+        operands = [kept["bases"][0], kept["early"][0], swap_cores(kept["early theirs"])]
         kept["blocks"] = scatter(operands, 0, plane, plane_rows, 2, [x])
         return kept["blocks"][0]
 
-    def run_early_sum(x):
-        (kept["early sum"],) = call(total_kernel, [shape(plane_rows, early_width)], kept["blocks"], [x])
-        return kept["early sum"]
-
-    second = {"core": [run_returned], bits[0]: [run_query], z1: [run_early_plane], "back": [run_early_sum]}
+    def run_early_line(x):
+        kept["blocks"] = scatter(kept["blocks"], z1, planes, place_rows, 1, [x])
+        return kept["blocks"][0]
+
+    def run_early_theirs(x):
+        (kept["early theirs"],) = call(copy_kernel, [halves(early_count)[1]], [kept["early"][1]], [x])
+        return kept["early theirs"]
+
+    second = {"core": [run_returned], bits[0]: [run_query], y: [run_early_theirs], z1: [run_early_plane]}
+    second["back"] = [run_early_line]
     dkv_mine, dkv_theirs, after = sum_summary(dkv_mine, dkv_theirs, bits, functools.partial(run_all, second))
     kblock, key_mine, key_theirs = call(
         key_kernel,
@@ -680,29 +691,31 @@
         [place, exp_key, values, dkv_mine, dkv_theirs],
         after,
         far=[features],
-        us=1.8,
+        us=1.3,
+        lazy=True,
     )
+    def spread(x, first_bit, count):
+        return [x, *exchange([x] * (count - 1), first_bit)]
+
     key = scatter([key_mine, swap_cores(key_theirs)], 0, plane, plane_rows)
-    (key,) = call(total_kernel, [shape(plane_rows, width)], key)
-    own = scatter([kept["early sum"], key], z1, planes, place_rows, 2)
-    own = total(own)
-    cut = (basis_count + 1) * width
-    own, last = own[:, :cut], own[:, cut:]
-    own = gather(own, z1, planes).astype(bf16)
+    early = spread(total(kept["blocks"], [key[0]]), z1, planes)
+    key = spread(total(key, [early[0]]), z1, planes)
+    early = join(early, z1, [key[0]])
+    key = spread(total(key), 0, plane)
+    early = spread(early, 0, plane)
+    key = join(key, 0, [early[0]])
     grad_x, token = call(
         input_grad_kernel,
         [square, shape(8, LANES)],
         [place, qblock, kblock, exp_key, dkv_mine, dkv_theirs, kept["graph"]],
-        [own],
+        [key],
         16,
         far=[w_query, w_key, w_value],
         us=3.5,
     )
-    last = gather(last, z1, planes, [token]).astype(bf16)
-    own = gather(own, 0, plane)
-    last = gather(last, 0, plane)
-    bases_grad, query_grad = finish(own, [basis_count, 0], -1)
-    value_grad, key_grad = finish(last, [0, 0], 0)
+    key_grad, done = finish(key, [0], -1)
+    early = join(early, 0, [token, done])
+    bases_grad, query_grad, value_grad, _ = finish(early, [basis_count, 0, 0], basis_count + 1)
     coef_sum = jnp.where(core == 0, dkv_mine, dkv_theirs)[HEAD_DIM + 8 :, :]
     coef_grad = coef_sum[:relations, :basis_count] * scale
     return layer_out, grad_x, query_grad, key_grad, value_grad, bases_grad, coef_grad

time: 139 us -> 136 us (0.978)
  waiting for transfers between devices: 29.6 us -> 28.1 us
  starting transfers between devices: 59.7 us -> 58.3 us
    ppermute x8, waiting for transfers between devices: 10.9 us -> 8.87 us  [swap_nodes(): return lax.ppermute(x, 'nodes', [(i, i ^ 1 << bit) for i in range(nodes)])]
  transfers between devices with their start and end apart: 39 -> 39, of which waited for: 19 -> 16; matrix products, arithmetic and copies ran while one was open for 1% -> 1% of each run, Pallas kernels for 25% -> 27%
where the time goes in v4:
time: 136 us; the launch traced here: 135 us
  starting transfers between devices  58.3 us (43%)
  Pallas kernels  46.6 us (34%)
  waiting for transfers between devices  28.1 us (21%)
  between operations  1.37 us (1%)
    pallas_call x31, Pallas kernels, call(): pl.pallas_call(kernel, out_shape=list(outs) + [pltpu.HBM(x.shape, x.dtype...  42.5 us
    ppermute x21, starting transfers between devices, exchange(): lax.ppermute(x, 'nodes', [(i, i ^ k << first_bit) for i in range(nodes)])  26.6 us
    ppermute x21, waiting for transfers between devices, exchange(): lax.ppermute(x, 'nodes', [(i, i ^ k << first_bit) for i in range(nodes)])  16.6 us
    ppermute x8, starting transfers between devices, swap_nodes(): return lax.ppermute(x, 'nodes', [(i, i ^ 1 << bit) for i in range(nodes)])  16.5 us
    ppermute x8, waiting for transfers between devices, swap_nodes(): return lax.ppermute(x, 'nodes', [(i, i ^ 1 << bit) for i in range(nodes)])  8.87 us
    all_to_all x1, starting transfers between devices, per_device(): lax.all_to_all(outgoing.reshape(nodes, slots, width), 'nodes', split_axis...  8.01 us
    all_to_all x1, starting transfers between devices, run_backward(): lax.all_to_all(sent[0].reshape(nodes, slots, width), 'nodes', split_axis=...  6.02 us
    pallas_call x2, Pallas kernels, finish(): pl.pallas_call(functools.partial(finish_kernel, scale=scale, value_at=val...  4.17 us
  transfers between devices with their start and end apart: 39, of which 16 were waited for; matrix products, arithmetic and copies ran while one was open for 1% of the time, Pallas kernels for 27%

profile of v4, /device:TPU:0, one launch (start us, length us, event | category | flops | bytes accessed | tf_op | source)
XLA Modules:
  0.0 135.5 jit_solution(10946012226014076740)
XLA Ops:
  0.8 5.4 %shard_map.162 = (f32[72,256]{1,0:T(8,128)S(1)}, f32[72,256]{1,0:T(8,128)S(1)}, bf16[512,512]{1,0:T(8,128)(2,1)}, bf16[4,256,512]{2,1,0:T(8,128)(2,1)S(1)}, bf16...) custom-call(s32[8,128]{1,0:T(8,128)S(1)} %broadcast_in_dim.2.refs_0_.refs_1_.place_r, ...), custom_call_target="tpu_custom_call" | custom-call | flops 6049999872 | bytes 4096 | tf_op jit(solution)/shard_map/pallas_call | solution.py:61
  6.8 8.0 %all-to-all-start = ((bf16[16,32,512]{2,1,0:T(8,128)(2,1)}), bf16[16,32,512]{2,1,0:T(8,128)(2,1)S(1)}, u32[]{:S(2)}, u32[]{:S(2)}) async-start(bf16[16,32,512]{2,1,0:T(8,128)(2,1)} %bitcast.12), calls=%async_computation | async-start | bytes 1048576 | tf_op jit(solution)/shard_map/all_to_all | solution.py:561
  17.0 2.6 %shard_map.164 = (f32[1024,512]{1,0:T(8,128)S(1)}, bf16[512,1024]{1,0:T(8,128)(2,1)}) custom-call(s32[8,4]{1,0:T(8,128)S(1)} %copy.18.refs_0_, f32[8,2]{1,0:T(8,128)S(1)} %copy.19.refs_1_, s32[8,4,128]{2,1,0:T(4,128)S(1)} %bitcast.19, s32[8,4,128]{2,1,0:T(4,128)S(1)} %bitcast.24, bf16[4,256,512]{2,1,0:T(8,128)(2,1)S(1)} %get-tuple-element.59.refs_4_.refs_7_, ...), custom_call_target="tpu_custom_call" | custom-call | flops 2310000128 | bytes 1081536 | tf_op jit(solution)/shard_map/pallas_call | solution.py:61
  22.6 2.7 %shard_map.166 = (f32[1024,512]{1,0:T(8,128)S(1)}, bf16[512,1024]{1,0:T(8,128)(2,1)}) custom-call(s32[8,4]{1,0:T(8,128)S(1)} %copy.18.refs_0_, f32[8,2]{1,0:T(8,128)S(1)} %copy.19.refs_1_, s32[8,4,128]{2,1,0:T(4,128)S(1)} %bitcast.20, s32[8,4,128]{2,1,0:T(4,128)S(1)} %bitcast.25, bf16[4,256,512]{2,1,0:T(8,128)(2,1)S(1)} %get-tuple-element.59.refs_4_.refs_7_, ...), custom_call_target="tpu_custom_call" | custom-call | flops 2310000128 | bytes 3178688 | tf_op jit(solution)/shard_map/pallas_call | solution.py:61
  25.6 2.6 %collective-permute-start.3 = (f32[72,256]{1,0:T(8,128)S(1)}, f32[72,256]{1,0:T(8,128)S(1)}, u32[]{:S(2)}, u32[]{:S(2)}) collective-permute-start(f32[72,256]{1,0:T(8,128)S(1)} %shard_map.167.refs_6_.refs_0_), channel_id=1, source_target_pairs={{0,4},{1,5},{2,6},{3,7},{4,0},{5,1},{6,2},{7,3},{8,12},{9,13},{10,... | collective-permute-start | bytes 221192 | tf_op jit(solution)/shard_map/ppermute | solution.py:499
  28.2 2.7 %shard_map.168 = (f32[1024,512]{1,0:T(8,128)S(1)}, bf16[512,1024]{1,0:T(8,128)(2,1)}) custom-call(s32[8,4]{1,0:T(8,128)S(1)} %copy.18.refs_0_, f32[8,2]{1,0:T(8,128)S(1)} %copy.19.refs_1_, s32[8,4,128]{2,1,0:T(4,128)S(1)} %bitcast.21, s32[8,4,128]{2,1,0:T(4,128)S(1)} %bitcast.26, bf16[4,256,512]{2,1,0:T(8,128)(2,1)S(1)} %get-tuple-element.59.refs_4_.refs_7_, ...), custom_call_target="tpu_custom_call" | custom-call | flops 2310000128 | bytes 3178688 | tf_op jit(solution)/shard_map/pallas_call | solution.py:61
  30.9 2.4 %collective-permute-start.4 = (f32[72,256]{1,0:T(8,128)S(1)}, f32[72,256]{1,0:T(8,128)S(1)}, u32[]{:S(2)}, u32[]{:S(2)}) collective-permute-start(f32[72,256]{1,0:T(8,128)S(1)} %shard_map.169.refs_6_.refs_0_), channel_id=1, source_target_pairs={{0,8},{1,9},{2,10},{3,11},{4,12},{5,13},{6,14},{7,15},{8,0},{9,1},... | collective-permute-start | bytes 221192 | tf_op jit(solution)/shard_map/ppermute | solution.py:499
  33.3 3.5 %shard_map.170 = (f32[1024,512]{1,0:T(8,128)S(1)}, bf16[512,512]{1,0:T(8,128)(2,1)}, bf16[512,1024]{1,0:T(8,128)(2,1)}) custom-call(s32[8,4]{1,0:T(8,128)S(1)} %copy.18.refs_0_, f32[8,2]{1,0:T(8,128)S(1)} %copy.19.refs_1_, s32[8,4,128]{2,1,0:T(4,128)S(1)} %bitcast.22, s32[8,4,128]{2,1,0:T(4,128)S(1)} %bitcast.27, bf16[4,256,512]{2,1,0:T(8,128)(2,1)S(1)} %copy-done.9, ...), custom_call_target="tpu_custom_call" | custom-call | flops 2310000128 | bytes 3178688 | tf_op jit(solution)/shard_map/pallas_call | solution.py:61
  37.0 6.0 %all-to-all-start.1 = ((bf16[16,32,512]{2,1,0:T(8,128)(2,1)}), bf16[16,32,512]{2,1,0:T(8,128)(2,1)S(1)}, u32[]{:S(2)}, u32[]{:S(2)}) async-start(bf16[16,32,512]{2,1,0:T(8,128)(2,1)} %bitcast.14), calls=%async_computation.1 | async-start | bytes 1048576 | tf_op jit(solution)/shard_map/all_to_all | solution.py:580
  43.0 12.6 %shard_map.172 = (f32[512,512]{1,0:T(8,128)S(1)}, f32[8,128]{1,0:T(8,128)S(1)}, f32[256,1024]{1,0:T(8,128)S(1)}, bf16[256,1024]{1,0:T(8,128)(2,1)S(1)}) custom-call(s32[8,4]{1,0:T(8,128)S(1)} %copy.18.refs_0_, s32[8,128]{1,0:T(8,128)S(1)} %broadcast_in_dim.2.refs_0_.refs_1_.place_ref, s32[8,4,128]{2,1,0:T(4,128)S(1)} %bitcast.23, s32[8,4,128]{2,1,0:T(4,128)S(1)} %bitcast.28, ...), custom_call_target="tpu_custom_call" | custom-call | flops 9900000256 | bytes 36992 | tf_op jit(solution)/shard_map/pallas_call | solution.py:61
  55.7 3.0 %shard_map.173 = (f32[80,256]{1,0:T(8,128)S(1)}, f32[80,256]{1,0:T(8,128)S(1)}, bf16[512,512]{1,0:T(8,128)(2,1)S(1)}, f32[512,512]{1,0:T(8,128)}) custom-call(s32[8,128]{1,0:T(8,128)S(1)} %broadcast_in_dim.2.refs_0_.refs_1_.place_ref, f32[512,512]{1,0:T(8,128)S(1)} %copy-done.12, f32[512,512]{1,0:T(8,128)S(1)} %copy-done.3, ...), custom_call_target="tpu_custom_call" | custom-call | flops 2969999872 | bytes 3301376 | tf_op jit(solution)/shard_map/pallas_call | solution.py:61
  61.9 2.1 %shard_map.176 = (f32[256,1024]{1,0:T(8,128)S(1)}, bf16[256,2048]{1,0:T(8,128)(2,1)S(1)}) custom-call(s32[8,128]{1,0:T(8,128)S(1)} %broadcast_in_dim.2.refs_0_.refs_1_.place_ref, bf16[512,512]{1,0:T(8,128)(2,1)S(1)} %get-tuple-element.73.refs_1_, f32[512,512]{1,0:T(8,128)S(1)} %copy-done.6, bf16[256,1024]{1,0:T(8,128)(2,1)S(1)} %copy-done.11, ...), custom_call_target="tpu_custom_call" | custom-call | flops 1980000000 | bytes 2101248 | tf_op jit(solution)/shard_map/pallas_call | solution.py:61
  66.7 3.1 %collective-permute-done.8.refs_1_ = f32[80,256]{1,0:T(8,128)S(1)} collective-permute-done((f32[80,256]{1,0:T(8,128)S(1)}, f32[80,256]{1,0:T(8,128)S(1)}, u32[]{:S(2)}, u32[]{:S(2)}) %collective-permute-start.8) | collective-permute-done | bytes 81952 | tf_op jit(solution)/shard_map/ppermute | solution.py:499
  76.0 2.4 %collective-permute-start.11 = (f32[80,256]{1,0:T(8,128)S(1)}, f32[80,256]{1,0:T(8,128)S(1)}, u32[]{:S(2)}, u32[]{:S(2)}) collective-permute-start(f32[80,256]{1,0:T(8,128)S(1)} %shard_map.181.refs_0_), channel_id=1, source_target_pairs={{0,8},{1,9},{2,10},{3,11},{4,12},{5,13},{6,14},{7,15},{8,0},{9,1},... | collective-permute-start | bytes 245768 | tf_op jit(solution)/shard_map/ppermute | solution.py:499
  78.4 3.6 %collective-permute-done.11.refs_1_ = f32[80,256]{1,0:T(8,128)S(1)} collective-permute-done((f32[80,256]{1,0:T(8,128)S(1)}, f32[80,256]{1,0:T(8,128)S(1)}, u32[]{:S(2)}, u32[]{:S(2)}) %collective-permute-start.11) | collective-permute-done | bytes 81952 | tf_op jit(solution)/shard_map/ppermute | solution.py:499
  82.1 4.8 %collective-permute-done.14.refs_3_ = bf16[64,2048]{1,0:T(8,128)(2,1)S(1)} collective-permute-done((bf16[64,2048]{1,0:T(8,128)(2,1)S(1)}, bf16[64,2048]{1,0:T(8,128)(2,1)S(1)}, u32[]{:S(2)}, u32[]{:S(2)}) %collective-permute-start.14) | collective-permute-done | bytes 262176 | tf_op jit(solution)/shard_map/ppermute | solution.py:519
  89.4 2.4 %collective-permute-start.21 = (bf16[16,2048]{1,0:T(8,128)(2,1)S(1)}, bf16[16,2048]{1,0:T(8,128)(2,1)S(1)}, u32[]{:S(2)}, u32[]{:S(2)}) collective-permute-start(bf16[16,2048]{1,0:T(8,128)(2,1)S(1)} %get-tuple-element.96), channel_id=1, source_target_pairs={{0,8},{1,9},{2,10},{3,11},{4,12},{5,13},{6,14},{7,15},{8,0},{9,1},... | collective-permute-start | bytes 196616 | tf_op jit(solution)/shard_map/ppermute | solution.py:519
  100.7 2.4 %collective-permute-start.25 = (bf16[64,512]{1,0:T(8,128)(2,1)S(1)}, bf16[64,512]{1,0:T(8,128)(2,1)S(1)}, u32[]{:S(2)}, u32[]{:S(2)}) collective-permute-start(bf16[64,512]{1,0:T(8,128)(2,1)S(1)} %shard_map.187.refs_0_.refs_5_), channel_id=1, source_target_pairs={{0,12},{1,13},{2,14},{3,15},{4,8},{5,9},{6,10},{7,11},{8,4},{9,5},... | collective-permute-start | bytes 196616 | tf_op jit(solution)/shard_map/ppermute | solution.py:519
  105.2 2.4 %collective-permute-start.31 = (bf16[16,2048]{1,0:T(8,128)(2,1)S(1)}, bf16[16,2048]{1,0:T(8,128)(2,1)S(1)}, u32[]{:S(2)}, u32[]{:S(2)}) collective-permute-start(bf16[16,2048]{1,0:T(8,128)(2,1)S(1)} %shard_map.186.refs_4_.refs_1_), channel_id=1, source_target_pairs={{0,12},{1,13},{2,14},{3,15},{4,8},{5,9},{6,10},{7,11},{8,4},{9,5},... | collective-permute-start | bytes 196616 | tf_op jit(solution)/shard_map/ppermute | solution.py:519
  109.5 3.0 %collective-permute-done.24.refs_2_ = bf16[64,512]{1,0:T(8,128)(2,1)S(1)} collective-permute-done((bf16[64,512]{1,0:T(8,128)(2,1)S(1)}, bf16[64,512]{1,0:T(8,128)(2,1)S(1)}, u32[]{:S(2)}, u32[]{:S(2)}) %collective-permute-start.24) | collective-permute-done | bytes 65568 | tf_op jit(solution)/shard_map/ppermute | solution.py:519
  113.9 2.2 %collective-permute-start.26 = (bf16[64,512]{1,0:T(8,128)(2,1)S(1)}, bf16[64,512]{1,0:T(8,128)(2,1)S(1)}, u32[]{:S(2)}, u32[]{:S(2)}) collective-permute-start(bf16[64,512]{1,0:T(8,128)(2,1)S(1)} %shard_map.188.refs_1_), channel_id=1, source_target_pairs={{0,1},{1,0},{2,3},{3,2},{4,5},{5,4},{6,7},{7,6},{8,9},{9,8},{10,11... | collective-permute-start | bytes 196616 | tf_op jit(solution)/shard_map/ppermute | solution.py:519
  119.8 2.7 %collective-permute-done.27.refs_3_ = bf16[64,512]{1,0:T(8,128)(2,1)S(1)} collective-permute-done((bf16[64,512]{1,0:T(8,128)(2,1)S(1)}, bf16[64,512]{1,0:T(8,128)(2,1)S(1)}, u32[]{:S(2)}, u32[]{:S(2)}) %collective-permute-start.27) | collective-permute-done | bytes 65568 | tf_op jit(solution)/shard_map/ppermute | solution.py:519
  122.6 3.8 %shard_map.191 = (f32[512,512]{1,0:T(8,128)}, f32[8,128]{1,0:T(8,128)S(1)}) custom-call(s32[8,128]{1,0:T(8,128)S(1)} %broadcast_in_dim.2.refs_0_.refs_1_.place_ref, bf16[512,512]{1,0:T(8,128)(2,1)S(1)} %get-tuple-element.73.refs_1_, bf16[512,512]{1,0:T(8,128)(2,1)S(1)} %get-tuple-element.88.refs_2_, f32[512,512]{1,0:T(8,128)S(1)} %copy-done.6, ...), custom_call_target="tpu_custom_call" | custom-call | flops 3849999872 | bytes 3313664 | tf_op jit(solution)/shard_map/pallas_call | solution.py:61
  132.3 3.0 %shard_map.194 = (f32[2,512,512]{2,1,0:T(8,128)}, f32[512,512]{1,0:T(8,128)}, f32[512,512]{1,0:T(8,128)}, f32[8,128]{1,0:T(8,128)}) custom-call(s32[8,128]{1,0:T(8,128)S(1)} %broadcast_in_dim.2.refs_0_.refs_1_.place_ref, f32[80,256]{1,0:T(8,128)S(1)} %shard_map.182.refs_5_.refs_3_.refs_4_.sum_mine_ref, ...), custom_call_target="tpu_custom_call" | custom-call | flops 3200000000 | tf_op jit(solution)/shard_map/pallas_call | solution.py:644
  (127 shorter events, 44.6 us)
Async XLA Ops:
  6.3 8.7 %collective-permute-start = (f32[72,256]{1,0:T(8,128)S(1)}, f32[72,256]{1,0:T(8,128)S(1)}, u32[]{:S(2)}, u32[]{:S(2)}) collective-permute-start(f32[72,256]{1,0:T(8,128)S(1)} %get-tuple-element.58), channel_id=1, source_target_pairs={{0,16},{16,0},{1,17},{17,1},{2,18},{18,2},{3,19},{19,3},{4,20},{20... | collective-permute-start | bytes 221192 | tf_op jit(solution)/shard_map/ppermute | solution.py:494
  6.8 30.1 %all-to-all-start = ((bf16[16,32,512]{2,1,0:T(8,128)(2,1)}), bf16[16,32,512]{2,1,0:T(8,128)(2,1)S(1)}, u32[]{:S(2)}, u32[]{:S(2)}) async-start(bf16[16,32,512]{2,1,0:T(8,128)(2,1)} %bitcast.12), calls=%async_computation | async-start | bytes 1048576 | tf_op jit(solution)/shard_map/all_to_all | solution.py:561
  36.9 18.8 %collective-permute-start.5 = (f32[72,256]{1,0:T(8,128)S(1)}, f32[72,256]{1,0:T(8,128)S(1)}, u32[]{:S(2)}, u32[]{:S(2)}) collective-permute-start(f32[72,256]{1,0:T(8,128)S(1)} %shard_map.171.refs_4_.refs_3_), channel_id=1, source_target_pairs={{0,16},{16,0},{1,17},{17,1},{2,18},{18,2},{3,19},{19,3},{4,20},{20... | collective-permute-start | bytes 221192 | tf_op jit(solution)/shard_map/ppermute | solution.py:494
  37.0 22.1 %all-to-all-start.1 = ((bf16[16,32,512]{2,1,0:T(8,128)(2,1)}), bf16[16,32,512]{2,1,0:T(8,128)(2,1)S(1)}, u32[]{:S(2)}, u32[]{:S(2)}) async-start(bf16[16,32,512]{2,1,0:T(8,128)(2,1)} %bitcast.14), calls=%async_computation.1 | async-start | bytes 1048576 | tf_op jit(solution)/shard_map/all_to_all | solution.py:580
  64.8 6.7 %collective-permute-start.10 = (bf16[256,2048]{1,0:T(8,128)(2,1)S(1)}, bf16[256,2048]{1,0:T(8,128)(2,1)S(1)}, u32[]{:S(2)}, u32[]{:S(2)}) collective-permute-start(bf16[256,2048]{1,0:T(8,128)(2,1)S(1)} %shard_map.178.refs_2_), channel_id=1, source_target_pairs={{0,16},{16,0},{1,17},{17,1},{2,18},{18,2},{3,19},{19,3},{4,20},{20... | collective-permute-start | bytes 3145736 | tf_op jit(solution)/shard_map/ppermute | solution.py:494
  69.8 6.2 %collective-permute-start.9 = (f32[80,256]{1,0:T(8,128)S(1)}, f32[80,256]{1,0:T(8,128)S(1)}, u32[]{:S(2)}, u32[]{:S(2)}) collective-permute-start(f32[80,256]{1,0:T(8,128)S(1)} %shard_map.179.refs_4_.refs_0_), channel_id=1, source_target_pairs={{0,4},{1,5},{2,6},{3,7},{4,0},{5,1},{6,2},{7,3},{8,12},{9,13},{10,... | collective-permute-start | bytes 245768 | tf_op jit(solution)/shard_map/ppermute | solution.py:499
  72.4 9.7 %collective-permute-start.13 = (bf16[64,2048]{1,0:T(8,128)(2,1)S(1)}, bf16[64,2048]{1,0:T(8,128)(2,1)S(1)}, u32[]{:S(2)}, u32[]{:S(2)}) collective-permute-start(bf16[64,2048]{1,0:T(8,128)(2,1)S(1)} %get-tuple-element.84), channel_id=1, source_target_pairs={{0,1},{1,0},{2,3},{3,2},{4,5},{5,4},{6,7},{7,6},{8,9},{9,8},{10,11... | collective-permute-start | bytes 786440 | tf_op jit(solution)/shard_map/ppermute | solution.py:519
  74.0 12.9 %collective-permute-start.14 = (bf16[64,2048]{1,0:T(8,128)(2,1)S(1)}, bf16[64,2048]{1,0:T(8,128)(2,1)S(1)}, u32[]{:S(2)}, u32[]{:S(2)}) collective-permute-start(bf16[64,2048]{1,0:T(8,128)(2,1)S(1)} %get-tuple-element.85), channel_id=1, source_target_pairs={{0,2},{1,3},{2,0},{3,1},{4,6},{5,7},{6,4},{7,5},{8,10},{9,11},{10,... | collective-permute-start | bytes 786440 | tf_op jit(solution)/shard_map/ppermute | solution.py:519
  75.4 11.5 %collective-permute-start.15 = (bf16[64,2048]{1,0:T(8,128)(2,1)S(1)}, bf16[64,2048]{1,0:T(8,128)(2,1)S(1)}, u32[]{:S(2)}, u32[]{:S(2)}) collective-permute-start(bf16[64,2048]{1,0:T(8,128)(2,1)S(1)} %get-tuple-element.86), channel_id=1, source_target_pairs={{0,3},{1,2},{2,1},{3,0},{4,7},{5,6},{6,5},{7,4},{8,11},{9,10},{10,... | collective-permute-start | bytes 786440 | tf_op jit(solution)/shard_map/ppermute | solution.py:519
  76.0 6.0 %collective-permute-start.11 = (f32[80,256]{1,0:T(8,128)S(1)}, f32[80,256]{1,0:T(8,128)S(1)}, u32[]{:S(2)}, u32[]{:S(2)}) collective-permute-start(f32[80,256]{1,0:T(8,128)S(1)} %shard_map.181.refs_0_), channel_id=1, source_target_pairs={{0,8},{1,9},{2,10},{3,11},{4,12},{5,13},{6,14},{7,15},{8,0},{9,1},... | collective-permute-start | bytes 245768 | tf_op jit(solution)/shard_map/ppermute | solution.py:499
  88.8 6.7 %collective-permute-start.20 = (bf16[16,2048]{1,0:T(8,128)(2,1)S(1)}, bf16[16,2048]{1,0:T(8,128)(2,1)S(1)}, u32[]{:S(2)}, u32[]{:S(2)}) collective-permute-start(bf16[16,2048]{1,0:T(8,128)(2,1)S(1)} %get-tuple-element.95), channel_id=1, source_target_pairs={{0,4},{1,5},{2,6},{3,7},{4,0},{5,1},{6,2},{7,3},{8,12},{9,13},{10,... | collective-permute-start | bytes 196616 | tf_op jit(solution)/shard_map/ppermute | solution.py:519
  89.4 7.6 %collective-permute-start.21 = (bf16[16,2048]{1,0:T(8,128)(2,1)S(1)}, bf16[16,2048]{1,0:T(8,128)(2,1)S(1)}, u32[]{:S(2)}, u32[]{:S(2)}) collective-permute-start(bf16[16,2048]{1,0:T(8,128)(2,1)S(1)} %get-tuple-element.96), channel_id=1, source_target_pairs={{0,8},{1,9},{2,10},{3,11},{4,12},{5,13},{6,14},{7,15},{8,0},{9,1},... | collective-permute-start | bytes 196616 | tf_op jit(solution)/shard_map/ppermute | solution.py:519
  91.8 6.2 %collective-permute-start.22 = (bf16[16,2048]{1,0:T(8,128)(2,1)S(1)}, bf16[16,2048]{1,0:T(8,128)(2,1)S(1)}, u32[]{:S(2)}, u32[]{:S(2)}) collective-permute-start(bf16[16,2048]{1,0:T(8,128)(2,1)S(1)} %get-tuple-element.97), channel_id=1, source_target_pairs={{0,12},{1,13},{2,14},{3,15},{4,8},{5,9},{6,10},{7,11},{8,4},{9,5},... | collective-permute-start | bytes 196616 | tf_op jit(solution)/shard_map/ppermute | solution.py:519
  100.7 6.9 %collective-permute-start.25 = (bf16[64,512]{1,0:T(8,128)(2,1)S(1)}, bf16[64,512]{1,0:T(8,128)(2,1)S(1)}, u32[]{:S(2)}, u32[]{:S(2)}) collective-permute-start(bf16[64,512]{1,0:T(8,128)(2,1)S(1)} %shard_map.187.refs_0_.refs_5_), channel_id=1, source_target_pairs={{0,12},{1,13},{2,14},{3,15},{4,8},{5,9},{6,10},{7,11},{8,4},{9,5},... | collective-permute-start | bytes 196616 | tf_op jit(solution)/shard_map/ppermute | solution.py:519
  103.1 9.4 %collective-permute-start.24 = (bf16[64,512]{1,0:T(8,128)(2,1)S(1)}, bf16[64,512]{1,0:T(8,128)(2,1)S(1)}, u32[]{:S(2)}, u32[]{:S(2)}) collective-permute-start(bf16[64,512]{1,0:T(8,128)(2,1)S(1)} %shard_map.187.refs_0_.refs_5_), channel_id=1, source_target_pairs={{0,8},{1,9},{2,10},{3,11},{4,12},{5,13},{6,14},{7,15},{8,0},{9,1},... | collective-permute-start | bytes 196616 | tf_op jit(solution)/shard_map/ppermute | solution.py:519
  103.1 9.4 %collective-permute-start.23 = (bf16[64,512]{1,0:T(8,128)(2,1)S(1)}, bf16[64,512]{1,0:T(8,128)(2,1)S(1)}, u32[]{:S(2)}, u32[]{:S(2)}) collective-permute-start(bf16[64,512]{1,0:T(8,128)(2,1)S(1)} %shard_map.187.refs_0_.refs_5_), channel_id=1, source_target_pairs={{0,4},{1,5},{2,6},{3,7},{4,0},{5,1},{6,2},{7,3},{8,12},{9,13},{10,... | collective-permute-start | bytes 196616 | tf_op jit(solution)/shard_map/ppermute | solution.py:519
  105.2 8.8 %collective-permute-start.31 = (bf16[16,2048]{1,0:T(8,128)(2,1)S(1)}, bf16[16,2048]{1,0:T(8,128)(2,1)S(1)}, u32[]{:S(2)}, u32[]{:S(2)}) collective-permute-start(bf16[16,2048]{1,0:T(8,128)(2,1)S(1)} %shard_map.186.refs_4_.refs_1_), channel_id=1, source_target_pairs={{0,12},{1,13},{2,14},{3,15},{4,8},{5,9},{6,10},{7,11},{8,4},{9,5},... | collective-permute-start | bytes 196616 | tf_op jit(solution)/shard_map/ppermute | solution.py:519
  107.5 8.7 %collective-permute-start.30 = (bf16[16,2048]{1,0:T(8,128)(2,1)S(1)}, bf16[16,2048]{1,0:T(8,128)(2,1)S(1)}, u32[]{:S(2)}, u32[]{:S(2)}) collective-permute-start(bf16[16,2048]{1,0:T(8,128)(2,1)S(1)} %shard_map.186.refs_4_.refs_1_), channel_id=1, source_target_pairs={{0,8},{1,9},{2,10},{3,11},{4,12},{5,13},{6,14},{7,15},{8,0},{9,1},... | collective-permute-start | bytes 196616 | tf_op jit(solution)/shard_map/ppermute | solution.py:519
  107.6 8.5 %collective-permute-start.29 = (bf16[16,2048]{1,0:T(8,128)(2,1)S(1)}, bf16[16,2048]{1,0:T(8,128)(2,1)S(1)}, u32[]{:S(2)}, u32[]{:S(2)}) collective-permute-start(bf16[16,2048]{1,0:T(8,128)(2,1)S(1)} %shard_map.186.refs_4_.refs_1_), channel_id=1, source_target_pairs={{0,4},{1,5},{2,6},{3,7},{4,0},{5,1},{6,2},{7,3},{8,12},{9,13},{10,... | collective-permute-start | bytes 196616 | tf_op jit(solution)/shard_map/ppermute | solution.py:519
  113.9 8.5 %collective-permute-start.27 = (bf16[64,512]{1,0:T(8,128)(2,1)S(1)}, bf16[64,512]{1,0:T(8,128)(2,1)S(1)}, u32[]{:S(2)}, u32[]{:S(2)}) collective-permute-start(bf16[64,512]{1,0:T(8,128)(2,1)S(1)} %shard_map.188.refs_1_), channel_id=1, source_target_pairs={{0,2},{1,3},{2,0},{3,1},{4,6},{5,7},{6,4},{7,5},{8,10},{9,11},{10,... | collective-permute-start | bytes 196616 | tf_op jit(solution)/shard_map/ppermute | solution.py:519
  113.9 8.5 %collective-permute-start.26 = (bf16[64,512]{1,0:T(8,128)(2,1)S(1)}, bf16[64,512]{1,0:T(8,128)(2,1)S(1)}, u32[]{:S(2)}, u32[]{:S(2)}) collective-permute-start(bf16[64,512]{1,0:T(8,128)(2,1)S(1)} %shard_map.188.refs_1_), channel_id=1, source_target_pairs={{0,1},{1,0},{2,3},{3,2},{4,5},{5,4},{6,7},{7,6},{8,9},{9,8},{10,11... | collective-permute-start | bytes 196616 | tf_op jit(solution)/shard_map/ppermute | solution.py:519
  116.3 11.4 %collective-permute-start.34 = (bf16[64,2048]{1,0:T(8,128)(2,1)S(1)}, bf16[64,2048]{1,0:T(8,128)(2,1)S(1)}, u32[]{:S(2)}, u32[]{:S(2)}) collective-permute-start(bf16[64,2048]{1,0:T(8,128)(2,1)S(1)} %shard_map.189.refs_5_.refs_1_), channel_id=1, source_target_pairs={{0,3},{1,2},{2,1},{3,0},{4,7},{5,6},{6,5},{7,4},{8,11},{9,10},{10,... | collective-permute-start | bytes 786440 | tf_op jit(solution)/shard_map/ppermute | solution.py:519
  117.6 11.7 %collective-permute-start.33 = (bf16[64,2048]{1,0:T(8,128)(2,1)S(1)}, bf16[64,2048]{1,0:T(8,128)(2,1)S(1)}, u32[]{:S(2)}, u32[]{:S(2)}) collective-permute-start(bf16[64,2048]{1,0:T(8,128)(2,1)S(1)} %shard_map.189.refs_5_.refs_1_), channel_id=1, source_target_pairs={{0,2},{1,3},{2,0},{3,1},{4,6},{5,7},{6,4},{7,5},{8,10},{9,11},{10,... | collective-permute-start | bytes 786440 | tf_op jit(solution)/shard_map/ppermute | solution.py:519
  118.6 10.7 %collective-permute-start.32 = (bf16[64,2048]{1,0:T(8,128)(2,1)S(1)}, bf16[64,2048]{1,0:T(8,128)(2,1)S(1)}, u32[]{:S(2)}, u32[]{:S(2)}) collective-permute-start(bf16[64,2048]{1,0:T(8,128)(2,1)S(1)} %shard_map.189.refs_5_.refs_1_), channel_id=1, source_target_pairs={{0,1},{1,0},{2,3},{3,2},{4,5},{5,4},{6,7},{7,6},{8,9},{9,8},{10,11... | collective-permute-start | bytes 786440 | tf_op jit(solution)/shard_map/ppermute | solution.py:519
  (32 other events, 225.1 us)

commit v5 on v4

--- a/solution.py
+++ b/solution.py
@@ -66,7 +66,7 @@
         scratch_shapes=scratches + ([pltpu.SemaphoreType.DMA((sems,))] if sems else []),
         compiler_params=pltpu.CompilerParams(vmem_limit_bytes=megabytes * 1024 * 1024),
         cost_estimate=pl.CostEstimate(
-            flops=int(us * 1.1e9),
+            flops=int(us * 1.5e9),
             bytes_accessed=sum(x.size * x.dtype.itemsize for x in arrays),
             transcendentals=0,
         ),
@@ -242,11 +242,11 @@
         kv = block_diagonal(kv)
         query = eq_ref[:, at]
         cot = cot_ref[:, at]
-        inverse = 1.0 / mm_exact_right(query * ks, same_head)
-        attended = mm_wide(query, kv) * inverse
+        normalizer = mm_exact_right(query * ks, same_head)
+        attended = mm_wide(query, kv) / normalizer
         layer_ref[:, at] = attended + conv_ref[:, at]
-        num_grad = cot * inverse
-        den_grad = -mm_exact_right(cot * attended, same_head) * inverse
+        num_grad = cot / normalizer
+        den_grad = -mm_exact_right(cot * attended, same_head) / normalizer
         packed.append(pack_diagonal(mm_wide(query, num_grad, TN)))
         sums.append(jnp.sum(query * den_grad, axis=0, keepdims=True))
         query_side = mm_wide(num_grad, kv, NT) + den_grad * ks

time: 136 us -> 136 us (level)
  transfers between devices with their start and end apart: 39 -> 39, of which waited for: 16 -> 15; matrix products, arithmetic and copies ran while one was open for 1% -> 1% of each run, Pallas kernels for 27% -> 27%
where the time goes in v5:
time: 136 us; the launch traced here: 135 us
  starting transfers between devices  58.4 us (43%)
  Pallas kernels  46.7 us (34%)
  waiting for transfers between devices  28 us (21%)
  between operations  1.37 us (1%)
    pallas_call x31, Pallas kernels, call(): pl.pallas_call(kernel, out_shape=list(outs) + [pltpu.HBM(x.shape, x.dtype...  42.5 us
    ppermute x21, starting transfers between devices, exchange(): lax.ppermute(x, 'nodes', [(i, i ^ k << first_bit) for i in range(nodes)])  26.7 us
    ppermute x21, waiting for transfers between devices, exchange(): lax.ppermute(x, 'nodes', [(i, i ^ k << first_bit) for i in range(nodes)])  16.5 us
    ppermute x8, starting transfers between devices, swap_nodes(): return lax.ppermute(x, 'nodes', [(i, i ^ 1 << bit) for i in range(nodes)])  16.4 us
    ppermute x8, waiting for transfers between devices, swap_nodes(): return lax.ppermute(x, 'nodes', [(i, i ^ 1 << bit) for i in range(nodes)])  8.91 us
    all_to_all x1, starting transfers between devices, per_device(): lax.all_to_all(outgoing.reshape(nodes, slots, width), 'nodes', split_axis...  8.01 us
    all_to_all x1, starting transfers between devices, run_backward(): lax.all_to_all(sent[0].reshape(nodes, slots, width), 'nodes', split_axis=...  6.02 us
    pallas_call x2, Pallas kernels, finish(): pl.pallas_call(functools.partial(finish_kernel, scale=scale, value_at=val...  4.17 us
  transfers between devices with their start and end apart: 39, of which 15 were waited for; matrix products, arithmetic and copies ran while one was open for 1% of the time, Pallas kernels for 27%

profile of v5, /device:TPU:0, one launch (start us, length us, event | category | flops | bytes accessed | tf_op | source)
XLA Modules:
  0.0 135.5 jit_solution(4201953828782521843)
XLA Ops:
  0.8 5.4 %shard_map.162 = (f32[72,256]{1,0:T(8,128)S(1)}, f32[72,256]{1,0:T(8,128)S(1)}, bf16[512,512]{1,0:T(8,128)(2,1)}, bf16[4,256,512]{2,1,0:T(8,128)(2,1)S(1)}, bf16...) custom-call(s32[8,128]{1,0:T(8,128)S(1)} %broadcast_in_dim.2.refs_0_.refs_1_.place_r, ...), custom_call_target="tpu_custom_call" | custom-call | flops 8249999872 | bytes 4096 | tf_op jit(solution)/shard_map/pallas_call | solution.py:61
  6.8 8.0 %all-to-all-start = ((bf16[16,32,512]{2,1,0:T(8,128)(2,1)}), bf16[16,32,512]{2,1,0:T(8,128)(2,1)S(1)}, u32[]{:S(2)}, u32[]{:S(2)}) async-start(bf16[16,32,512]{2,1,0:T(8,128)(2,1)} %bitcast.12), calls=%async_computation | async-start | bytes 1048576 | tf_op jit(solution)/shard_map/all_to_all | solution.py:561
  17.0 2.6 %shard_map.164 = (f32[1024,512]{1,0:T(8,128)S(1)}, bf16[512,1024]{1,0:T(8,128)(2,1)}) custom-call(s32[8,4]{1,0:T(8,128)S(1)} %copy.18.refs_0_, f32[8,2]{1,0:T(8,128)S(1)} %copy.19.refs_1_, s32[8,4,128]{2,1,0:T(4,128)S(1)} %bitcast.19, s32[8,4,128]{2,1,0:T(4,128)S(1)} %bitcast.24, bf16[4,256,512]{2,1,0:T(8,128)(2,1)S(1)} %get-tuple-element.59.refs_4_.refs_7_, ...), custom_call_target="tpu_custom_call" | custom-call | flops 3150000128 | bytes 1081536 | tf_op jit(solution)/shard_map/pallas_call | solution.py:61
  22.6 2.7 %shard_map.166 = (f32[1024,512]{1,0:T(8,128)S(1)}, bf16[512,1024]{1,0:T(8,128)(2,1)}) custom-call(s32[8,4]{1,0:T(8,128)S(1)} %copy.18.refs_0_, f32[8,2]{1,0:T(8,128)S(1)} %copy.19.refs_1_, s32[8,4,128]{2,1,0:T(4,128)S(1)} %bitcast.20, s32[8,4,128]{2,1,0:T(4,128)S(1)} %bitcast.25, bf16[4,256,512]{2,1,0:T(8,128)(2,1)S(1)} %get-tuple-element.59.refs_4_.refs_7_, ...), custom_call_target="tpu_custom_call" | custom-call | flops 3150000128 | bytes 3178688 | tf_op jit(solution)/shard_map/pallas_call | solution.py:61
  25.6 2.6 %collective-permute-start.3 = (f32[72,256]{1,0:T(8,128)S(1)}, f32[72,256]{1,0:T(8,128)S(1)}, u32[]{:S(2)}, u32[]{:S(2)}) collective-permute-start(f32[72,256]{1,0:T(8,128)S(1)} %shard_map.167.refs_6_.refs_0_), channel_id=1, source_target_pairs={{0,4},{1,5},{2,6},{3,7},{4,0},{5,1},{6,2},{7,3},{8,12},{9,13},{10,... | collective-permute-start | bytes 221192 | tf_op jit(solution)/shard_map/ppermute | solution.py:499
  28.2 2.7 %shard_map.168 = (f32[1024,512]{1,0:T(8,128)S(1)}, bf16[512,1024]{1,0:T(8,128)(2,1)}) custom-call(s32[8,4]{1,0:T(8,128)S(1)} %copy.18.refs_0_, f32[8,2]{1,0:T(8,128)S(1)} %copy.19.refs_1_, s32[8,4,128]{2,1,0:T(4,128)S(1)} %bitcast.21, s32[8,4,128]{2,1,0:T(4,128)S(1)} %bitcast.26, bf16[4,256,512]{2,1,0:T(8,128)(2,1)S(1)} %get-tuple-element.59.refs_4_.refs_7_, ...), custom_call_target="tpu_custom_call" | custom-call | flops 3150000128 | bytes 3178688 | tf_op jit(solution)/shard_map/pallas_call | solution.py:61
  30.9 2.4 %collective-permute-start.4 = (f32[72,256]{1,0:T(8,128)S(1)}, f32[72,256]{1,0:T(8,128)S(1)}, u32[]{:S(2)}, u32[]{:S(2)}) collective-permute-start(f32[72,256]{1,0:T(8,128)S(1)} %shard_map.169.refs_6_.refs_0_), channel_id=1, source_target_pairs={{0,8},{1,9},{2,10},{3,11},{4,12},{5,13},{6,14},{7,15},{8,0},{9,1},... | collective-permute-start | bytes 221192 | tf_op jit(solution)/shard_map/ppermute | solution.py:499
  33.3 3.5 %shard_map.170 = (f32[1024,512]{1,0:T(8,128)S(1)}, bf16[512,512]{1,0:T(8,128)(2,1)}, bf16[512,1024]{1,0:T(8,128)(2,1)}) custom-call(s32[8,4]{1,0:T(8,128)S(1)} %copy.18.refs_0_, f32[8,2]{1,0:T(8,128)S(1)} %copy.19.refs_1_, s32[8,4,128]{2,1,0:T(4,128)S(1)} %bitcast.22, s32[8,4,128]{2,1,0:T(4,128)S(1)} %bitcast.27, bf16[4,256,512]{2,1,0:T(8,128)(2,1)S(1)} %copy-done.9, ...), custom_call_target="tpu_custom_call" | custom-call | flops 3150000128 | bytes 3178688 | tf_op jit(solution)/shard_map/pallas_call | solution.py:61
  37.0 6.0 %all-to-all-start.1 = ((bf16[16,32,512]{2,1,0:T(8,128)(2,1)}), bf16[16,32,512]{2,1,0:T(8,128)(2,1)S(1)}, u32[]{:S(2)}, u32[]{:S(2)}) async-start(bf16[16,32,512]{2,1,0:T(8,128)(2,1)} %bitcast.14), calls=%async_computation.1 | async-start | bytes 1048576 | tf_op jit(solution)/shard_map/all_to_all | solution.py:580
  43.0 12.6 %shard_map.172 = (f32[512,512]{1,0:T(8,128)S(1)}, f32[8,128]{1,0:T(8,128)S(1)}, f32[256,1024]{1,0:T(8,128)S(1)}, bf16[256,1024]{1,0:T(8,128)(2,1)S(1)}) custom-call(s32[8,4]{1,0:T(8,128)S(1)} %copy.18.refs_0_, s32[8,128]{1,0:T(8,128)S(1)} %broadcast_in_dim.2.refs_0_.refs_1_.place_ref, s32[8,4,128]{2,1,0:T(4,128)S(1)} %bitcast.23, s32[8,4,128]{2,1,0:T(4,128)S(1)} %bitcast.28, ...), custom_call_target="tpu_custom_call" | custom-call | flops 13500000256 | bytes 36992 | tf_op jit(solution)/shard_map/pallas_call | solution.py:61
  55.7 3.0 %shard_map.173 = (f32[80,256]{1,0:T(8,128)S(1)}, f32[80,256]{1,0:T(8,128)S(1)}, bf16[512,512]{1,0:T(8,128)(2,1)S(1)}, f32[512,512]{1,0:T(8,128)}) custom-call(s32[8,128]{1,0:T(8,128)S(1)} %broadcast_in_dim.2.refs_0_.refs_1_.place_ref, f32[512,512]{1,0:T(8,128)S(1)} %copy-done.12, f32[512,512]{1,0:T(8,128)S(1)} %copy-done.3, ...), custom_call_target="tpu_custom_call" | custom-call | flops 4049999872 | bytes 3301376 | tf_op jit(solution)/shard_map/pallas_call | solution.py:61
  61.9 2.1 %shard_map.176 = (f32[256,1024]{1,0:T(8,128)S(1)}, bf16[256,2048]{1,0:T(8,128)(2,1)S(1)}) custom-call(s32[8,128]{1,0:T(8,128)S(1)} %broadcast_in_dim.2.refs_0_.refs_1_.place_ref, bf16[512,512]{1,0:T(8,128)(2,1)S(1)} %get-tuple-element.73.refs_1_, f32[512,512]{1,0:T(8,128)S(1)} %copy-done.6, bf16[256,1024]{1,0:T(8,128)(2,1)S(1)} %copy-done.11, ...), custom_call_target="tpu_custom_call" | custom-call | flops 2700000000 | bytes 2101248 | tf_op jit(solution)/shard_map/pallas_call | solution.py:61
  66.7 3.1 %collective-permute-done.8.refs_1_ = f32[80,256]{1,0:T(8,128)S(1)} collective-permute-done((f32[80,256]{1,0:T(8,128)S(1)}, f32[80,256]{1,0:T(8,128)S(1)}, u32[]{:S(2)}, u32[]{:S(2)}) %collective-permute-start.8) | collective-permute-done | bytes 81952 | tf_op jit(solution)/shard_map/ppermute | solution.py:499
  76.0 2.4 %collective-permute-start.11 = (f32[80,256]{1,0:T(8,128)S(1)}, f32[80,256]{1,0:T(8,128)S(1)}, u32[]{:S(2)}, u32[]{:S(2)}) collective-permute-start(f32[80,256]{1,0:T(8,128)S(1)} %shard_map.181.refs_0_), channel_id=1, source_target_pairs={{0,8},{1,9},{2,10},{3,11},{4,12},{5,13},{6,14},{7,15},{8,0},{9,1},... | collective-permute-start | bytes 245768 | tf_op jit(solution)/shard_map/ppermute | solution.py:499
  78.4 3.6 %collective-permute-done.11.refs_1_ = f32[80,256]{1,0:T(8,128)S(1)} collective-permute-done((f32[80,256]{1,0:T(8,128)S(1)}, f32[80,256]{1,0:T(8,128)S(1)}, u32[]{:S(2)}, u32[]{:S(2)}) %collective-permute-start.11) | collective-permute-done | bytes 81952 | tf_op jit(solution)/shard_map/ppermute | solution.py:499
  82.1 4.7 %collective-permute-done.14.refs_3_ = bf16[64,2048]{1,0:T(8,128)(2,1)S(1)} collective-permute-done((bf16[64,2048]{1,0:T(8,128)(2,1)S(1)}, bf16[64,2048]{1,0:T(8,128)(2,1)S(1)}, u32[]{:S(2)}, u32[]{:S(2)}) %collective-permute-start.14) | collective-permute-done | bytes 262176 | tf_op jit(solution)/shard_map/ppermute | solution.py:519
  89.4 2.4 %collective-permute-start.21 = (bf16[16,2048]{1,0:T(8,128)(2,1)S(1)}, bf16[16,2048]{1,0:T(8,128)(2,1)S(1)}, u32[]{:S(2)}, u32[]{:S(2)}) collective-permute-start(bf16[16,2048]{1,0:T(8,128)(2,1)S(1)} %get-tuple-element.96), channel_id=1, source_target_pairs={{0,8},{1,9},{2,10},{3,11},{4,12},{5,13},{6,14},{7,15},{8,0},{9,1},... | collective-permute-start | bytes 196616 | tf_op jit(solution)/shard_map/ppermute | solution.py:519
  100.7 2.4 %collective-permute-start.25 = (bf16[64,512]{1,0:T(8,128)(2,1)S(1)}, bf16[64,512]{1,0:T(8,128)(2,1)S(1)}, u32[]{:S(2)}, u32[]{:S(2)}) collective-permute-start(bf16[64,512]{1,0:T(8,128)(2,1)S(1)} %shard_map.187.refs_0_.refs_5_), channel_id=1, source_target_pairs={{0,12},{1,13},{2,14},{3,15},{4,8},{5,9},{6,10},{7,11},{8,4},{9,5},... | collective-permute-start | bytes 196616 | tf_op jit(solution)/shard_map/ppermute | solution.py:519
  105.1 2.4 %collective-permute-start.31 = (bf16[16,2048]{1,0:T(8,128)(2,1)S(1)}, bf16[16,2048]{1,0:T(8,128)(2,1)S(1)}, u32[]{:S(2)}, u32[]{:S(2)}) collective-permute-start(bf16[16,2048]{1,0:T(8,128)(2,1)S(1)} %shard_map.186.refs_4_.refs_1_), channel_id=1, source_target_pairs={{0,12},{1,13},{2,14},{3,15},{4,8},{5,9},{6,10},{7,11},{8,4},{9,5},... | collective-permute-start | bytes 196616 | tf_op jit(solution)/shard_map/ppermute | solution.py:519
  109.5 3.0 %collective-permute-done.24.refs_2_ = bf16[64,512]{1,0:T(8,128)(2,1)S(1)} collective-permute-done((bf16[64,512]{1,0:T(8,128)(2,1)S(1)}, bf16[64,512]{1,0:T(8,128)(2,1)S(1)}, u32[]{:S(2)}, u32[]{:S(2)}) %collective-permute-start.24) | collective-permute-done | bytes 65568 | tf_op jit(solution)/shard_map/ppermute | solution.py:519
  113.9 2.3 %collective-permute-start.26 = (bf16[64,512]{1,0:T(8,128)(2,1)S(1)}, bf16[64,512]{1,0:T(8,128)(2,1)S(1)}, u32[]{:S(2)}, u32[]{:S(2)}) collective-permute-start(bf16[64,512]{1,0:T(8,128)(2,1)S(1)} %shard_map.188.refs_1_), channel_id=1, source_target_pairs={{0,1},{1,0},{2,3},{3,2},{4,5},{5,4},{6,7},{7,6},{8,9},{9,8},{10,11... | collective-permute-start | bytes 196616 | tf_op jit(solution)/shard_map/ppermute | solution.py:519
  119.8 2.7 %collective-permute-done.27.refs_3_ = bf16[64,512]{1,0:T(8,128)(2,1)S(1)} collective-permute-done((bf16[64,512]{1,0:T(8,128)(2,1)S(1)}, bf16[64,512]{1,0:T(8,128)(2,1)S(1)}, u32[]{:S(2)}, u32[]{:S(2)}) %collective-permute-start.27) | collective-permute-done | bytes 65568 | tf_op jit(solution)/shard_map/ppermute | solution.py:519
  122.7 3.8 %shard_map.191 = (f32[512,512]{1,0:T(8,128)}, f32[8,128]{1,0:T(8,128)S(1)}) custom-call(s32[8,128]{1,0:T(8,128)S(1)} %broadcast_in_dim.2.refs_0_.refs_1_.place_ref, bf16[512,512]{1,0:T(8,128)(2,1)S(1)} %get-tuple-element.73.refs_1_, bf16[512,512]{1,0:T(8,128)(2,1)S(1)} %get-tuple-element.88.refs_2_, f32[512,512]{1,0:T(8,128)S(1)} %copy-done.6, ...), custom_call_target="tpu_custom_call" | custom-call | flops 5249999872 | bytes 3313664 | tf_op jit(solution)/shard_map/pallas_call | solution.py:61
  132.3 3.0 %shard_map.194 = (f32[2,512,512]{2,1,0:T(8,128)}, f32[512,512]{1,0:T(8,128)}, f32[512,512]{1,0:T(8,128)}, f32[8,128]{1,0:T(8,128)}) custom-call(s32[8,128]{1,0:T(8,128)S(1)} %broadcast_in_dim.2.refs_0_.refs_1_.place_ref, f32[80,256]{1,0:T(8,128)S(1)} %shard_map.182.refs_5_.refs_3_.refs_4_.sum_mine_ref, ...), custom_call_target="tpu_custom_call" | custom-call | flops 3200000000 | tf_op jit(solution)/shard_map/pallas_call | solution.py:644
  (127 shorter events, 44.6 us)
Async XLA Ops:
  6.3 8.7 %collective-permute-start = (f32[72,256]{1,0:T(8,128)S(1)}, f32[72,256]{1,0:T(8,128)S(1)}, u32[]{:S(2)}, u32[]{:S(2)}) collective-permute-start(f32[72,256]{1,0:T(8,128)S(1)} %get-tuple-element.58), channel_id=1, source_target_pairs={{0,16},{16,0},{1,17},{17,1},{2,18},{18,2},{3,19},{19,3},{4,20},{20... | collective-permute-start | bytes 221192 | tf_op jit(solution)/shard_map/ppermute | solution.py:494
  6.8 30.1 %all-to-all-start = ((bf16[16,32,512]{2,1,0:T(8,128)(2,1)}), bf16[16,32,512]{2,1,0:T(8,128)(2,1)S(1)}, u32[]{:S(2)}, u32[]{:S(2)}) async-start(bf16[16,32,512]{2,1,0:T(8,128)(2,1)} %bitcast.12), calls=%async_computation | async-start | bytes 1048576 | tf_op jit(solution)/shard_map/all_to_all | solution.py:561
  36.9 18.8 %collective-permute-start.5 = (f32[72,256]{1,0:T(8,128)S(1)}, f32[72,256]{1,0:T(8,128)S(1)}, u32[]{:S(2)}, u32[]{:S(2)}) collective-permute-start(f32[72,256]{1,0:T(8,128)S(1)} %shard_map.171.refs_4_.refs_3_), channel_id=1, source_target_pairs={{0,16},{16,0},{1,17},{17,1},{2,18},{18,2},{3,19},{19,3},{4,20},{20... | collective-permute-start | bytes 221192 | tf_op jit(solution)/shard_map/ppermute | solution.py:494
  37.0 22.1 %all-to-all-start.1 = ((bf16[16,32,512]{2,1,0:T(8,128)(2,1)}), bf16[16,32,512]{2,1,0:T(8,128)(2,1)S(1)}, u32[]{:S(2)}, u32[]{:S(2)}) async-start(bf16[16,32,512]{2,1,0:T(8,128)(2,1)} %bitcast.14), calls=%async_computation.1 | async-start | bytes 1048576 | tf_op jit(solution)/shard_map/all_to_all | solution.py:580
  64.8 6.7 %collective-permute-start.10 = (bf16[256,2048]{1,0:T(8,128)(2,1)S(1)}, bf16[256,2048]{1,0:T(8,128)(2,1)S(1)}, u32[]{:S(2)}, u32[]{:S(2)}) collective-permute-start(bf16[256,2048]{1,0:T(8,128)(2,1)S(1)} %shard_map.178.refs_2_), channel_id=1, source_target_pairs={{0,16},{16,0},{1,17},{17,1},{2,18},{18,2},{3,19},{19,3},{4,20},{20... | collective-permute-start | bytes 3145736 | tf_op jit(solution)/shard_map/ppermute | solution.py:494
  69.8 6.2 %collective-permute-start.9 = (f32[80,256]{1,0:T(8,128)S(1)}, f32[80,256]{1,0:T(8,128)S(1)}, u32[]{:S(2)}, u32[]{:S(2)}) collective-permute-start(f32[80,256]{1,0:T(8,128)S(1)} %shard_map.179.refs_4_.refs_0_), channel_id=1, source_target_pairs={{0,4},{1,5},{2,6},{3,7},{4,0},{5,1},{6,2},{7,3},{8,12},{9,13},{10,... | collective-permute-start | bytes 245768 | tf_op jit(solution)/shard_map/ppermute | solution.py:499
  72.4 9.7 %collective-permute-start.13 = (bf16[64,2048]{1,0:T(8,128)(2,1)S(1)}, bf16[64,2048]{1,0:T(8,128)(2,1)S(1)}, u32[]{:S(2)}, u32[]{:S(2)}) collective-permute-start(bf16[64,2048]{1,0:T(8,128)(2,1)S(1)} %get-tuple-element.84), channel_id=1, source_target_pairs={{0,1},{1,0},{2,3},{3,2},{4,5},{5,4},{6,7},{7,6},{8,9},{9,8},{10,11... | collective-permute-start | bytes 786440 | tf_op jit(solution)/shard_map/ppermute | solution.py:519
  73.9 12.9 %collective-permute-start.14 = (bf16[64,2048]{1,0:T(8,128)(2,1)S(1)}, bf16[64,2048]{1,0:T(8,128)(2,1)S(1)}, u32[]{:S(2)}, u32[]{:S(2)}) collective-permute-start(bf16[64,2048]{1,0:T(8,128)(2,1)S(1)} %get-tuple-element.85), channel_id=1, source_target_pairs={{0,2},{1,3},{2,0},{3,1},{4,6},{5,7},{6,4},{7,5},{8,10},{9,11},{10,... | collective-permute-start | bytes 786440 | tf_op jit(solution)/shard_map/ppermute | solution.py:519
  75.4 11.5 %collective-permute-start.15 = (bf16[64,2048]{1,0:T(8,128)(2,1)S(1)}, bf16[64,2048]{1,0:T(8,128)(2,1)S(1)}, u32[]{:S(2)}, u32[]{:S(2)}) collective-permute-start(bf16[64,2048]{1,0:T(8,128)(2,1)S(1)} %get-tuple-element.86), channel_id=1, source_target_pairs={{0,3},{1,2},{2,1},{3,0},{4,7},{5,6},{6,5},{7,4},{8,11},{9,10},{10,... | collective-permute-start | bytes 786440 | tf_op jit(solution)/shard_map/ppermute | solution.py:519
  76.0 6.1 %collective-permute-start.11 = (f32[80,256]{1,0:T(8,128)S(1)}, f32[80,256]{1,0:T(8,128)S(1)}, u32[]{:S(2)}, u32[]{:S(2)}) collective-permute-start(f32[80,256]{1,0:T(8,128)S(1)} %shard_map.181.refs_0_), channel_id=1, source_target_pairs={{0,8},{1,9},{2,10},{3,11},{4,12},{5,13},{6,14},{7,15},{8,0},{9,1},... | collective-permute-start | bytes 245768 | tf_op jit(solution)/shard_map/ppermute | solution.py:499
  88.8 6.7 %collective-permute-start.20 = (bf16[16,2048]{1,0:T(8,128)(2,1)S(1)}, bf16[16,2048]{1,0:T(8,128)(2,1)S(1)}, u32[]{:S(2)}, u32[]{:S(2)}) collective-permute-start(bf16[16,2048]{1,0:T(8,128)(2,1)S(1)} %get-tuple-element.95), channel_id=1, source_target_pairs={{0,4},{1,5},{2,6},{3,7},{4,0},{5,1},{6,2},{7,3},{8,12},{9,13},{10,... | collective-permute-start | bytes 196616 | tf_op jit(solution)/shard_map/ppermute | solution.py:519
  89.4 7.5 %collective-permute-start.21 = (bf16[16,2048]{1,0:T(8,128)(2,1)S(1)}, bf16[16,2048]{1,0:T(8,128)(2,1)S(1)}, u32[]{:S(2)}, u32[]{:S(2)}) collective-permute-start(bf16[16,2048]{1,0:T(8,128)(2,1)S(1)} %get-tuple-element.96), channel_id=1, source_target_pairs={{0,8},{1,9},{2,10},{3,11},{4,12},{5,13},{6,14},{7,15},{8,0},{9,1},... | collective-permute-start | bytes 196616 | tf_op jit(solution)/shard_map/ppermute | solution.py:519
  91.8 6.2 %collective-permute-start.22 = (bf16[16,2048]{1,0:T(8,128)(2,1)S(1)}, bf16[16,2048]{1,0:T(8,128)(2,1)S(1)}, u32[]{:S(2)}, u32[]{:S(2)}) collective-permute-start(bf16[16,2048]{1,0:T(8,128)(2,1)S(1)} %get-tuple-element.97), channel_id=1, source_target_pairs={{0,12},{1,13},{2,14},{3,15},{4,8},{5,9},{6,10},{7,11},{8,4},{9,5},... | collective-permute-start | bytes 196616 | tf_op jit(solution)/shard_map/ppermute | solution.py:519
  100.7 6.8 %collective-permute-start.25 = (bf16[64,512]{1,0:T(8,128)(2,1)S(1)}, bf16[64,512]{1,0:T(8,128)(2,1)S(1)}, u32[]{:S(2)}, u32[]{:S(2)}) collective-permute-start(bf16[64,512]{1,0:T(8,128)(2,1)S(1)} %shard_map.187.refs_0_.refs_5_), channel_id=1, source_target_pairs={{0,12},{1,13},{2,14},{3,15},{4,8},{5,9},{6,10},{7,11},{8,4},{9,5},... | collective-permute-start | bytes 196616 | tf_op jit(solution)/shard_map/ppermute | solution.py:519
  103.1 9.4 %collective-permute-start.24 = (bf16[64,512]{1,0:T(8,128)(2,1)S(1)}, bf16[64,512]{1,0:T(8,128)(2,1)S(1)}, u32[]{:S(2)}, u32[]{:S(2)}) collective-permute-start(bf16[64,512]{1,0:T(8,128)(2,1)S(1)} %shard_map.187.refs_0_.refs_5_), channel_id=1, source_target_pairs={{0,8},{1,9},{2,10},{3,11},{4,12},{5,13},{6,14},{7,15},{8,0},{9,1},... | collective-permute-start | bytes 196616 | tf_op jit(solution)/shard_map/ppermute | solution.py:519
  103.1 9.4 %collective-permute-start.23 = (bf16[64,512]{1,0:T(8,128)(2,1)S(1)}, bf16[64,512]{1,0:T(8,128)(2,1)S(1)}, u32[]{:S(2)}, u32[]{:S(2)}) collective-permute-start(bf16[64,512]{1,0:T(8,128)(2,1)S(1)} %shard_map.187.refs_0_.refs_5_), channel_id=1, source_target_pairs={{0,4},{1,5},{2,6},{3,7},{4,0},{5,1},{6,2},{7,3},{8,12},{9,13},{10,... | collective-permute-start | bytes 196616 | tf_op jit(solution)/shard_map/ppermute | solution.py:519
  105.1 8.7 %collective-permute-start.31 = (bf16[16,2048]{1,0:T(8,128)(2,1)S(1)}, bf16[16,2048]{1,0:T(8,128)(2,1)S(1)}, u32[]{:S(2)}, u32[]{:S(2)}) collective-permute-start(bf16[16,2048]{1,0:T(8,128)(2,1)S(1)} %shard_map.186.refs_4_.refs_1_), channel_id=1, source_target_pairs={{0,12},{1,13},{2,14},{3,15},{4,8},{5,9},{6,10},{7,11},{8,4},{9,5},... | collective-permute-start | bytes 196616 | tf_op jit(solution)/shard_map/ppermute | solution.py:519
  107.5 8.7 %collective-permute-start.30 = (bf16[16,2048]{1,0:T(8,128)(2,1)S(1)}, bf16[16,2048]{1,0:T(8,128)(2,1)S(1)}, u32[]{:S(2)}, u32[]{:S(2)}) collective-permute-start(bf16[16,2048]{1,0:T(8,128)(2,1)S(1)} %shard_map.186.refs_4_.refs_1_), channel_id=1, source_target_pairs={{0,8},{1,9},{2,10},{3,11},{4,12},{5,13},{6,14},{7,15},{8,0},{9,1},... | collective-permute-start | bytes 196616 | tf_op jit(solution)/shard_map/ppermute | solution.py:519
  107.5 8.6 %collective-permute-start.29 = (bf16[16,2048]{1,0:T(8,128)(2,1)S(1)}, bf16[16,2048]{1,0:T(8,128)(2,1)S(1)}, u32[]{:S(2)}, u32[]{:S(2)}) collective-permute-start(bf16[16,2048]{1,0:T(8,128)(2,1)S(1)} %shard_map.186.refs_4_.refs_1_), channel_id=1, source_target_pairs={{0,4},{1,5},{2,6},{3,7},{4,0},{5,1},{6,2},{7,3},{8,12},{9,13},{10,... | collective-permute-start | bytes 196616 | tf_op jit(solution)/shard_map/ppermute | solution.py:519
  113.9 8.7 %collective-permute-start.27 = (bf16[64,512]{1,0:T(8,128)(2,1)S(1)}, bf16[64,512]{1,0:T(8,128)(2,1)S(1)}, u32[]{:S(2)}, u32[]{:S(2)}) collective-permute-start(bf16[64,512]{1,0:T(8,128)(2,1)S(1)} %shard_map.188.refs_1_), channel_id=1, source_target_pairs={{0,2},{1,3},{2,0},{3,1},{4,6},{5,7},{6,4},{7,5},{8,10},{9,11},{10,... | collective-permute-start | bytes 196616 | tf_op jit(solution)/shard_map/ppermute | solution.py:519
  113.9 8.6 %collective-permute-start.26 = (bf16[64,512]{1,0:T(8,128)(2,1)S(1)}, bf16[64,512]{1,0:T(8,128)(2,1)S(1)}, u32[]{:S(2)}, u32[]{:S(2)}) collective-permute-start(bf16[64,512]{1,0:T(8,128)(2,1)S(1)} %shard_map.188.refs_1_), channel_id=1, source_target_pairs={{0,1},{1,0},{2,3},{3,2},{4,5},{5,4},{6,7},{7,6},{8,9},{9,8},{10,11... | collective-permute-start | bytes 196616 | tf_op jit(solution)/shard_map/ppermute | solution.py:519
  116.2 11.5 %collective-permute-start.34 = (bf16[64,2048]{1,0:T(8,128)(2,1)S(1)}, bf16[64,2048]{1,0:T(8,128)(2,1)S(1)}, u32[]{:S(2)}, u32[]{:S(2)}) collective-permute-start(bf16[64,2048]{1,0:T(8,128)(2,1)S(1)} %shard_map.189.refs_5_.refs_1_), channel_id=1, source_target_pairs={{0,3},{1,2},{2,1},{3,0},{4,7},{5,6},{6,5},{7,4},{8,11},{9,10},{10,... | collective-permute-start | bytes 786440 | tf_op jit(solution)/shard_map/ppermute | solution.py:519
  117.5 11.7 %collective-permute-start.33 = (bf16[64,2048]{1,0:T(8,128)(2,1)S(1)}, bf16[64,2048]{1,0:T(8,128)(2,1)S(1)}, u32[]{:S(2)}, u32[]{:S(2)}) collective-permute-start(bf16[64,2048]{1,0:T(8,128)(2,1)S(1)} %shard_map.189.refs_5_.refs_1_), channel_id=1, source_target_pairs={{0,2},{1,3},{2,0},{3,1},{4,6},{5,7},{6,4},{7,5},{8,10},{9,11},{10,... | collective-permute-start | bytes 786440 | tf_op jit(solution)/shard_map/ppermute | solution.py:519
  118.5 10.7 %collective-permute-start.32 = (bf16[64,2048]{1,0:T(8,128)(2,1)S(1)}, bf16[64,2048]{1,0:T(8,128)(2,1)S(1)}, u32[]{:S(2)}, u32[]{:S(2)}) collective-permute-start(bf16[64,2048]{1,0:T(8,128)(2,1)S(1)} %shard_map.189.refs_5_.refs_1_), channel_id=1, source_target_pairs={{0,1},{1,0},{2,3},{3,2},{4,5},{5,4},{6,7},{7,6},{8,9},{9,8},{10,11... | collective-permute-start | bytes 786440 | tf_op jit(solution)/shard_map/ppermute | solution.py:519
  (32 other events, 221.5 us)
